TPU v7x, 32 devices: a whole 2x2x4 slice. The times are simulated.
32 devices in a mesh: groups: 2 (over x), owners: 16 (over z, y, core).
Axes of the slice: x: 2, y: 2, z: 4, core: 2. Of those that a mesh axis runs over, the one named last changes fastest.
Arguments:
- embeddings: bfloat16 [32768, 384], P(('groups', 'owners')), parts along dimension 0, may hold values from -400 to 400
- buckets: int32 [32768], P(('groups', 'owners')), parts along dimension 0, may hold values from 0 to 15, as said below
- ranks: int32 [32768], P(('groups', 'owners')), parts along dimension 0, may hold values from 0 to 16383, each once
Outputs:
- highest: float32 [32768], P(('groups', 'owners')), parts along dimension 0
There are 2 independent parts, one for each index of `groups`. A program takes and returns all parts, laid end to end along the dimension named above; each array names one. Nothing has to cross between parts.
Inputs may be any that keep to these rules, and one draw needn't show every extreme that they name: `buckets`: among the documents of one device no value appears more than 128 times; one value, the same on every device, appears exactly 128 times on every device.
All inputs are finite; a program needn't handle non-finite values.
Results may differ from a plain program's by a relative error of at most 0.0015.
Values may be sent and summed in bfloat16 or wider, within the bound.
No kernel may reach another device: no remote copies, remote signals or barrier semaphores. Data moves between devices by JAX's collectives and lax.ppermute only.
A program may use at most 64 MiB of HBM per device.

v0:
```python
import jax
import jax.numpy as jnp
from jax import lax
from jax.sharding import PartitionSpec as P

far_rank = 1073741824


def from_partner(value, axis, apart):
    mask = 2**apart
    pairs = [(source, source ^ mask) for source in range(lax.axis_size(axis))]
    return lax.ppermute(value, axis, pairs)


def normalize(rows_in):
    widened = rows_in.astype(jnp.float32)
    total = jnp.sum(widened * widened, axis=-1, keepdims=True) + 1e-06
    factor = lax.rsqrt(total)
    return (widened * factor).astype(jnp.bfloat16)


def fold_block(highest, queries, query_rank, columns, column_rank):
    query_count = queries.shape[0]
    tile_rows = min(512, query_count)
    pieces = query_count // tile_rows
    query_tiles = queries.reshape(pieces, tile_rows, queries.shape[1])
    rank_tiles = query_rank.reshape(pieces, tile_rows)
    best_tiles = highest.reshape(pieces, tile_rows)

    def one_query_tile(packed):
        tile_queries, tile_rank, running = packed
        scores = lax.dot_general(
            tile_queries, columns, (((1,), (1,)), ((), ())), preferred_element_type=jnp.float32
        )
        scores = jnp.where(column_rank[None, :] < tile_rank[:, None], scores, -1.0)
        return jnp.maximum(running, jnp.max(scores, axis=1))

    return lax.map(one_query_tile, (query_tiles, rank_tiles, best_tiles)).reshape(query_count)


def body(embeddings, buckets, ranks):
    owner_count = lax.axis_size("owners")
    row_count, feature_width = embeddings.shape
    capacity = 2 * row_count // owner_count
    slot_total = owner_count * capacity
    targets = jnp.arange(owner_count, dtype=jnp.int32)
    onehot = (buckets[:, None] == targets[None, :]).astype(jnp.int32)
    before = jnp.cumsum(onehot, axis=0) - onehot
    slot_index = jnp.sum(before * onehot, axis=1)
    position = buckets * capacity + slot_index
    source = (
        jnp.full((slot_total,), row_count, jnp.int32)
        .at[position]
        .set(jnp.arange(row_count, dtype=jnp.int32))
    )
    padded_rows = jnp.concatenate([embeddings, jnp.zeros((1, feature_width), jnp.bfloat16)], axis=0)
    padded_rank = jnp.concatenate([ranks, jnp.full((1,), far_rank, jnp.int32)], axis=0)
    send_rows = padded_rows[source]
    send_rank = padded_rank[source]
    got_rows, got_rank = (
        lax.all_to_all(
            send_rows.reshape(owner_count, capacity, feature_width),
            "owners",
            split_axis=0,
            concat_axis=0,
            tiled=True,
        ),
        lax.all_to_all(
            send_rank.reshape(owner_count, capacity),
            "owners",
            split_axis=0,
            concat_axis=0,
            tiled=True,
        ),
    )
    got_rows = got_rows.reshape(slot_total, feature_width)
    got_rank = got_rank.reshape(slot_total)
    unit_rows = normalize(got_rows)
    own_block = (unit_rows, got_rank)
    highest = jnp.full((slot_total,), -1.0, jnp.float32)
    highest = fold_block(highest, unit_rows, got_rank, unit_rows, got_rank)
    near_block = from_partner((own_block[0], own_block[1]), "owners", 0)
    across_block = from_partner((own_block[0], own_block[1]), "owners", 1)
    diagonal_block = from_partner((across_block[0], across_block[1]), "owners", 0)
    highest = fold_block(highest, unit_rows, got_rank, near_block[0], near_block[1])
    highest = fold_block(highest, unit_rows, got_rank, across_block[0], across_block[1])
    highest = fold_block(highest, unit_rows, got_rank, diagonal_block[0], diagonal_block[1])
    returned = lax.all_to_all(
        highest.reshape(owner_count, capacity), "owners", split_axis=0, concat_axis=0, tiled=True
    )
    return returned.reshape(slot_total)[position]


def solution(mesh):
    in_specs = (P(("groups", "owners"), None), P(("groups", "owners")), P(("groups", "owners")))
    out_specs = P(("groups", "owners"))
    return jax.shard_map(body, mesh=mesh, in_specs=in_specs, out_specs=out_specs, check_vma=False)
```

profile of v0, /device:TPU:0, one launch (start us, length us, event | category | flops | bytes accessed | tf_op | source)
XLA Modules:
  0.0 169.6 jit_solution(4706628484622801937)
XLA Ops:
  0.7 4.5 %reduce-window.6 = s32[16,8,128]{2,1,0:T(8,128)S(1)} reduce-window(s32[16,8,128]{2,1,0:T(8,128)S(1)} %fusion.17, s32[]{:T(128)} %constant.73.clone.1), window={size=1x1x128 pad=0_0x0_0x127_0}, to_apply=%region_0.0 | reduce-window | flops 2080768 | bytes 131076 | tf_op jit(solution)/shard_map/reduce-window
  7.0 4.3 %scatter_custom_fusion = s32[2048]{0:T(1024)S(1)} fusion(s32[1024]{0:T(1024)S(1)} %get-tuple-element.207, s32[1024]{0:T(1024)S(1)} %iota.11, s32[]{:T(128)} %constant.76.clone.1), kind=kCustom, calls=%fused_computation.46 | custom fusion | bytes 8196 | tf_op jit(solution)/shard_map/scatter | solution.py:54
  12.1 20.5 %gather_fusion = s32[2048]{0:T(1024)} fusion(s32[1025]{0:T(1024)S(1)} %pad_add_fusion, s32[2048]{0:T(1024)S(1)} %fusion.18), kind=kCustom, calls=%fused_computation | custom fusion | bytes 24576 | tf_op jit(solution)/shard_map/gather | solution.py:59
  32.6 7.4 %all-to-all-start = ((s32[16,1,128]{2,1,0:T(1,128)}), s32[16,1,128]{2,1,0:T(1,128)}, u32[]{:S(2)}, u32[]{:S(2)}) async-start(s32[16,1,128]{2,1,0:T(1,128)} %bitcast.16), calls=%async_computation | async-start | bytes 16384 | tf_op jit(solution)/shard_map/all_to_all | solution.py:68
  40.1 9.1 %gather_fusion.1 = bf16[2048,384]{1,0:T(8,128)(2,1)} fusion(bf16[1025,384]{1,0:T(8,128)(2,1)S(1)} %concatenate.7, s32[2048]{0:T(1024)S(1)} %fusion.18), kind=kCustom, calls=%fused_computation.1 | custom fusion | bytes 3153920 | tf_op jit(solution)/shard_map/gather | solution.py:58
  49.2 6.0 %all-to-all-start.1 = ((bf16[16,128,384]{2,1,0:T(8,128)(2,1)}), bf16[16,128,384]{2,1,0:T(8,128)(2,1)S(1)}, u32[]{:S(2)}, u32[]{:S(2)}) async-start(bf16[16,128,384]{2,1,0:T(8,128)(2,1)} %bitcast.18), calls=%async_computation.1 | async-start | bytes 3145728 | tf_op jit(solution)/shard_map/all_to_all | solution.py:61
  55.1 1.9 %collective-permute-start.2 = (s32[2048]{0:T(1024)}, s32[2048]{0:T(1024)}, u32[]{:S(2)}, u32[]{:S(2)}) collective-permute-start(s32[2048]{0:T(1024)} %bitcast.22), channel_id=1, source_target_pairs={{0,2},{1,3},{2,0},{3,1},{4,6},{5,7},{6,4},{7,5},{8,10},{9,11},{10,... | collective-permute-start | bytes 24584 | tf_op jit(solution)/shard_map/ppermute | solution.py:12
  59.0 7.0 %collective-permute-done.2 = s32[2048]{0:T(1024)} collective-permute-done((s32[2048]{0:T(1024)}, s32[2048]{0:T(1024)}, u32[]{:S(2)}, u32[]{:S(2)}) %collective-permute-start.2) | collective-permute-done | bytes 8224 | tf_op jit(solution)/shard_map/ppermute | solution.py:12
  65.9 21.2 %all-to-all-done.1 = bf16[16,128,384]{2,1,0:T(8,128)(2,1)S(1)} async-done(((bf16[16,128,384]{2,1,0:T(8,128)(2,1)}), bf16[16,128,384]{2,1,0:T(8,128)(2,1)S(1)}, u32[]{:S(2)}, u32[]{:S(2)}) %all-to-all-start.1) | async-done | bytes 1572896 | tf_op jit(solution)/shard_map/all_to_all | solution.py:61
  87.5 1.5 fusion.12
  89.8 2.7 %collective-permute-start.3 = (bf16[2048,384]{1,0:T(8,128)(2,1)}, bf16[2048,384]{1,0:T(8,128)(2,1)}, u32[]{:S(2)}, u32[]{:S(2)}) collective-permute-start(bf16[2048,384]{1,0:T(8,128)(2,1)} %fusion.12), channel_id=1, source_target_pairs={{0,2},{1,3},{2,0},{3,1},{4,6},{5,7},{6,4},{7,5},{8,10},{9,11},{10,... | collective-permute-start | bytes 4718600 | tf_op jit(solution)/shard_map/ppermute | solution.py:12
  93.2 11.5 %while.40 = (s32[]{:T(128)}, f32[4,512]{1,0:T(4,128)S(1)}, s32[16,128]{1,0:T(8,128)}, s32[4,512]{1,0:T(4,128)S(1)}, bf16[4,512,384]{2,1,0:T(8,128)(2,1)S(1)}, /*...) while((s32[]{:T(128)}, f32[4,512]{1,0:T(4,128)S(1)}, s32[16,128]{1,0:T(8,128)}, s32[4,512]{1,0:T(4,128)S(1)}, ...), condition=%wide.region_7.8_spmd, body=%wide.region_5.7_spmd.sunk | while | flops 808452096 | bytes 1990753 | solution.py:38
  93.2 2.8 %select_reduce_fusion.8 = f32[512]{0:T(512)S(1)} fusion(bf16[2048,384]{1,0:T(8,128)(2,1)} %get-tuple-element.397, s32[2048]{0:T(1024)} %bitcast.79, s32[512]{0:T(512)S(1)} %bitcast.101, bf16[4,512,384]{2,1,0:T(8,128)(2,1)S(1)} %get-tuple-element.396, s32[]{:T(128)} %get-tuple-element.384), kind=kOutput, calls=%fused_computation.4.clone.1 | convolution fusion | flops 808451584 | bytes 1978372 | tf_op jit(solution)/shard_map/while/body/eval_jaxpr/dot_general | solution.py:32
  96.1 2.8 %select_reduce_fusion.8 = f32[512]{0:T(512)S(1)} fusion(bf16[2048,384]{1,0:T(8,128)(2,1)} %get-tuple-element.397, s32[2048]{0:T(1024)} %bitcast.79, s32[512]{0:T(512)S(1)} %bitcast.101, bf16[4,512,384]{2,1,0:T(8,128)(2,1)S(1)} %get-tuple-element.396, s32[]{:T(128)} %get-tuple-element.384), kind=kOutput, calls=%fused_computation.4.clone.1 | convolution fusion | flops 808451584 | bytes 1978372 | tf_op jit(solution)/shard_map/while/body/eval_jaxpr/dot_general | solution.py:32
  98.9 2.8 %select_reduce_fusion.8 = f32[512]{0:T(512)S(1)} fusion(bf16[2048,384]{1,0:T(8,128)(2,1)} %get-tuple-element.397, s32[2048]{0:T(1024)} %bitcast.79, s32[512]{0:T(512)S(1)} %bitcast.101, bf16[4,512,384]{2,1,0:T(8,128)(2,1)S(1)} %get-tuple-element.396, s32[]{:T(128)} %get-tuple-element.384), kind=kOutput, calls=%fused_computation.4.clone.1 | convolution fusion | flops 808451584 | bytes 1978372 | tf_op jit(solution)/shard_map/while/body/eval_jaxpr/dot_general | solution.py:32
  101.8 2.8 %select_reduce_fusion.8 = f32[512]{0:T(512)S(1)} fusion(bf16[2048,384]{1,0:T(8,128)(2,1)} %get-tuple-element.397, s32[2048]{0:T(1024)} %bitcast.79, s32[512]{0:T(512)S(1)} %bitcast.101, bf16[4,512,384]{2,1,0:T(8,128)(2,1)S(1)} %get-tuple-element.396, s32[]{:T(128)} %get-tuple-element.384), kind=kOutput, calls=%fused_computation.4.clone.1 | convolution fusion | flops 808451584 | bytes 1978372 | tf_op jit(solution)/shard_map/while/body/eval_jaxpr/dot_general | solution.py:32
  104.7 5.9 %while.41 = (s32[]{:T(128)}, f32[4,512]{1,0:T(4,128)S(1)}, f32[4,512]{1,0:T(4,128)S(1)}, s32[2048]{0:T(1024)S(1)}, s32[4,512]{1,0:T(4,128)S(1)}, /*index=5*/bf16...) while((s32[]{:T(128)}, f32[4,512]{1,0:T(4,128)S(1)}, ...), condition=%wide.region_10.11_spmd, body=%wide.region_8.10_spmd.sunk | while | flops 808452096 | bytes 1992813 | solution.py:38
  104.7 1.4 select_reduce_fusion.9
  106.2 1.4 select_reduce_fusion.9
  107.7 1.4 select_reduce_fusion.9
  109.2 1.4 select_reduce_fusion.9
  110.6 16.7 %collective-permute-done.3 = bf16[2048,384]{1,0:T(8,128)(2,1)} collective-permute-done((bf16[2048,384]{1,0:T(8,128)(2,1)}, bf16[2048,384]{1,0:T(8,128)(2,1)}, u32[]{:S(2)}, u32[]{:S(2)}) %collective-permute-start.3) | collective-permute-done | bytes 1572896 | tf_op jit(solution)/shard_map/ppermute | solution.py:12
  127.3 11.5 %while.42 = (s32[]{:T(128)}, f32[4,512]{1,0:T(4,128)S(1)}, f32[4,512]{1,0:T(4,128)S(1)}, s32[2048]{0:T(1024)}, s32[4,512]{1,0:T(4,128)S(1)}, /*index=5*/bf16[4,5...) while((s32[]{:T(128)}, f32[4,512]{1,0:T(4,128)S(1)}, f32[4,512]{1,0:T(4,128)S(1)}, ...), condition=%wide.region_13.14_spmd, body=%wide.region_11.13_spmd.sunk | while | flops 808452096 | bytes 1992813 | solution.py:38
  127.3 2.8 %select_reduce_fusion.10 = f32[512]{0:T(512)S(1)} fusion(bf16[2048,384]{1,0:T(8,128)(2,1)} %get-tuple-element.451, s32[2048]{0:T(1024)} %get-tuple-element.448, s32[512]{0:T(512)S(1)} %bitcast.103, bf16[4,512,384]{2,1,0:T(8,128)(2,1)S(1)} %get-tuple-element.450, s32[]{:T(128)} %get-tuple-element.436), kind=kOutput, calls=%fused_computation.16.clone.1 | convolution fusion | flops 808451584 | bytes 1978372 | tf_op jit(solution)/shard_map/while/body/eval_jaxpr/dot_general | solution.py:32
  130.2 2.8 %select_reduce_fusion.10 = f32[512]{0:T(512)S(1)} fusion(bf16[2048,384]{1,0:T(8,128)(2,1)} %get-tuple-element.451, s32[2048]{0:T(1024)} %get-tuple-element.448, s32[512]{0:T(512)S(1)} %bitcast.103, bf16[4,512,384]{2,1,0:T(8,128)(2,1)S(1)} %get-tuple-element.450, s32[]{:T(128)} %get-tuple-element.436), kind=kOutput, calls=%fused_computation.16.clone.1 | convolution fusion | flops 808451584 | bytes 1978372 | tf_op jit(solution)/shard_map/while/body/eval_jaxpr/dot_general | solution.py:32
  133.1 2.8 %select_reduce_fusion.10 = f32[512]{0:T(512)S(1)} fusion(bf16[2048,384]{1,0:T(8,128)(2,1)} %get-tuple-element.451, s32[2048]{0:T(1024)} %get-tuple-element.448, s32[512]{0:T(512)S(1)} %bitcast.103, bf16[4,512,384]{2,1,0:T(8,128)(2,1)S(1)} %get-tuple-element.450, s32[]{:T(128)} %get-tuple-element.436), kind=kOutput, calls=%fused_computation.16.clone.1 | convolution fusion | flops 808451584 | bytes 1978372 | tf_op jit(solution)/shard_map/while/body/eval_jaxpr/dot_general | solution.py:32
  136.0 2.8 %select_reduce_fusion.10 = f32[512]{0:T(512)S(1)} fusion(bf16[2048,384]{1,0:T(8,128)(2,1)} %get-tuple-element.451, s32[2048]{0:T(1024)} %get-tuple-element.448, s32[512]{0:T(512)S(1)} %bitcast.103, bf16[4,512,384]{2,1,0:T(8,128)(2,1)S(1)} %get-tuple-element.450, s32[]{:T(128)} %get-tuple-element.436), kind=kOutput, calls=%fused_computation.16.clone.1 | convolution fusion | flops 808451584 | bytes 1978372 | tf_op jit(solution)/shard_map/while/body/eval_jaxpr/dot_general | solution.py:32
  138.9 5.9 %while.43 = (s32[]{:T(128)}, f32[4,512]{1,0:T(4,128)S(1)}, f32[4,512]{1,0:T(4,128)S(1)}, s32[2048]{0:T(1024)S(1)}, s32[4,512]{1,0:T(4,128)S(1)}, /*index=5*/bf16...) while((s32[]{:T(128)}, f32[4,512]{1,0:T(4,128)S(1)}, ...), condition=%wide.region_16.17_spmd, body=%wide.region_14.16_spmd.sunk | while | flops 808452096 | bytes 1992813 | solution.py:38
  141.9 1.4 select_reduce_fusion.11
  143.3 1.4 select_reduce_fusion.11
  144.8 14.2 %all_to_all.26 = f32[16,1,128]{2,1,0:T(1,128)S(1)} all-to-all(f32[16,1,128]{2,1,0:T(1,128)S(1)} %all_to_all.21), channel_id=1, replica_groups=mesh['groups'=2,'owners'=16] {'owners'}, dimensions={0} | all-to-all | bytes 16384 | tf_op jit(solution)/shard_map/all_to_all | solution.py:88
  159.1 10.5 %gather_fusion.2 = f32[1024]{0:T(1024)} fusion(f32[2048]{0:T(1024)S(1)} %bitcast.94, s32[1024]{0:T(1024)S(1)} %get-tuple-element.206), kind=kCustom, calls=%fused_computation.2 | custom fusion | bytes 12288 | tf_op jit(solution)/shard_map/gather | solution.py:91
  (87 shorter events, 10.9 us)
Async XLA Ops:
  12.1 28.0 %copy-start = (bf16[1024,384]{1,0:T(8,128)(2,1)S(1)}, bf16[1024,384]{1,0:T(8,128)(2,1)}, u32[]{:S(2)}) copy-start(bf16[1024,384]{1,0:T(8,128)(2,1)} %param.11) | copy-start | bytes 2359300
  32.6 16.6 %all-to-all-start = ((s32[16,1,128]{2,1,0:T(1,128)}), s32[16,1,128]{2,1,0:T(1,128)}, u32[]{:S(2)}, u32[]{:S(2)}) async-start(s32[16,1,128]{2,1,0:T(1,128)} %bitcast.16), calls=%async_computation | async-start | bytes 16384 | tf_op jit(solution)/shard_map/all_to_all | solution.py:68
  49.2 37.9 %all-to-all-start.1 = ((bf16[16,128,384]{2,1,0:T(8,128)(2,1)}), bf16[16,128,384]{2,1,0:T(8,128)(2,1)S(1)}, u32[]{:S(2)}, u32[]{:S(2)}) async-start(bf16[16,128,384]{2,1,0:T(8,128)(2,1)} %bitcast.18), calls=%async_computation.1 | async-start | bytes 3145728 | tf_op jit(solution)/shard_map/all_to_all | solution.py:61
  55.1 10.8 %collective-permute-start.2 = (s32[2048]{0:T(1024)}, s32[2048]{0:T(1024)}, u32[]{:S(2)}, u32[]{:S(2)}) collective-permute-start(s32[2048]{0:T(1024)} %bitcast.22), channel_id=1, source_target_pairs={{0,2},{1,3},{2,0},{3,1},{4,6},{5,7},{6,4},{7,5},{8,10},{9,11},{10,... | collective-permute-start | bytes 24584 | tf_op jit(solution)/shard_map/ppermute | solution.py:12
  57.1 47.6 %collective-permute-start = (s32[2048]{0:T(1024)}, s32[2048]{0:T(1024)S(1)}, u32[]{:S(2)}, u32[]{:S(2)}) collective-permute-start(s32[2048]{0:T(1024)} %bitcast.22), channel_id=1, source_target_pairs={{0,1},{1,0},{2,3},{3,2},{4,5},{5,4},{6,7},{7,6},{8,9},{9,8},{10,11... | collective-permute-start | bytes 24584 | tf_op jit(solution)/shard_map/ppermute | solution.py:12
  65.9 72.9 %collective-permute-start.4 = (s32[2048]{0:T(1024)}, s32[2048]{0:T(1024)S(1)}, u32[]{:S(2)}, u32[]{:S(2)}) collective-permute-start(s32[2048]{0:T(1024)} %collective-permute-done.2), channel_id=1, source_target_pairs={{0,1},{1,0},{2,3},{3,2},{4,5},{5,4},{6,7},{7,6},{8,9},{9,8},{10,11... | collective-permute-start | bytes 24584 | tf_op jit(solution)/shard_map/ppermute | solution.py:12
  89.0 15.7 %collective-permute-start.1 = (bf16[2048,384]{1,0:T(8,128)(2,1)}, bf16[2048,384]{1,0:T(8,128)(2,1)S(1)}, u32[]{:S(2)}, u32[]{:S(2)}) collective-permute-start(bf16[2048,384]{1,0:T(8,128)(2,1)} %fusion.12), channel_id=1, source_target_pairs={{0,1},{1,0},{2,3},{3,2},{4,5},{5,4},{6,7},{7,6},{8,9},{9,8},{10,11... | collective-permute-start | bytes 4718600 | tf_op jit(solution)/shard_map/ppermute | solution.py:12
  89.8 37.5 %collective-permute-start.3 = (bf16[2048,384]{1,0:T(8,128)(2,1)}, bf16[2048,384]{1,0:T(8,128)(2,1)}, u32[]{:S(2)}, u32[]{:S(2)}) collective-permute-start(bf16[2048,384]{1,0:T(8,128)(2,1)} %fusion.12), channel_id=1, source_target_pairs={{0,2},{1,3},{2,0},{3,1},{4,6},{5,7},{6,4},{7,5},{8,10},{9,11},{10,... | collective-permute-start | bytes 4718600 | tf_op jit(solution)/shard_map/ppermute | solution.py:12
  127.3 11.6 %collective-permute-start.5 = (bf16[2048,384]{1,0:T(8,128)(2,1)}, bf16[2048,384]{1,0:T(8,128)(2,1)S(1)}, u32[]{:S(2)}, u32[]{:S(2)}) collective-permute-start(bf16[2048,384]{1,0:T(8,128)(2,1)} %collective-permute-done.3), channel_id=1, source_target_pairs={{0,1},{1,0},{2,3},{3,2},{4,5},{5,4},{6,7},{7,6},{8,9},{9,8},{10,11... | collective-permute-start | bytes 4718600 | tf_op jit(solution)/shard_map/ppermute | solution.py:12
where the time goes:
time: 170 us
  local copies, waits for them, and re-layouts  46.3 us (27%)
  waiting for transfers between devices  44.9 us (26%)
  matrix products  33.3 us (20%)
  starting transfers between devices  18.8 us (11%)
  blocking collectives  14.2 us (8%)
  other arithmetic  11.5 us (7%)
    dot_general x16, matrix products, one_query_tile(): lax.dot_general(tile_queries, columns, (((1,), (1,)), ((), ())), preferre...  33.3 us
    ppermute x6, waiting for transfers between devices, from_partner(): return lax.ppermute(value, axis, pairs)  23.7 us
    all_to_all x1, waiting for transfers between devices, body(): lax.all_to_all(send_rows.reshape(owner_count, capacity, feature_width), '...  21.2 us
    gather x1, local copies, waits for them, and re-layouts, body(): send_rank = padded_rank[source]  20.5 us
    all_to_all x1, blocking collectives, body(): lax.all_to_all(highest.reshape(owner_count, capacity), 'owners', split_ax...  14.2 us
    gather x1, local copies, waits for them, and re-layouts, body(): return returned.reshape(slot_total)[position]  10.5 us
    gather x1, local copies, waits for them, and re-layouts, body(): send_rows = padded_rows[source]  9.05 us
    all_to_all x1, starting transfers between devices, body(): lax.all_to_all(send_rank.reshape(owner_count, capacity), 'owners', split_...  7.44 us
  transfers between devices with their start and end apart: 8, of which 3 were waited for; matrix products, arithmetic and copies ran while one was open for 25% of the time, Pallas kernels for 0%

commit v1 on v0

--- a/solution.py
+++ b/solution.py
@@ -1,15 +1,200 @@
+import functools
+
 import jax
 import jax.numpy as jnp
 from jax import lax
+from jax.experimental import pallas as pl
+from jax.experimental.pallas import tpu as pltpu
 from jax.sharding import PartitionSpec as P
 
 far_rank = 1073741824
-
-
-def from_partner(value, axis, apart):
-    mask = 2**apart
+SHARDS = 4
+EXTRA = 16
+PAD_RANK = 65536.0
+VMEM_LIMIT = 48 * 1024 * 1024
+
+
+def from_partner(value, axis, mask):
     pairs = [(source, source ^ mask) for source in range(lax.axis_size(axis))]
     return lax.ppermute(value, axis, pairs)
+
+
+def dot_nt(left, right):
+    return lax.dot_general(left, right, (((1,), (1,)), ((), ())), preferred_element_type=jnp.float32)
+
+
+def one_hot(keys, first, count):
+    rows = lax.broadcasted_iota(jnp.int32, (count, keys.shape[1]), 0) + first
+    return jnp.where(rows == keys, 1.0, 0.0).astype(jnp.bfloat16)
+
+
+def route_kernel(chunks, docs, tile, home_ref, rows_ref, bucket_ref, rank_ref, *out_refs):
+    row_count, width = rows_ref.shape
+    home = home_ref[0]
+    distance = (bucket_ref[...] // SHARDS) ^ home
+    lines = max(chunks, 16)
+    member = lax.broadcasted_iota(jnp.int32, (lines, row_count), 0) == distance
+    member_f = jnp.where(member, 1.0, 0.0)
+    earlier = (
+        lax.broadcasted_iota(jnp.int32, (row_count, row_count), 0)
+        < lax.broadcasted_iota(jnp.int32, (row_count, row_count), 1)
+    )
+    before = jnp.dot(
+        member_f.astype(jnp.bfloat16),
+        jnp.where(earlier, 1.0, 0.0).astype(jnp.bfloat16),
+        preferred_element_type=jnp.float32,
+    )
+    place = jnp.sum(before * member_f, axis=0, keepdims=True)
+    over = jnp.where(jnp.max(place, axis=1, keepdims=True) >= docs, 1.0, 0.0)
+    keys = jnp.where(place < docs, distance * tile + place.astype(jnp.int32), -1)
+    out_refs[chunks][...] = keys
+    widened = rows_ref[...].astype(jnp.float32)
+    total = jnp.sum(widened * widened, axis=1, keepdims=True) + 1e-06
+    unit = (widened * lax.rsqrt(total)).astype(jnp.bfloat16)
+    ranks = rank_ref[...]
+    digit = lax.broadcasted_iota(jnp.int32, (EXTRA, row_count), 0)
+    high = (ranks // 256 - 256).astype(jnp.float32)
+    low = (ranks % 256).astype(jnp.float32)
+    digits = jnp.where(digit == 0, high, jnp.where(digit == 1, low, 0.0)).astype(jnp.bfloat16)
+    for chunk in range(chunks):
+        chosen = one_hot(keys, chunk * tile, tile)
+        moved = jnp.dot(chosen, unit, preferred_element_type=jnp.float32)
+        out_refs[chunk][...] = moved.astype(jnp.bfloat16)
+        tail = dot_nt(digits, chosen)
+        tail = jnp.where(lax.broadcasted_iota(jnp.int32, (EXTRA, tile), 0) == 2, over, tail)
+        if tile < width:
+            tail = jnp.concatenate([tail, jnp.zeros((EXTRA, width - tile), jnp.float32)], axis=1)
+        out_refs[chunk][docs:tile, :] = tail.astype(jnp.bfloat16)
+
+
+def route(chunks, docs, tile, embeddings, buckets, ranks, home):
+    row_count, width = embeddings.shape
+    smem = pl.BlockSpec(memory_space=pltpu.SMEM)
+    vmem = pl.BlockSpec(memory_space=pltpu.VMEM)
+    return pl.pallas_call(
+        functools.partial(route_kernel, chunks, docs, tile),
+        out_shape=[jax.ShapeDtypeStruct((tile, width), jnp.bfloat16)] * chunks
+        + [jax.ShapeDtypeStruct((1, row_count), jnp.int32)],
+        in_specs=[smem, vmem, vmem, vmem],
+        out_specs=[vmem] * (chunks + 1),
+        compiler_params=pltpu.CompilerParams(vmem_limit_bytes=VMEM_LIMIT),
+        cost_estimate=pl.CostEstimate(
+            flops=2 * chunks * tile * row_count * width, bytes_accessed=4 * row_count * width, transcendentals=0
+        ),
+        name="route",
+    )(home, embeddings, buckets.reshape(1, row_count), ranks.reshape(1, row_count))
+
+
+def rank_row(chunk_ref, docs, tile):
+    tail = chunk_ref[docs:tile, :].astype(jnp.float32)
+    return tail[0:1, :tile] * 256.0 + tail[1:2, :tile] + PAD_RANK
+
+
+def spread_ranks(chunk_ref, docs, tile, target_ref, first):
+    tail = chunk_ref[docs:tile, :].astype(jnp.float32)
+    same = lax.broadcasted_iota(jnp.int32, (128, 128), 0) == lax.broadcasted_iota(jnp.int32, (128, 128), 1)
+    ones = jnp.ones((256, 128), jnp.bfloat16)
+    for block in range(tile // 128):
+        lanes = slice(128 * block, 128 * block + 128)
+        diagonal = jnp.concatenate(
+            [jnp.where(same, tail[0:1, lanes] * 256.0, 0.0), jnp.where(same, tail[1:2, lanes], 0.0)], axis=1
+        ).astype(jnp.bfloat16)
+        spread = jnp.dot(diagonal, ones, preferred_element_type=jnp.float32) + PAD_RANK
+        target_ref[first + 128 * block : first + 128 * block + 128, :] = spread
+
+
+def fold(best, query, query_rank, column_ref, column_rank):
+    scores = dot_nt(column_ref[...], query)
+    lanes = query.shape[0]
+    column_rank = jnp.concatenate([column_rank] * (lanes // 128), axis=1)
+    scores = jnp.where(column_rank < query_rank, scores, -1.0)
+    return jnp.maximum(best, jnp.max(scores.reshape(-1, 8, lanes), axis=0))
+
+
+def compare_kernel(docs, tile, query_count, column_count, *refs):
+    query_refs = refs[:query_count]
+    column_refs = refs[query_count : query_count + column_count]
+    out_refs = refs[query_count + column_count : 2 * query_count + column_count]
+    over_ref, spread_ref, query_ref, query_rank_ref, best_ref = refs[2 * query_count + column_count :]
+    over = jnp.zeros((1, 128), jnp.float32)
+    for column in column_refs:
+        over = jnp.maximum(over, column[docs:tile, :].astype(jnp.float32)[2:3, :128])
+    over_ref[...] = over.astype(jnp.int32)
+    for place, column in enumerate(column_refs):
+        spread_ranks(column, docs, tile, spread_ref, place * tile)
+    for place, query in enumerate(query_refs):
+        query_ref[place * tile : place * tile + tile, :] = query[...]
+        query_rank_ref[:, place * tile : place * tile + tile] = rank_row(query, docs, tile)
+    lanes = 256
+
+    def one_tile(step, carry):
+        first = pl.multiple_of(step * lanes, lanes)
+        query = query_ref[pl.ds(first, lanes), :]
+        query_rank = query_rank_ref[:, pl.ds(first, lanes)]
+        best = jnp.full((8, lanes), -1.0, jnp.float32)
+        for place, column in enumerate(column_refs):
+            best = fold(best, query, query_rank, column, spread_ref[place * tile : place * tile + tile, :])
+        best_ref[:, pl.ds(first, lanes)] = jnp.max(best, axis=0, keepdims=True)
+        return carry
+
+    lax.fori_loop(0, query_count * tile // lanes, one_tile, 0)
+    for place, out in enumerate(out_refs):
+        out[...] = best_ref[:, place * tile : place * tile + tile]
+
+
+def compare(docs, tile, queries, columns):
+    vmem = pl.BlockSpec(memory_space=pltpu.VMEM)
+    query_count, column_count = len(queries), len(columns)
+    width = queries[0].shape[1]
+    return pl.pallas_call(
+        functools.partial(compare_kernel, docs, tile, query_count, column_count),
+        out_shape=[jax.ShapeDtypeStruct((1, tile), jnp.float32)] * query_count
+        + [jax.ShapeDtypeStruct((1, 128), jnp.int32)],
+        in_specs=[vmem] * (query_count + column_count),
+        out_specs=[vmem] * (query_count + 1),
+        scratch_shapes=[
+            pltpu.VMEM((column_count * tile, 128), jnp.float32),
+            pltpu.VMEM((query_count * tile, width), jnp.bfloat16),
+            pltpu.VMEM((1, query_count * tile), jnp.float32),
+            pltpu.VMEM((1, query_count * tile), jnp.float32),
+        ],
+        compiler_params=pltpu.CompilerParams(vmem_limit_bytes=VMEM_LIMIT),
+        cost_estimate=pl.CostEstimate(
+            flops=2 * query_count * column_count * tile * tile * width,
+            bytes_accessed=2 * (query_count + column_count) * tile * width,
+            transcendentals=0,
+        ),
+        name="compare",
+    )(*queries, *columns)
+
+
+def place_kernel(chunks, tile, key_ref, *refs):
+    keys = key_ref[...]
+    out_ref = refs[chunks]
+    gathered = jnp.zeros((16, keys.shape[1]), jnp.float32)
+    line = lax.broadcasted_iota(jnp.int32, (16, tile), 0)
+    for chunk in range(chunks):
+        value = refs[chunk][...]
+        first = value.astype(jnp.bfloat16).astype(jnp.float32)
+        second = (value - first).astype(jnp.bfloat16).astype(jnp.float32)
+        third = value - first - second
+        parts = jnp.where(line == 0, first, jnp.where(line == 1, second, jnp.where(line == 2, third, 0.0)))
+        gathered += jnp.dot(
+            parts.astype(jnp.bfloat16), one_hot(keys, chunk * tile, tile), preferred_element_type=jnp.float32
+        )
+    out_ref[...] = jnp.sum(gathered, axis=0, keepdims=True)
+
+
+def place(chunks, tile, keys, values):
+    vmem = pl.BlockSpec(memory_space=pltpu.VMEM)
+    return pl.pallas_call(
+        functools.partial(place_kernel, chunks, tile),
+        out_shape=jax.ShapeDtypeStruct(keys.shape, jnp.float32),
+        in_specs=[vmem] * (chunks + 1),
+        out_specs=vmem,
+        compiler_params=pltpu.CompilerParams(vmem_limit_bytes=VMEM_LIMIT),
+        name="place",
+    )(keys, *values)
 
 
 def normalize(rows_in):
@@ -38,7 +223,7 @@
     return lax.map(one_query_tile, (query_tiles, rank_tiles, best_tiles)).reshape(query_count)
 
 
-def body(embeddings, buckets, ranks):
+def roomy(embeddings, buckets, ranks):
     owner_count = lax.axis_size("owners")
     row_count, feature_width = embeddings.shape
     capacity = 2 * row_count // owner_count
@@ -91,6 +276,26 @@
     return returned.reshape(slot_total)[position]
 
 
+def body(embeddings, buckets, ranks):
+    owner_count = lax.axis_size("owners")
+    row_count, _ = embeddings.shape
+    chunks = owner_count // SHARDS
+    full = SHARDS * 2 * row_count // owner_count
+    tile = -(-(3 * full // 4) // 128) * 128
+    docs = tile - EXTRA
+    home = (lax.axis_index("owners") // SHARDS).astype(jnp.int32).reshape(1)
+    *sent, keys = route(chunks, docs, tile, embeddings, buckets, ranks, home)
+    own = [sent[0]] + [from_partner(sent[k], "owners", SHARDS * k) for k in range(1, chunks)]
+    across = [from_partner(block, "owners", 2) for block in own]
+    near = [from_partner(block, "owners", 1) for block in own]
+    diagonal = [from_partner(block, "owners", 1) for block in across]
+    columns = own + near + across + diagonal
+    *best, over = compare(docs, tile, own, columns)
+    returned = [best[0]] + [from_partner(best[k], "owners", SHARDS * k) for k in range(1, chunks)]
+    found = place(chunks, tile, keys, returned).reshape(row_count)
+    return lax.cond(over[0, 0] > 0, roomy, lambda *_: found, embeddings, buckets, ranks)
+
+
 def solution(mesh):
     in_specs = (P(("groups", "owners"), None), P(("groups", "owners")), P(("groups", "owners")))
     out_specs = P(("groups", "owners"))

time: 170 us -> 66.3 us (0.39)
  local copies, waits for them, and re-layouts: 46.3 us -> 0.6 us
  matrix products: 33.3 us -> 0 us
  Pallas kernels: 0 us -> 16.8 us
  waiting for transfers between devices: 44.9 us -> 30.5 us
  blocking collectives: 14.2 us -> 0 us
  other arithmetic: 11.5 us -> 0 us
    gather x3 -> x0, local copies, waits for them, and re-layouts: 40.1 us -> none  [the longest x1 20.5 us: body(): send_rank = padded_rank[source]]
    dot_general x16 -> x0, matrix products: 33.3 us -> none  [one_query_tile(): lax.dot_general(tile_queries, columns, (((1,), (1,)), ((), ())), preferre...]
    all_to_all x2 -> x0, waiting for transfers between devices: 21.2 us -> none  [the longest x1 21.2 us: body(): lax.all_to_all(send_rows.reshape(owner_count, capacity, feature_width), '...]
    pallas_call x0 -> x3, Pallas kernels: none -> 16.8 us  [the longest x1 12.1 us: compare(): pl.pallas_call(functools.partial(compare_kernel, docs, tile, query_count,...]
    all_to_all x1 -> x0, blocking collectives: 14.2 us -> none  [body(): lax.all_to_all(highest.reshape(owner_count, capacity), 'owners', split_ax...]
    all_to_all x2 -> x0, starting transfers between devices: 13.4 us -> none  [the longest x1 7.44 us: body(): lax.all_to_all(send_rank.reshape(owner_count, capacity), 'owners', split_...]
    ppermute x6 -> x18, starting transfers between devices: 5.37 us -> 18 us  [from_partner(): return lax.ppermute(value, axis, pairs)]
    ppermute x6 -> x18, waiting for transfers between devices: 23.7 us -> 30.5 us  [from_partner(): return lax.ppermute(value, axis, pairs)]
  transfers between devices with their start and end apart: 8 -> 18, of which waited for: 3 -> 9; matrix products, arithmetic and copies ran while one was open for 25% -> 0% of each run, Pallas kernels for 0% -> 0%
where the time goes in v1:
time: 66.3 us; the launch traced here: 66.2 us
  waiting for transfers between devices  30.5 us (46%)
  starting transfers between devices  18 us (27%)
  Pallas kernels  16.8 us (25%)
    ppermute x18, waiting for transfers between devices, from_partner(): return lax.ppermute(value, axis, pairs)  30.5 us
    ppermute x18, starting transfers between devices, from_partner(): return lax.ppermute(value, axis, pairs)  18 us
    pallas_call x1, Pallas kernels, compare(): pl.pallas_call(functools.partial(compare_kernel, docs, tile, query_count,...  12.1 us
    pallas_call x1, Pallas kernels, route(): pl.pallas_call(functools.partial(route_kernel, chunks, docs, tile), out_s...  4.05 us
  transfers between devices with their start and end apart: 18, of which 9 were waited for; matrix products, arithmetic and copies ran while one was open for 0% of the time, Pallas kernels for 0%

profile of v1, /device:TPU:0, one launch (start us, length us, event | category | flops | bytes accessed | tf_op | source)
XLA Modules:
  0.0 66.2 jit_solution(10993240124699391015)
XLA Ops:
  0.0 4.1 %route.1 = (bf16[384,384]{1,0:T(8,128)(2,1)S(1)}, bf16[384,384]{1,0:T(8,128)(2,1)S(1)}, bf16[384,384]{1,0:T(8,128)(2,1)S(1)}, bf16[384,384]{1,0:T(8,128)(2,1)S(1)}, s32[1,1024]{1,0:T(1,128)S(1)}) custom-call(s32[1]{0:T(128)} %bitcast.25.home_ref, bf16[1024,384]{1,0:T(8,128)(2,1)} %rows_ref.1, s32[1,1024]{1,0:T(1,128)} %bitcast.112, s32[1,1024]{1,0:T(1,128)} %bitcast.115), custom_call_target="tpu_custom_call" | custom-call | flops 1207959552 | bytes 1572864 | tf_op jit(solution)/shard_map/route/pallas_call | solution.py:74
  4.1 3.0 %collective-permute-start.6 = (bf16[384,384]{1,0:T(8,128)(2,1)S(1)}, bf16[384,384]{1,0:T(8,128)(2,1)S(1)}, u32[]{:S(2)}, u32[]{:S(2)}) collective-permute-start(bf16[384,384]{1,0:T(8,128)(2,1)S(1)} %get-tuple-element.174), channel_id=1, source_target_pairs={{0,4},{1,5},{2,6},{3,7},{4,0},{5,1},{6,2},{7,3},{8,12},{9,13},{10,... | collective-permute-start | bytes 884744 | tf_op jit(solution)/shard_map/ppermute | solution.py:19
  7.1 2.6 %collective-permute-start.7 = (bf16[384,384]{1,0:T(8,128)(2,1)S(1)}, bf16[384,384]{1,0:T(8,128)(2,1)S(1)}, u32[]{:S(2)}, u32[]{:S(2)}) collective-permute-start(bf16[384,384]{1,0:T(8,128)(2,1)S(1)} %get-tuple-element.175), channel_id=1, source_target_pairs={{0,8},{1,9},{2,10},{3,11},{4,12},{5,13},{6,14},{7,15},{8,0},{9,1},... | collective-permute-start | bytes 884744 | tf_op jit(solution)/shard_map/ppermute | solution.py:19
  9.7 0.0 collective-permute-start.8
  9.7 1.7 %collective-permute-start.13 = (bf16[384,384]{1,0:T(8,128)(2,1)S(1)}, bf16[384,384]{1,0:T(8,128)(2,1)S(1)}, u32[]{:S(2)}, u32[]{:S(2)}) collective-permute-start(bf16[384,384]{1,0:T(8,128)(2,1)S(1)} %get-tuple-element.173.refs_0_.refs_4_), channel_id=1, source_target_pairs={{0,2},{1,3},{2,0},{3,1},{4,6},{5,7},{6,4},{7,5},{8,10},{9,11},{10,... | collective-permute-start | bytes 884744 | tf_op jit(solution)/shard_map/ppermute | solution.py:19
  11.4 8.2 %collective-permute-done.6.refs_1_.refs_5_ = bf16[384,384]{1,0:T(8,128)(2,1)S(1)} collective-permute-done((bf16[384,384]{1,0:T(8,128)(2,1)S(1)}, bf16[384,384]{1,0:T(8,128)(2,1)S(1)}, u32[]{:S(2)}, u32[]{:S(2)}) %collective-permute-start.6) | collective-permute-done | bytes 294944 | tf_op jit(solution)/shard_map/ppermute | solution.py:19
  19.6 1.7 %collective-permute-start.14 = (bf16[384,384]{1,0:T(8,128)(2,1)S(1)}, bf16[384,384]{1,0:T(8,128)(2,1)S(1)}, u32[]{:S(2)}, u32[]{:S(2)}) collective-permute-start(bf16[384,384]{1,0:T(8,128)(2,1)S(1)} %collective-permute-done.6.refs_1_.refs_5_), channel_id=1, source_target_pairs={{0,2},{1,3},{2,0},{3,1},{4,6},{5,7},{6,4},{7,5},{8,10},{9,11},{10,... | collective-permute-start | bytes 884744 | tf_op jit(solution)/shard_map/ppermute | solution.py:19
  21.3 9.2 %collective-permute-done.7.refs_2_.refs_6_ = bf16[384,384]{1,0:T(8,128)(2,1)S(1)} collective-permute-done((bf16[384,384]{1,0:T(8,128)(2,1)S(1)}, bf16[384,384]{1,0:T(8,128)(2,1)S(1)}, u32[]{:S(2)}, u32[]{:S(2)}) %collective-permute-start.7) | collective-permute-done | bytes 294944 | tf_op jit(solution)/shard_map/ppermute | solution.py:19
  30.6 1.5 %collective-permute-start.15 = (bf16[384,384]{1,0:T(8,128)(2,1)S(1)}, bf16[384,384]{1,0:T(8,128)(2,1)S(1)}, u32[]{:S(2)}, u32[]{:S(2)}) collective-permute-start(bf16[384,384]{1,0:T(8,128)(2,1)S(1)} %collective-permute-done.7.refs_2_.refs_6_), channel_id=1, source_target_pairs={{0,2},{1,3},{2,0},{3,1},{4,6},{5,7},{6,4},{7,5},{8,10},{9,11},{10,... | collective-permute-start | bytes 884744 | tf_op jit(solution)/shard_map/ppermute | solution.py:19
  32.1 0.5 collective-permute-start.16
  32.6 0.0 collective-permute-done.13.refs_12_
  32.6 0.0 collective-permute-start.10
  32.6 0.0 collective-permute-done.9.refs_8_
  32.6 0.5 collective-permute-start.11
  33.1 0.1 collective-permute-start.12
  33.2 4.1 %collective-permute-done.15.refs_14_ = bf16[384,384]{1,0:T(8,128)(2,1)S(1)} collective-permute-done((bf16[384,384]{1,0:T(8,128)(2,1)S(1)}, bf16[384,384]{1,0:T(8,128)(2,1)S(1)}, u32[]{:S(2)}, u32[]{:S(2)}) %collective-permute-start.15) | collective-permute-done | bytes 294944 | tf_op jit(solution)/shard_map/ppermute | solution.py:19
  37.3 3.2 %collective-permute-done.16.refs_15_ = bf16[384,384]{1,0:T(8,128)(2,1)S(1)} collective-permute-done((bf16[384,384]{1,0:T(8,128)(2,1)S(1)}, bf16[384,384]{1,0:T(8,128)(2,1)S(1)}, u32[]{:S(2)}, u32[]{:S(2)}) %collective-permute-start.16) | collective-permute-done | bytes 294944 | tf_op jit(solution)/shard_map/ppermute | solution.py:19
  40.5 0.5 collective-permute-start.19
  41.0 0.1 collective-permute-start.20
  41.0 1.0 %collective-permute-done.18.refs_17_ = bf16[384,384]{1,0:T(8,128)(2,1)S(1)} collective-permute-done((bf16[384,384]{1,0:T(8,128)(2,1)S(1)}, bf16[384,384]{1,0:T(8,128)(2,1)S(1)}, u32[]{:S(2)}, u32[]{:S(2)}) %collective-permute-start.18) | collective-permute-done | bytes 294944 | tf_op jit(solution)/shard_map/ppermute | solution.py:19
  42.0 0.4 collective-permute-done.19.refs_18_
  42.5 0.4 collective-permute-done.20.refs_19_
  42.9 12.1 %compare.4 = (f32[1,384]{1,0:T(1,128)S(1)}, f32[1,384]{1,0:T(1,128)S(1)}, f32[1,384]{1,0:T(1,128)S(1)}, f32[1,384]{1,0:T(1,128)S(1)}, s32[1,128]{1,0:T(1,128)S(1)}) custom-call(bf16[384,384]{1,0:T(8,128)(2,1)S(1)} %get-tuple-element.173.refs_0_.refs_4_, bf16[384,384]{1,0:T(8,128)(2,1)S(1)} %collective-permute-done.6.refs_1_.refs_5_, ...), custom_call_target="tpu_custom_call" | custom-call | flops 7247757312 | bytes 5898240 | tf_op jit(solution)/shard_map/compare/pallas_call | solution.py:149
  55.0 3.2 %collective-permute-start.21 = (f32[1,384]{1,0:T(1,128)S(1)}, f32[1,384]{1,0:T(1,128)S(1)}, u32[]{:S(2)}, u32[]{:S(2)}) collective-permute-start(f32[1,384]{1,0:T(1,128)S(1)} %get-tuple-element.180), channel_id=1, source_target_pairs={{0,4},{1,5},{2,6},{3,7},{4,0},{5,1},{6,2},{7,3},{8,12},{9,13},{10,... | collective-permute-start | bytes 4616 | tf_op jit(solution)/shard_map/ppermute | solution.py:19
  58.2 1.1 %collective-permute-start.22 = (f32[1,384]{1,0:T(1,128)S(1)}, f32[1,384]{1,0:T(1,128)S(1)}, u32[]{:S(2)}, u32[]{:S(2)}) collective-permute-start(f32[1,384]{1,0:T(1,128)S(1)} %get-tuple-element.181), channel_id=1, source_target_pairs={{0,8},{1,9},{2,10},{3,11},{4,12},{5,13},{6,14},{7,15},{8,0},{9,1},... | collective-permute-start | bytes 4616 | tf_op jit(solution)/shard_map/ppermute | solution.py:19
  59.4 1.4 %collective-permute-start.23 = (f32[1,384]{1,0:T(1,128)S(1)}, f32[1,384]{1,0:T(1,128)S(1)}, u32[]{:S(2)}, u32[]{:S(2)}) collective-permute-start(f32[1,384]{1,0:T(1,128)S(1)} %get-tuple-element.182), channel_id=1, source_target_pairs={{0,12},{1,13},{2,14},{3,15},{4,8},{5,9},{6,10},{7,11},{8,4},{9,5},... | collective-permute-start | bytes 4616 | tf_op jit(solution)/shard_map/ppermute | solution.py:19
  60.8 1.9 %collective-permute-done.22.refs_2_ = f32[1,384]{1,0:T(1,128)S(1)} collective-permute-done((f32[1,384]{1,0:T(1,128)S(1)}, f32[1,384]{1,0:T(1,128)S(1)}, u32[]{:S(2)}, u32[]{:S(2)}) %collective-permute-start.22) | collective-permute-done | bytes 1568 | tf_op jit(solution)/shard_map/ppermute | solution.py:19
  62.7 2.0 %collective-permute-done.23.refs_3_ = f32[1,384]{1,0:T(1,128)S(1)} collective-permute-done((f32[1,384]{1,0:T(1,128)S(1)}, f32[1,384]{1,0:T(1,128)S(1)}, u32[]{:S(2)}, u32[]{:S(2)}) %collective-permute-start.23) | collective-permute-done | bytes 1568 | tf_op jit(solution)/shard_map/ppermute | solution.py:19
  64.7 0.6 place.1
  65.3 0.2 conditional.1
  65.6 0.0 copy-start.3
  65.6 0.6 copy-done.3
  (16 shorter events, 0.0 us)
Async XLA Ops:
  4.1 15.6 %collective-permute-start.6 = (bf16[384,384]{1,0:T(8,128)(2,1)S(1)}, bf16[384,384]{1,0:T(8,128)(2,1)S(1)}, u32[]{:S(2)}, u32[]{:S(2)}) collective-permute-start(bf16[384,384]{1,0:T(8,128)(2,1)S(1)} %get-tuple-element.174), channel_id=1, source_target_pairs={{0,4},{1,5},{2,6},{3,7},{4,0},{5,1},{6,2},{7,3},{8,12},{9,13},{10,... | collective-permute-start | bytes 884744 | tf_op jit(solution)/shard_map/ppermute | solution.py:19
  7.1 23.5 %collective-permute-start.7 = (bf16[384,384]{1,0:T(8,128)(2,1)S(1)}, bf16[384,384]{1,0:T(8,128)(2,1)S(1)}, u32[]{:S(2)}, u32[]{:S(2)}) collective-permute-start(bf16[384,384]{1,0:T(8,128)(2,1)S(1)} %get-tuple-element.175), channel_id=1, source_target_pairs={{0,8},{1,9},{2,10},{3,11},{4,12},{5,13},{6,14},{7,15},{8,0},{9,1},... | collective-permute-start | bytes 884744 | tf_op jit(solution)/shard_map/ppermute | solution.py:19
  9.7 22.4 %collective-permute-start.8 = (bf16[384,384]{1,0:T(8,128)(2,1)S(1)}, bf16[384,384]{1,0:T(8,128)(2,1)S(1)}, u32[]{:S(2)}, u32[]{:S(2)}) collective-permute-start(bf16[384,384]{1,0:T(8,128)(2,1)S(1)} %get-tuple-element.176), channel_id=1, source_target_pairs={{0,12},{1,13},{2,14},{3,15},{4,8},{5,9},{6,10},{7,11},{8,4},{9,5},... | collective-permute-start | bytes 884744 | tf_op jit(solution)/shard_map/ppermute | solution.py:19
  9.7 55.6 %copy-start = (bf16[1024,384]{1,0:T(8,128)(2,1)S(1)}, bf16[1024,384]{1,0:T(8,128)(2,1)}, u32[]{:S(2)}) copy-start(bf16[1024,384]{1,0:T(8,128)(2,1)} %rows_ref.1) | copy-start | bytes 2359300
  9.7 55.6 %copy-start.1 = (s32[1024]{0:T(1024)S(1)}, s32[1024]{0:T(1024)}, u32[]{:S(2)}) copy-start(s32[1024]{0:T(1024)} %param.14) | copy-start | bytes 12292
  9.7 55.7 %copy-start.2 = (s32[1024]{0:T(1024)S(1)}, s32[1024]{0:T(1024)}, u32[]{:S(2)}) copy-start(s32[1024]{0:T(1024)} %param.15) | copy-start | bytes 12292
  9.7 22.9 %collective-permute-start.13 = (bf16[384,384]{1,0:T(8,128)(2,1)S(1)}, bf16[384,384]{1,0:T(8,128)(2,1)S(1)}, u32[]{:S(2)}, u32[]{:S(2)}) collective-permute-start(bf16[384,384]{1,0:T(8,128)(2,1)S(1)} %get-tuple-element.173.refs_0_.refs_4_), channel_id=1, source_target_pairs={{0,2},{1,3},{2,0},{3,1},{4,6},{5,7},{6,4},{7,5},{8,10},{9,11},{10,... | collective-permute-start | bytes 884744 | tf_op jit(solution)/shard_map/ppermute | solution.py:19
  11.4 21.2 %collective-permute-start.9 = (bf16[384,384]{1,0:T(8,128)(2,1)S(1)}, bf16[384,384]{1,0:T(8,128)(2,1)S(1)}, u32[]{:S(2)}, u32[]{:S(2)}) collective-permute-start(bf16[384,384]{1,0:T(8,128)(2,1)S(1)} %get-tuple-element.173.refs_0_.refs_4_), channel_id=1, source_target_pairs={{0,1},{1,0},{2,3},{3,2},{4,5},{5,4},{6,7},{7,6},{8,9},{9,8},{10,11... | collective-permute-start | bytes 884744 | tf_op jit(solution)/shard_map/ppermute | solution.py:19
  19.6 13.5 %collective-permute-start.14 = (bf16[384,384]{1,0:T(8,128)(2,1)S(1)}, bf16[384,384]{1,0:T(8,128)(2,1)S(1)}, u32[]{:S(2)}, u32[]{:S(2)}) collective-permute-start(bf16[384,384]{1,0:T(8,128)(2,1)S(1)} %collective-permute-done.6.refs_1_.refs_5_), channel_id=1, source_target_pairs={{0,2},{1,3},{2,0},{3,1},{4,6},{5,7},{6,4},{7,5},{8,10},{9,11},{10,... | collective-permute-start | bytes 884744 | tf_op jit(solution)/shard_map/ppermute | solution.py:19
  30.6 6.7 %collective-permute-start.15 = (bf16[384,384]{1,0:T(8,128)(2,1)S(1)}, bf16[384,384]{1,0:T(8,128)(2,1)S(1)}, u32[]{:S(2)}, u32[]{:S(2)}) collective-permute-start(bf16[384,384]{1,0:T(8,128)(2,1)S(1)} %collective-permute-done.7.refs_2_.refs_6_), channel_id=1, source_target_pairs={{0,2},{1,3},{2,0},{3,1},{4,6},{5,7},{6,4},{7,5},{8,10},{9,11},{10,... | collective-permute-start | bytes 884744 | tf_op jit(solution)/shard_map/ppermute | solution.py:19
  32.1 8.4 %collective-permute-start.16 = (bf16[384,384]{1,0:T(8,128)(2,1)S(1)}, bf16[384,384]{1,0:T(8,128)(2,1)S(1)}, u32[]{:S(2)}, u32[]{:S(2)}) collective-permute-start(bf16[384,384]{1,0:T(8,128)(2,1)S(1)} %collective-permute-done.8.refs_3_.refs_7_), channel_id=1, source_target_pairs={{0,2},{1,3},{2,0},{3,1},{4,6},{5,7},{6,4},{7,5},{8,10},{9,11},{10,... | collective-permute-start | bytes 884744 | tf_op jit(solution)/shard_map/ppermute | solution.py:19
  32.6 7.9 %collective-permute-start.10 = (bf16[384,384]{1,0:T(8,128)(2,1)S(1)}, bf16[384,384]{1,0:T(8,128)(2,1)S(1)}, u32[]{:S(2)}, u32[]{:S(2)}) collective-permute-start(bf16[384,384]{1,0:T(8,128)(2,1)S(1)} %collective-permute-done.6.refs_1_.refs_5_), channel_id=1, source_target_pairs={{0,1},{1,0},{2,3},{3,2},{4,5},{5,4},{6,7},{7,6},{8,9},{9,8},{10,11... | collective-permute-start | bytes 884744 | tf_op jit(solution)/shard_map/ppermute | solution.py:19
  32.6 8.4 %collective-permute-start.11 = (bf16[384,384]{1,0:T(8,128)(2,1)S(1)}, bf16[384,384]{1,0:T(8,128)(2,1)S(1)}, u32[]{:S(2)}, u32[]{:S(2)}) collective-permute-start(bf16[384,384]{1,0:T(8,128)(2,1)S(1)} %collective-permute-done.7.refs_2_.refs_6_), channel_id=1, source_target_pairs={{0,1},{1,0},{2,3},{3,2},{4,5},{5,4},{6,7},{7,6},{8,9},{9,8},{10,11... | collective-permute-start | bytes 884744 | tf_op jit(solution)/shard_map/ppermute | solution.py:19
  33.1 7.9 %collective-permute-start.12 = (bf16[384,384]{1,0:T(8,128)(2,1)S(1)}, bf16[384,384]{1,0:T(8,128)(2,1)S(1)}, u32[]{:S(2)}, u32[]{:S(2)}) collective-permute-start(bf16[384,384]{1,0:T(8,128)(2,1)S(1)} %collective-permute-done.8.refs_3_.refs_7_), channel_id=1, source_target_pairs={{0,1},{1,0},{2,3},{3,2},{4,5},{5,4},{6,7},{7,6},{8,9},{9,8},{10,11... | collective-permute-start | bytes 884744 | tf_op jit(solution)/shard_map/ppermute | solution.py:19
  37.3 3.8 %collective-permute-start.17 = (bf16[384,384]{1,0:T(8,128)(2,1)S(1)}, bf16[384,384]{1,0:T(8,128)(2,1)S(1)}, u32[]{:S(2)}, u32[]{:S(2)}) collective-permute-start(bf16[384,384]{1,0:T(8,128)(2,1)S(1)} %collective-permute-done.13.refs_12_), channel_id=1, source_target_pairs={{0,1},{1,0},{2,3},{3,2},{4,5},{5,4},{6,7},{7,6},{8,9},{9,8},{10,11... | collective-permute-start | bytes 884744 | tf_op jit(solution)/shard_map/ppermute | solution.py:19
  40.5 1.6 %collective-permute-start.18 = (bf16[384,384]{1,0:T(8,128)(2,1)S(1)}, bf16[384,384]{1,0:T(8,128)(2,1)S(1)}, u32[]{:S(2)}, u32[]{:S(2)}) collective-permute-start(bf16[384,384]{1,0:T(8,128)(2,1)S(1)} %collective-permute-done.14.refs_13_), channel_id=1, source_target_pairs={{0,1},{1,0},{2,3},{3,2},{4,5},{5,4},{6,7},{7,6},{8,9},{9,8},{10,11... | collective-permute-start | bytes 884744 | tf_op jit(solution)/shard_map/ppermute | solution.py:19
  40.5 2.0 %collective-permute-start.19 = (bf16[384,384]{1,0:T(8,128)(2,1)S(1)}, bf16[384,384]{1,0:T(8,128)(2,1)S(1)}, u32[]{:S(2)}, u32[]{:S(2)}) collective-permute-start(bf16[384,384]{1,0:T(8,128)(2,1)S(1)} %collective-permute-done.15.refs_14_), channel_id=1, source_target_pairs={{0,1},{1,0},{2,3},{3,2},{4,5},{5,4},{6,7},{7,6},{8,9},{9,8},{10,11... | collective-permute-start | bytes 884744 | tf_op jit(solution)/shard_map/ppermute | solution.py:19
  41.0 1.9 %collective-permute-start.20 = (bf16[384,384]{1,0:T(8,128)(2,1)S(1)}, bf16[384,384]{1,0:T(8,128)(2,1)S(1)}, u32[]{:S(2)}, u32[]{:S(2)}) collective-permute-start(bf16[384,384]{1,0:T(8,128)(2,1)S(1)} %collective-permute-done.16.refs_15_), channel_id=1, source_target_pairs={{0,1},{1,0},{2,3},{3,2},{4,5},{5,4},{6,7},{7,6},{8,9},{9,8},{10,11... | collective-permute-start | bytes 884744 | tf_op jit(solution)/shard_map/ppermute | solution.py:19
  55.0 5.8 %collective-permute-start.21 = (f32[1,384]{1,0:T(1,128)S(1)}, f32[1,384]{1,0:T(1,128)S(1)}, u32[]{:S(2)}, u32[]{:S(2)}) collective-permute-start(f32[1,384]{1,0:T(1,128)S(1)} %get-tuple-element.180), channel_id=1, source_target_pairs={{0,4},{1,5},{2,6},{3,7},{4,0},{5,1},{6,2},{7,3},{8,12},{9,13},{10,... | collective-permute-start | bytes 4616 | tf_op jit(solution)/shard_map/ppermute | solution.py:19
  58.2 4.5 %collective-permute-start.22 = (f32[1,384]{1,0:T(1,128)S(1)}, f32[1,384]{1,0:T(1,128)S(1)}, u32[]{:S(2)}, u32[]{:S(2)}) collective-permute-start(f32[1,384]{1,0:T(1,128)S(1)} %get-tuple-element.181), channel_id=1, source_target_pairs={{0,8},{1,9},{2,10},{3,11},{4,12},{5,13},{6,14},{7,15},{8,0},{9,1},... | collective-permute-start | bytes 4616 | tf_op jit(solution)/shard_map/ppermute | solution.py:19
  59.4 5.4 %collective-permute-start.23 = (f32[1,384]{1,0:T(1,128)S(1)}, f32[1,384]{1,0:T(1,128)S(1)}, u32[]{:S(2)}, u32[]{:S(2)}) collective-permute-start(f32[1,384]{1,0:T(1,128)S(1)} %get-tuple-element.182), channel_id=1, source_target_pairs={{0,12},{1,13},{2,14},{3,15},{4,8},{5,9},{6,10},{7,11},{8,4},{9,5},... | collective-permute-start | bytes 4616 | tf_op jit(solution)/shard_map/ppermute | solution.py:19
  65.6 0.6 copy-start.3

commit v2 on v0

v2 whole, which is shorter than its diff:
```python
import functools

import jax
import jax.numpy as jnp
from jax import lax
from jax.experimental import pallas as pl
from jax.experimental.pallas import tpu as pltpu
from jax.sharding import PartitionSpec as P

SHARDS = 4
EXTRA = 16
PAD_RANK = 65536.0
LANES = 512
VMEM_LIMIT = 48 * 1024 * 1024
ROUTE_VMEM_LIMIT = 60 * 1024 * 1024


def from_partner(value, axis, mask):
    pairs = [(source, source ^ mask) for source in range(lax.axis_size(axis))]
    return lax.ppermute(value, axis, pairs)


def dot_nt(left, right):
    return lax.dot_general(left, right, (((1,), (1,)), ((), ())), preferred_element_type=jnp.float32)


def one_hot(keys, first, count):
    rows = lax.broadcasted_iota(jnp.int32, (count, keys.shape[1]), 0) + first
    return jnp.where(rows == keys, 1.0, 0.0).astype(jnp.bfloat16)


def lead(tile, width):
    return 2 * -(-tile // width) + 1


def fold_lines(lines, over, width):
    tile = lines.shape[1]
    rows = []
    for line in range(2):
        for first in range(0, tile, width):
            row = lines[line : line + 1, first : min(first + width, tile)]
            if row.shape[1] < width:
                row = jnp.concatenate([row, jnp.zeros((1, width - row.shape[1]), jnp.float32)], axis=1)
            rows.append(row)
    rows.append(jnp.broadcast_to(over, (1, width)))
    rows.append(jnp.zeros((EXTRA - len(rows), width), jnp.float32))
    return jnp.concatenate(rows, axis=0)


def rank_lines(head_ref, tile):
    width = head_ref.shape[1]
    tail = head_ref[0:EXTRA, :].astype(jnp.float32)
    pieces = -(-tile // width)
    lines = [
        jnp.concatenate([tail[pieces * line + p : pieces * line + p + 1] for p in range(pieces)], axis=1)[:, :tile]
        for line in range(2)
    ]
    return lines[0], lines[1], tail[2 * pieces : 2 * pieces + 1, :128]


def route_kernel(cuts, home_ref, rows_hbm_ref, bucket_hbm_ref, rank_hbm_ref, *refs):
    *out_refs, rows_ref, bucket_ref, rank_ref, copied = refs
    sources = (bucket_hbm_ref, rank_hbm_ref, rows_hbm_ref)
    targets = (bucket_ref, rank_ref, rows_ref)
    copies = [pltpu.make_async_copy(*pair, copied.at[place]) for place, pair in enumerate(zip(sources, targets))]
    for copy in copies:
        copy.start()
    row_count, width = rows_ref.shape
    chunks, tile = len(cuts), sum(cuts[0])
    used = lead(tile, width)
    copies[0].wait()
    distance = (bucket_ref[...] // SHARDS) ^ home_ref[0]
    lines, span = max(chunks, 16), 256
    earlier = lax.broadcasted_iota(jnp.int32, (span, span), 0) < lax.broadcasted_iota(jnp.int32, (span, span), 1)
    earlier = jnp.where(earlier, 1.0, 0.0).astype(jnp.bfloat16)
    member = lax.broadcasted_iota(jnp.int32, (lines, row_count), 0) == distance
    member = jnp.where(member, 1.0, 0.0)
    past, places = jnp.zeros((lines, 1), jnp.float32), []
    for first in range(0, row_count, span):
        some = member[:, first : first + span]
        before = jnp.dot(some.astype(jnp.bfloat16), earlier, preferred_element_type=jnp.float32) + past
        places.append(jnp.sum(before * some, axis=0, keepdims=True))
        past += jnp.sum(some, axis=1, keepdims=True)
    place = jnp.concatenate(places, axis=1)
    over = jnp.where(jnp.max(past, axis=0, keepdims=True) > tile - used, 1.0, 0.0)
    keys = jnp.where(place < tile - used, distance * tile + place.astype(jnp.int32) + used, -1)
    out_refs[-1][...] = keys
    copies[1].wait()
    ranks = rank_ref[...]
    digit = lax.broadcasted_iota(jnp.int32, (EXTRA, row_count), 0)
    high = (ranks // 256 - 256).astype(jnp.float32)
    low = (ranks % 256).astype(jnp.float32)
    digits = jnp.where(digit == 0, high, jnp.where(digit == 1, low, 0.0)).astype(jnp.bfloat16)
    copies[2].wait()
    widened = rows_ref[...].astype(jnp.float32)
    total = jnp.sum(widened * widened, axis=1, keepdims=True) + 1e-06
    unit = (widened * lax.rsqrt(total)).astype(jnp.bfloat16)
    turned = jnp.transpose(digits.astype(jnp.float32)).astype(jnp.bfloat16)
    turned = jnp.concatenate([turned, jnp.zeros((row_count, 128 - EXTRA), jnp.bfloat16)], axis=1)
    unit = jnp.concatenate([unit, turned], axis=1)
    pieces = iter(out_refs)
    for chunk in range(chunks):
        chosen = one_hot(keys, chunk * tile, tile)
        both = jnp.dot(chosen, unit, preferred_element_type=jnp.float32)
        moved = both[:, :width].astype(jnp.bfloat16)
        first = 0
        for rows in cuts[chunk]:
            piece = next(pieces)
            piece[...] = moved[first : first + rows, :]
            if first == 0:
                tail = fold_lines(jnp.transpose(both[:, width:])[:EXTRA], over, width).astype(jnp.bfloat16)
                is_lead = lax.broadcasted_iota(jnp.int32, (EXTRA, width), 0) < used
                piece[0:EXTRA, :] = jnp.where(is_lead, tail, moved[0:EXTRA, :])
            first += rows


def route(cuts, embeddings, buckets, ranks, home):
    row_count, width = embeddings.shape
    smem = pl.BlockSpec(memory_space=pltpu.SMEM)
    vmem = pl.BlockSpec(memory_space=pltpu.VMEM)
    shapes = [jax.ShapeDtypeStruct((rows, width), jnp.bfloat16) for cut in cuts for rows in cut]
    *pieces, keys = pl.pallas_call(
        functools.partial(route_kernel, cuts),
        out_shape=shapes + [jax.ShapeDtypeStruct((1, row_count), jnp.int32)],
        in_specs=[smem] + [pl.BlockSpec(memory_space=pl.ANY)] * 3,
        out_specs=[vmem] * (len(shapes) + 1),
        scratch_shapes=[
            pltpu.VMEM((row_count, width), jnp.bfloat16),
            pltpu.VMEM((1, row_count), jnp.int32),
            pltpu.VMEM((1, row_count), jnp.int32),
            pltpu.SemaphoreType.DMA((3,)),
        ],
        compiler_params=pltpu.CompilerParams(vmem_limit_bytes=ROUTE_VMEM_LIMIT),
        name="route",
    )(home, embeddings, buckets.reshape(1, row_count), ranks.reshape(1, row_count))
    pieces = iter(pieces)
    return [[next(pieces) for _ in cut] for cut in cuts], keys


def spread_ranks(head_ref, tile, offset, target_ref, first, rows):
    high, low, _ = rank_lines(head_ref, tile)
    same = lax.broadcasted_iota(jnp.int32, (128, 128), 0) == lax.broadcasted_iota(jnp.int32, (128, 128), 1)
    ones = jnp.ones((256, 128), jnp.bfloat16)
    for block in range(0, rows, 128):
        lanes = slice(offset + block, offset + block + 128)
        diagonal = jnp.concatenate(
            [jnp.where(same, high[:, lanes] * 256.0, 0.0), jnp.where(same, low[:, lanes], 0.0)], axis=1
        ).astype(jnp.bfloat16)
        spread = jnp.dot(diagonal, ones, preferred_element_type=jnp.float32) + PAD_RANK
        target_ref[first + block : first + block + 128, :] = spread


def fold(best, query, query_rank, column_ref, column_rank):
    scores = dot_nt(column_ref[...], query)
    lanes = query.shape[0]
    column_rank = jnp.concatenate([column_rank] * (lanes // 128), axis=1)
    scores = jnp.where(column_rank < query_rank, scores, -1.0)
    return jnp.maximum(best, jnp.max(scores.reshape(-1, 8, lanes), axis=0))


def compare_kernel(plan, *refs):
    tile, queries, columns, jobs, has_held, has_best, has_over, keep, split, piece_count, lane_count = plan
    refs = iter(refs)
    piece_refs = [next(refs) for _ in range(piece_count)]
    held_refs = [next(refs) for _ in range(2 * has_held)]
    start_ref = next(refs) if has_best else None
    past_ref = next(refs) if has_over else None
    out_refs = [next(refs) for _ in range(lane_count // tile if split else 1)]
    over_ref = next(refs)
    query_ref, query_rank_ref = held_refs if has_held else (next(refs), next(refs))
    spread_ref, best_ref = refs

    over = past_ref[...].astype(jnp.float32) if has_over else jnp.zeros((1, 128), jnp.float32)
    spans, first = [], 0
    for head, piece, offset in columns:
        rows = piece_refs[piece].shape[0]
        if offset == 0:
            over = jnp.maximum(over, rank_lines(piece_refs[head], tile)[2])
        spread_ranks(piece_refs[head], tile, offset, spread_ref, first, rows)
        spans.append((piece_refs[piece], first, first + rows))
        first += rows
    over_ref[...] = over.astype(jnp.int32)

    first = 0
    for query in queries:
        high, low, _ = rank_lines(piece_refs[query[0]], tile)
        query_rank_ref[:, first : first + tile] = high * 256.0 + low + PAD_RANK
        for piece in query:
            rows = piece_refs[piece].shape[0]
            query_ref[first : first + rows, :] = piece_refs[piece][...]
            first += rows
    best_ref[...] = jnp.full((1, lane_count), -1.0, jnp.float32)
    if has_best:
        best_ref[:, : start_ref.shape[1]] = start_ref[...]

    for lane_from, lane_to, column_from, column_to in jobs:

        def one_tile(step, carry, column_from=column_from, column_to=column_to):
            lanes = pl.ds(pl.multiple_of(step * LANES, LANES), LANES)
            query = query_ref[lanes, :]
            query_rank = query_rank_ref[:, lanes]
            best = jnp.broadcast_to(best_ref[:, lanes], (8, LANES))
            for column_ref, start, stop in spans[column_from:column_to]:
                best = fold(best, query, query_rank, column_ref, spread_ref[start:stop, :])
            best_ref[:, lanes] = jnp.max(best, axis=0, keepdims=True)
            return carry

        lax.fori_loop(lane_from // LANES, lane_to // LANES, one_tile, 0)
    if split:
        for place, out_ref in enumerate(out_refs):
            out_ref[...] = best_ref[:, place * tile : place * tile + tile]
    else:
        out_refs[0][...] = best_ref[...]


def columns_of(block):
    first, out = 0, []
    for piece in block:
        out.append((block[0], piece, first))
        first += piece.shape[0]
    return out


def compare(tile, columns, jobs, queries=(), held=(), best=None, over=None, keep=False, split=False):
    pieces = []

    def index_of(array):
        for place, other in enumerate(pieces):
            if other is array:
                return place
        pieces.append(array)
        return len(pieces) - 1

    column_plan = tuple((index_of(head), index_of(piece), offset) for head, piece, offset in columns)
    query_plan = tuple(tuple(index_of(piece) for piece in block) for block in queries)
    lane_count = held[0].shape[0] if held else len(queries) * tile
    width = pieces[0].shape[1]
    plan = (
        tile, query_plan, column_plan, tuple(jobs), bool(held), best is not None, over is not None, keep, split,
        len(pieces), lane_count,
    )
    operands = pieces + list(held) + [array for array in (best, over) if array is not None]
    query_shapes = [((lane_count, width), jnp.bfloat16), ((1, lane_count), jnp.float32)]
    lines = lane_count // tile if split else 1
    outs = [jax.ShapeDtypeStruct((1, lane_count // lines), jnp.float32)] * lines
    outs.append(jax.ShapeDtypeStruct((1, 128), jnp.int32))
    scratch = []
    if keep:
        outs += [jax.ShapeDtypeStruct(*shape) for shape in query_shapes]
    elif not held:
        scratch += [pltpu.VMEM(*shape) for shape in query_shapes]
    column_rows = sum(piece.shape[0] for _, piece, _ in columns)
    scratch += [pltpu.VMEM((column_rows, 128), jnp.float32), pltpu.VMEM((1, lane_count), jnp.float32)]
    vmem = pl.BlockSpec(memory_space=pltpu.VMEM)
    results = pl.pallas_call(
        functools.partial(compare_kernel, plan),
        out_shape=outs,
        in_specs=[vmem] * len(operands),
        out_specs=[vmem] * len(outs),
        scratch_shapes=scratch,
        compiler_params=pltpu.CompilerParams(vmem_limit_bytes=VMEM_LIMIT),
        name="compare",
    )(*operands)
    found = results[:lines] if split else results[0]
    return found, results[lines], results[lines + 1 :]


def place_kernel(chunks, tile, key_ref, *refs):
    keys = key_ref[...]
    out_ref = refs[chunks]
    gathered = jnp.zeros((16, keys.shape[1]), jnp.float32)
    line = lax.broadcasted_iota(jnp.int32, (16, tile), 0)
    for chunk in range(chunks):
        value = refs[chunk][...]
        first = value.astype(jnp.bfloat16).astype(jnp.float32)
        second = (value - first).astype(jnp.bfloat16).astype(jnp.float32)
        third = value - first - second
        parts = jnp.where(line == 0, first, jnp.where(line == 1, second, jnp.where(line == 2, third, 0.0)))
        gathered += jnp.dot(
            parts.astype(jnp.bfloat16), one_hot(keys, chunk * tile, tile), preferred_element_type=jnp.float32
        )
    out_ref[...] = jnp.sum(gathered, axis=0, keepdims=True)


def place(chunks, tile, keys, values):
    vmem = pl.BlockSpec(memory_space=pltpu.VMEM)
    return pl.pallas_call(
        functools.partial(place_kernel, chunks, tile),
        out_shape=jax.ShapeDtypeStruct(keys.shape, jnp.float32),
        in_specs=[vmem] * (chunks + 1),
        out_specs=vmem,
        compiler_params=pltpu.CompilerParams(vmem_limit_bytes=VMEM_LIMIT),
        name="place",
    )(keys, *values)


def swap(block, mask):
    return [from_partner(piece, "owners", mask) for piece in block]


def after(value, *others):
    return lax.optimization_barrier((value, *others))[0]


def give_back(chunks, tile, keys, best):
    returned = [best[0]] + [from_partner(best[k], "owners", SHARDS * k) for k in range(1, chunks)]
    return place(chunks, tile, keys, returned).reshape(keys.shape[1])


def roomy(chunks, tile, embeddings, buckets, ranks, home):
    sent, keys = route(((tile,),) * chunks, embeddings, buckets, ranks, home)
    own = [sent[0]] + [swap(sent[k], SHARDS * k) for k in range(1, chunks)]
    pair = own + [swap(block, 1) for block in own]
    lanes = chunks * tile
    columns = sum(map(columns_of, pair), [])
    best, over, held = compare(tile, columns, ((0, lanes, 0, len(columns)),), own, keep=True)
    columns = sum((columns_of(swap(block, 2)) for block in pair), [])
    best, *_ = compare(tile, columns, ((0, lanes, 0, len(columns)),), held=held, best=best, split=True)
    return give_back(chunks, tile, keys, best)


def snug(chunks, tile, embeddings, buckets, ranks, home):
    sent, keys = route(((tile,),) * chunks, embeddings, buckets, ranks, home)
    lanes, wave = chunks * tile, chunks // 4
    first_lanes = 3 * wave * tile // LANES * LANES
    half_lanes = 2 * wave * tile

    def hop(blocks, mask, *others):
        return [swap([after(piece, *others) for piece in block] if others else block, mask) for block in blocks]

    def z_hop(place, *others):
        group = range(place * wave, place * wave + wave)
        return sum((hop(sent[k : k + 1], SHARDS * k, *others) if k else sent[:1] for k in group), [])

    def columns(*groups):
        return sum(map(columns_of, sum(groups, [])), [])

    z0 = z_hop(0)
    z1 = z_hop(1)
    z2 = z_hop(2)
    z3 = z_hop(3)
    y0 = hop(z0, 2)
    c0 = hop(z0, 1)
    d0 = hop(y0, 1)
    y1 = hop(z1, 2)
    y2 = hop(z2, 2)
    seen = columns(z0, z1, z2, y0, c0, d0)
    k1, over, _ = compare(tile, seen, ((0, first_lanes, 0, len(seen)),), z0 + z1 + z2)
    c1 = hop(z1, 1, k1)
    c2 = hop(z2, 1, k1)
    d1 = hop(y1, 1, k1)
    z3 = [[after(piece, k1) for piece in block] for block in z3]
    y3 = hop(z3, 2)
    c3 = hop(z3, 1)
    d2 = hop(y2, 1)
    every = seen + columns(z3, y2, c3, d2, c1, c2, y1, d1)
    jobs = ((first_lanes, lanes, 0, len(seen)), (0, lanes, len(seen), len(every)))
    k2, over, held = compare(tile, every, jobs, z0 + z1 + z2 + z3, best=k1, over=over, keep=True)
    y3 = [[after(piece, k2) for piece in block] for block in y3]
    d3 = hop(y3, 1)
    last = columns(y3, d3)
    best, over, _ = compare(tile, last, ((0, lanes, 0, len(last)),), held=held, best=k2, over=over, split=True)
    return give_back(chunks, tile, keys, best), over[0, 0] > 0


def body(embeddings, buckets, ranks):
    chunks = lax.axis_size("owners") // SHARDS
    full = SHARDS * 2 * embeddings.shape[0] // lax.axis_size("owners")
    tile = -(-(3 * full // 4) // 128) * 128
    roomy_tile = -(-(full + EXTRA) // 128) * 128
    home = (lax.axis_index("owners") // SHARDS).astype(jnp.int32).reshape(1)
    found, short = snug(chunks, tile, embeddings, buckets, ranks, home)
    return lax.cond(
        short,
        functools.partial(roomy, chunks, roomy_tile),
        lambda *_: found,
        embeddings,
        buckets,
        ranks,
        home,
    )


def solution(mesh):
    in_specs = (P(("groups", "owners"), None), P(("groups", "owners")), P(("groups", "owners")))
    out_specs = P(("groups", "owners"))
    return jax.shard_map(body, mesh=mesh, in_specs=in_specs, out_specs=out_specs, check_vma=False)
```

time: 170 us -> 59.5 us (0.35)
  local copies, waits for them, and re-layouts: 46.3 us -> 1.56 us
  matrix products: 33.3 us -> 0 us
  waiting for transfers between devices: 44.9 us -> 21.1 us
  Pallas kernels: 0 us -> 18.1 us
  blocking collectives: 14.2 us -> 0 us
  other arithmetic: 11.5 us -> 0 us
    gather x3 -> x0, local copies, waits for them, and re-layouts: 40.1 us -> none  [the longest x1 20.5 us: body(): send_rank = padded_rank[source]]
    dot_general x16 -> x0, matrix products: 33.3 us -> none  [one_query_tile(): lax.dot_general(tile_queries, columns, (((1,), (1,)), ((), ())), preferre...]
    all_to_all x2 -> x0, waiting for transfers between devices: 21.2 us -> none  [the longest x1 21.2 us: body(): lax.all_to_all(send_rows.reshape(owner_count, capacity, feature_width), '...]
    pallas_call x0 -> x5, Pallas kernels: none -> 18.1 us  [the longest x3 13.3 us: compare(): pl.pallas_call(functools.partial(compare_kernel, plan), out_shape=outs, i...]
    all_to_all x1 -> x0, blocking collectives: 14.2 us -> none  [body(): lax.all_to_all(highest.reshape(owner_count, capacity), 'owners', split_ax...]
    all_to_all x2 -> x0, starting transfers between devices: 13.4 us -> none  [the longest x1 7.44 us: body(): lax.all_to_all(send_rank.reshape(owner_count, capacity), 'owners', split_...]
    ppermute x6 -> x18, starting transfers between devices: 5.37 us -> 18.2 us  [from_partner(): return lax.ppermute(value, axis, pairs)]
    another operation x3 -> x0, other arithmetic: 4.61 us -> none
  transfers between devices with their start and end apart: 8 -> 18, of which waited for: 3 -> 8; matrix products, arithmetic and copies ran while one was open for 25% -> 0% of each run, Pallas kernels for 0% -> 19%
where the time goes in v2:
time: 59.5 us; the launch traced here: 59.3 us
  waiting for transfers between devices  21.1 us (35%)
  starting transfers between devices  18.2 us (31%)
  Pallas kernels  18.1 us (30%)
  local copies, waits for them, and re-layouts  1.56 us (3%)
    ppermute x18, waiting for transfers between devices, from_partner(): return lax.ppermute(value, axis, pairs)  21.1 us
    ppermute x18, starting transfers between devices, from_partner(): return lax.ppermute(value, axis, pairs)  18.2 us
    pallas_call x3, Pallas kernels, compare(): pl.pallas_call(functools.partial(compare_kernel, plan), out_shape=outs, i...  13.3 us
    pallas_call x1, Pallas kernels, route(): pl.pallas_call(functools.partial(route_kernel, cuts), out_shape=shapes +...  4.16 us
    unnamed x12, local copies, waits for them, and re-layouts  1.56 us
  transfers between devices with their start and end apart: 18, of which 8 were waited for; matrix products, arithmetic and copies ran while one was open for 0% of the time, Pallas kernels for 19%

profile of v2, /device:TPU:0, one launch (start us, length us, event | category | flops | bytes accessed | tf_op | source)
XLA Modules:
  0.0 59.3 jit_solution(14682720000942809875)
XLA Ops:
  0.0 4.2 %route.3 = (bf16[384,384]{1,0:T(8,128)(2,1)}, bf16[384,384]{1,0:T(8,128)(2,1)}, bf16[384,384]{1,0:T(8,128)(2,1)}, bf16[384,384]{1,0:T(8,128)(2,1)}, s32[1,1024]{1,0:T(1,128)}) custom-call(s32[1]{0:T(128)} %bitcast.4.home_ref, bf16[1024,384]{1,0:T(8,128)(2,1)} %rows_hbm_ref.1, s32[1,1024]{1,0:T(1,128)} %bitcast.10, s32[1,1024]{1,0:T(1,128)} %bitcast.12), custom_call_target="tpu_custom_call" | custom-call | tf_op jit(solution)/shard_map/route/pallas_call | solution.py:122
  4.2 3.0 %collective-permute-start.21 = (bf16[384,384]{1,0:T(8,128)(2,1)}, bf16[384,384]{1,0:T(8,128)(2,1)S(1)}, u32[]{:S(2)}, u32[]{:S(2)}) collective-permute-start(bf16[384,384]{1,0:T(8,128)(2,1)} %get-tuple-element.57.refs_0_), channel_id=1, source_target_pairs={{0,2},{1,3},{2,0},{3,1},{4,6},{5,7},{6,4},{7,5},{8,10},{9,11},{10,... | collective-permute-start | bytes 884744 | tf_op jit(solution)/shard_map/ppermute | solution.py:20
  7.2 1.6 %collective-permute-start.19 = (bf16[384,384]{1,0:T(8,128)(2,1)}, bf16[384,384]{1,0:T(8,128)(2,1)S(1)}, u32[]{:S(2)}, u32[]{:S(2)}) collective-permute-start(bf16[384,384]{1,0:T(8,128)(2,1)} %get-tuple-element.58), channel_id=1, source_target_pairs={{0,4},{1,5},{2,6},{3,7},{4,0},{5,1},{6,2},{7,3},{8,12},{9,13},{10,... | collective-permute-start | bytes 884744 | tf_op jit(solution)/shard_map/ppermute | solution.py:20
  8.8 2.6 %collective-permute-start.20 = (bf16[384,384]{1,0:T(8,128)(2,1)}, bf16[384,384]{1,0:T(8,128)(2,1)S(1)}, u32[]{:S(2)}, u32[]{:S(2)}) collective-permute-start(bf16[384,384]{1,0:T(8,128)(2,1)} %get-tuple-element.59), channel_id=1, source_target_pairs={{0,8},{1,9},{2,10},{3,11},{4,12},{5,13},{6,14},{7,15},{8,0},{9,1},... | collective-permute-start | bytes 884744 | tf_op jit(solution)/shard_map/ppermute | solution.py:20
  11.4 0.0 collective-permute-start.22
  11.4 3.0 %collective-permute-done.21.refs_3_ = bf16[384,384]{1,0:T(8,128)(2,1)S(1)} collective-permute-done((bf16[384,384]{1,0:T(8,128)(2,1)}, bf16[384,384]{1,0:T(8,128)(2,1)S(1)}, u32[]{:S(2)}, u32[]{:S(2)}) %collective-permute-start.21) | collective-permute-done | bytes 294944 | tf_op jit(solution)/shard_map/ppermute | solution.py:20
  14.4 7.7 %collective-permute-done.19.refs_1_ = bf16[384,384]{1,0:T(8,128)(2,1)S(1)} collective-permute-done((bf16[384,384]{1,0:T(8,128)(2,1)}, bf16[384,384]{1,0:T(8,128)(2,1)S(1)}, u32[]{:S(2)}, u32[]{:S(2)}) %collective-permute-start.19) | collective-permute-done | bytes 294944 | tf_op jit(solution)/shard_map/ppermute | solution.py:20
  22.1 0.4 collective-permute-start.30
  22.4 2.6 %collective-permute-start.18 = (bf16[384,384]{1,0:T(8,128)(2,1)}, bf16[384,384]{1,0:T(8,128)(2,1)S(1)}, u32[]{:S(2)}, u32[]{:S(2)}) collective-permute-start(bf16[384,384]{1,0:T(8,128)(2,1)} %get-tuple-element.56), channel_id=1, source_target_pairs={{0,12},{1,13},{2,14},{3,15},{4,8},{5,9},{6,10},{7,11},{8,4},{9,5},... | collective-permute-start | bytes 884744 | tf_op jit(solution)/shard_map/ppermute | solution.py:20
  25.1 1.5 %collective-permute-start.25 = (bf16[384,384]{1,0:T(8,128)(2,1)S(1)}, bf16[384,384]{1,0:T(8,128)(2,1)S(1)}, u32[]{:S(2)}, u32[]{:S(2)}) collective-permute-start(bf16[384,384]{1,0:T(8,128)(2,1)S(1)} %collective-permute-done.20.refs_2_), channel_id=1, source_target_pairs={{0,2},{1,3},{2,0},{3,1},{4,6},{5,7},{6,4},{7,5},{8,10},{9,11},{10,... | collective-permute-start | bytes 884744 | tf_op jit(solution)/shard_map/ppermute | solution.py:20
  26.6 1.0 %copy-done = bf16[384,384]{1,0:T(8,128)(2,1)S(1)} copy-done((bf16[384,384]{1,0:T(8,128)(2,1)S(1)}, bf16[384,384]{1,0:T(8,128)(2,1)}, u32[]{:S(2)}) %copy-start) | copy-done | bytes 294936
  27.6 3.4 %compare.9 = (f32[1,1152]{1,0:T(1,128)S(1)}, s32[1,128]{1,0:T(1,128)S(1)}) custom-call(bf16[384,384]{1,0:T(8,128)(2,1)S(1)} %copy-done, bf16[384,384]{1,0:T(8,128)(2,1)S(1)} %collective-permute-done.19.refs_1_, bf16[384,384]{1,0:T(8,128)(2,1)S(1)} %collective-permute-done.20.refs_2_, bf16[384,384]{1,0:T(8,128)(2,1)S(1)} %collective-permute-done.21.refs_3_, ...), custom_call_target="tpu_custom_call" | custom-call | tf_op jit(solution)/shard_map/compare/pallas_call | solution.py:255
  30.9 1.1 %collective-permute-done.30.refs_12_ = bf16[384,384]{1,0:T(8,128)(2,1)S(1)} collective-permute-done((bf16[384,384]{1,0:T(8,128)(2,1)S(1)}, bf16[384,384]{1,0:T(8,128)(2,1)S(1)}, u32[]{:S(2)}, u32[]{:S(2)}) %collective-permute-start.30) | collective-permute-done | bytes 294944 | tf_op jit(solution)/shard_map/ppermute | solution.py:20
  32.0 0.5 collective-permute-start.29
  32.5 0.0 collective-permute-start.28
  32.6 0.5 collective-permute-start.26
  33.1 2.9 %collective-permute-done.25.refs_7_ = bf16[384,384]{1,0:T(8,128)(2,1)S(1)} collective-permute-done((bf16[384,384]{1,0:T(8,128)(2,1)S(1)}, bf16[384,384]{1,0:T(8,128)(2,1)S(1)}, u32[]{:S(2)}, u32[]{:S(2)}) %collective-permute-start.25) | collective-permute-done | bytes 294944 | tf_op jit(solution)/shard_map/ppermute | solution.py:20
  36.0 0.7 %collective-permute-start.24 = (bf16[384,384]{1,0:T(8,128)(2,1)S(1)}, bf16[384,384]{1,0:T(8,128)(2,1)S(1)}, u32[]{:S(2)}, u32[]{:S(2)}) collective-permute-start(bf16[384,384]{1,0:T(8,128)(2,1)S(1)} %collective-permute-done.18.refs_6_), channel_id=1, source_target_pairs={{0,2},{1,3},{2,0},{3,1},{4,6},{5,7},{6,4},{7,5},{8,10},{9,11},{10,... | collective-permute-start | bytes 884744 | tf_op jit(solution)/shard_map/ppermute | solution.py:20
  36.7 0.9 %collective-permute-done.27.refs_9_ = bf16[384,384]{1,0:T(8,128)(2,1)S(1)} collective-permute-done((bf16[384,384]{1,0:T(8,128)(2,1)S(1)}, bf16[384,384]{1,0:T(8,128)(2,1)S(1)}, u32[]{:S(2)}, u32[]{:S(2)}) %collective-permute-start.27) | collective-permute-done | bytes 294944 | tf_op jit(solution)/shard_map/ppermute | solution.py:20
  37.6 7.9 %compare.10 = (f32[1,1536]{1,0:T(1,128)S(1)}, s32[1,128]{1,0:T(1,128)S(1)}, bf16[1536,384]{1,0:T(8,128)(2,1)S(1)}, f32[1,1536]{1,0:T(1,128)S(1)}) custom-call(bf16[384,384]{1,0:T(8,128)(2,1)S(1)} %copy-done, bf16[384,384]{1,0:T(8,128)(2,1)S(1)} %collective-permute-done.19.refs_1_, bf16[384,384]{1,0:T(8,128)(2,1)S(1)} %collective-permute-done.20.refs_2_, ...), custom_call_target="tpu_custom_call" | custom-call | tf_op jit(solution)/shard_map/compare/pallas_call | solution.py:255
  45.4 0.2 collective-permute-start.32
  45.6 1.5 %collective-permute-done.32.refs_1_ = bf16[384,384]{1,0:T(8,128)(2,1)S(1)} collective-permute-done((bf16[384,384]{1,0:T(8,128)(2,1)S(1)}, bf16[384,384]{1,0:T(8,128)(2,1)S(1)}, u32[]{:S(2)}, u32[]{:S(2)}) %collective-permute-start.32) | collective-permute-done | bytes 294944 | tf_op jit(solution)/shard_map/ppermute | solution.py:20
  47.1 2.1 %compare.11 = (f32[1,384]{1,0:T(1,128)S(1)}, f32[1,384]{1,0:T(1,128)S(1)}, f32[1,384]{1,0:T(1,128)S(1)}, f32[1,384]{1,0:T(1,128)S(1)}, s32[1,128]{1,0:T(1,128)S(1)}) custom-call(bf16[384,384]{1,0:T(8,128)(2,1)S(1)} %collective-permute-done.24.refs_0_, bf16[384,384]{1,0:T(8,128)(2,1)S(1)} %collective-permute-done.32.refs_1_, ...), custom_call_target="tpu_custom_call" | custom-call | tf_op jit(solution)/shard_map/compare/pallas_call | solution.py:255
  49.2 2.2 %collective-permute-start.33 = (f32[1,384]{1,0:T(1,128)S(1)}, f32[1,384]{1,0:T(1,128)S(1)}, u32[]{:S(2)}, u32[]{:S(2)}) collective-permute-start(f32[1,384]{1,0:T(1,128)S(1)} %get-tuple-element.74), channel_id=1, source_target_pairs={{0,4},{1,5},{2,6},{3,7},{4,0},{5,1},{6,2},{7,3},{8,12},{9,13},{10,... | collective-permute-start | bytes 4616 | tf_op jit(solution)/shard_map/ppermute | solution.py:20
  51.4 1.2 %collective-permute-start.34 = (f32[1,384]{1,0:T(1,128)S(1)}, f32[1,384]{1,0:T(1,128)S(1)}, u32[]{:S(2)}, u32[]{:S(2)}) collective-permute-start(f32[1,384]{1,0:T(1,128)S(1)} %get-tuple-element.75), channel_id=1, source_target_pairs={{0,8},{1,9},{2,10},{3,11},{4,12},{5,13},{6,14},{7,15},{8,0},{9,1},... | collective-permute-start | bytes 4616 | tf_op jit(solution)/shard_map/ppermute | solution.py:20
  52.5 1.3 %collective-permute-start.35 = (f32[1,384]{1,0:T(1,128)S(1)}, f32[1,384]{1,0:T(1,128)S(1)}, u32[]{:S(2)}, u32[]{:S(2)}) collective-permute-start(f32[1,384]{1,0:T(1,128)S(1)} %get-tuple-element.76), channel_id=1, source_target_pairs={{0,12},{1,13},{2,14},{3,15},{4,8},{5,9},{6,10},{7,11},{8,4},{9,5},... | collective-permute-start | bytes 4616 | tf_op jit(solution)/shard_map/ppermute | solution.py:20
  53.9 2.0 %collective-permute-done.34.refs_2_ = f32[1,384]{1,0:T(1,128)S(1)} collective-permute-done((f32[1,384]{1,0:T(1,128)S(1)}, f32[1,384]{1,0:T(1,128)S(1)}, u32[]{:S(2)}, u32[]{:S(2)}) %collective-permute-start.34) | collective-permute-done | bytes 1568 | tf_op jit(solution)/shard_map/ppermute | solution.py:20
  55.8 2.1 %collective-permute-done.35.refs_3_ = f32[1,384]{1,0:T(1,128)S(1)} collective-permute-done((f32[1,384]{1,0:T(1,128)S(1)}, f32[1,384]{1,0:T(1,128)S(1)}, u32[]{:S(2)}, u32[]{:S(2)}) %collective-permute-start.35) | collective-permute-done | bytes 1568 | tf_op jit(solution)/shard_map/ppermute | solution.py:20
  57.9 0.6 place.3
  58.5 0.2 conditional.1
  58.7 0.0 copy-start.7
  58.8 0.6 copy-done.7
  (22 shorter events, 0.1 us)
Async XLA Ops:
  4.2 10.2 %collective-permute-start.21 = (bf16[384,384]{1,0:T(8,128)(2,1)}, bf16[384,384]{1,0:T(8,128)(2,1)S(1)}, u32[]{:S(2)}, u32[]{:S(2)}) collective-permute-start(bf16[384,384]{1,0:T(8,128)(2,1)} %get-tuple-element.57.refs_0_), channel_id=1, source_target_pairs={{0,2},{1,3},{2,0},{3,1},{4,6},{5,7},{6,4},{7,5},{8,10},{9,11},{10,... | collective-permute-start | bytes 884744 | tf_op jit(solution)/shard_map/ppermute | solution.py:20
  7.2 14.9 %collective-permute-start.19 = (bf16[384,384]{1,0:T(8,128)(2,1)}, bf16[384,384]{1,0:T(8,128)(2,1)S(1)}, u32[]{:S(2)}, u32[]{:S(2)}) collective-permute-start(bf16[384,384]{1,0:T(8,128)(2,1)} %get-tuple-element.58), channel_id=1, source_target_pairs={{0,4},{1,5},{2,6},{3,7},{4,0},{5,1},{6,2},{7,3},{8,12},{9,13},{10,... | collective-permute-start | bytes 884744 | tf_op jit(solution)/shard_map/ppermute | solution.py:20
  8.8 16.3 %collective-permute-start.20 = (bf16[384,384]{1,0:T(8,128)(2,1)}, bf16[384,384]{1,0:T(8,128)(2,1)S(1)}, u32[]{:S(2)}, u32[]{:S(2)}) collective-permute-start(bf16[384,384]{1,0:T(8,128)(2,1)} %get-tuple-element.59), channel_id=1, source_target_pairs={{0,8},{1,9},{2,10},{3,11},{4,12},{5,13},{6,14},{7,15},{8,0},{9,1},... | collective-permute-start | bytes 884744 | tf_op jit(solution)/shard_map/ppermute | solution.py:20
  11.4 15.2 %collective-permute-start.22 = (bf16[384,384]{1,0:T(8,128)(2,1)}, bf16[384,384]{1,0:T(8,128)(2,1)S(1)}, u32[]{:S(2)}, u32[]{:S(2)}) collective-permute-start(bf16[384,384]{1,0:T(8,128)(2,1)} %get-tuple-element.57.refs_0_), channel_id=1, source_target_pairs={{0,1},{1,0},{2,3},{3,2},{4,5},{5,4},{6,7},{7,6},{8,9},{9,8},{10,11... | collective-permute-start | bytes 884744 | tf_op jit(solution)/shard_map/ppermute | solution.py:20
  14.4 12.2 %collective-permute-start.23 = (bf16[384,384]{1,0:T(8,128)(2,1)S(1)}, bf16[384,384]{1,0:T(8,128)(2,1)S(1)}, u32[]{:S(2)}, u32[]{:S(2)}) collective-permute-start(bf16[384,384]{1,0:T(8,128)(2,1)S(1)} %collective-permute-done.21.refs_3_), channel_id=1, source_target_pairs={{0,1},{1,0},{2,3},{3,2},{4,5},{5,4},{6,7},{7,6},{8,9},{9,8},{10,11... | collective-permute-start | bytes 884744 | tf_op jit(solution)/shard_map/ppermute | solution.py:20
  22.1 9.9 %collective-permute-start.30 = (bf16[384,384]{1,0:T(8,128)(2,1)S(1)}, bf16[384,384]{1,0:T(8,128)(2,1)S(1)}, u32[]{:S(2)}, u32[]{:S(2)}) collective-permute-start(bf16[384,384]{1,0:T(8,128)(2,1)S(1)} %collective-permute-done.19.refs_1_), channel_id=1, source_target_pairs={{0,2},{1,3},{2,0},{3,1},{4,6},{5,7},{6,4},{7,5},{8,10},{9,11},{10,... | collective-permute-start | bytes 884744 | tf_op jit(solution)/shard_map/ppermute | solution.py:20
  22.4 10.1 %collective-permute-start.18 = (bf16[384,384]{1,0:T(8,128)(2,1)}, bf16[384,384]{1,0:T(8,128)(2,1)S(1)}, u32[]{:S(2)}, u32[]{:S(2)}) collective-permute-start(bf16[384,384]{1,0:T(8,128)(2,1)} %get-tuple-element.56), channel_id=1, source_target_pairs={{0,12},{1,13},{2,14},{3,15},{4,8},{5,9},{6,10},{7,11},{8,4},{9,5},... | collective-permute-start | bytes 884744 | tf_op jit(solution)/shard_map/ppermute | solution.py:20
  25.1 10.9 %collective-permute-start.25 = (bf16[384,384]{1,0:T(8,128)(2,1)S(1)}, bf16[384,384]{1,0:T(8,128)(2,1)S(1)}, u32[]{:S(2)}, u32[]{:S(2)}) collective-permute-start(bf16[384,384]{1,0:T(8,128)(2,1)S(1)} %collective-permute-done.20.refs_2_), channel_id=1, source_target_pairs={{0,2},{1,3},{2,0},{3,1},{4,6},{5,7},{6,4},{7,5},{8,10},{9,11},{10,... | collective-permute-start | bytes 884744 | tf_op jit(solution)/shard_map/ppermute | solution.py:20
  26.6 1.0 %copy-start = (bf16[384,384]{1,0:T(8,128)(2,1)S(1)}, bf16[384,384]{1,0:T(8,128)(2,1)}, u32[]{:S(2)}) copy-start(bf16[384,384]{1,0:T(8,128)(2,1)} %get-tuple-element.57.refs_0_) | copy-start | bytes 884740
  32.0 3.9 %collective-permute-start.31 = (bf16[384,384]{1,0:T(8,128)(2,1)S(1)}, bf16[384,384]{1,0:T(8,128)(2,1)S(1)}, u32[]{:S(2)}, u32[]{:S(2)}) collective-permute-start(bf16[384,384]{1,0:T(8,128)(2,1)S(1)} %collective-permute-done.30.refs_12_), channel_id=1, source_target_pairs={{0,1},{1,0},{2,3},{3,2},{4,5},{5,4},{6,7},{7,6},{8,9},{9,8},{10,11... | collective-permute-start | bytes 884744 | tf_op jit(solution)/shard_map/ppermute | solution.py:20
  32.0 4.6 %collective-permute-start.29 = (bf16[384,384]{1,0:T(8,128)(2,1)S(1)}, bf16[384,384]{1,0:T(8,128)(2,1)S(1)}, u32[]{:S(2)}, u32[]{:S(2)}) collective-permute-start(bf16[384,384]{1,0:T(8,128)(2,1)S(1)} %collective-permute-done.20.refs_2_), channel_id=1, source_target_pairs={{0,1},{1,0},{2,3},{3,2},{4,5},{5,4},{6,7},{7,6},{8,9},{9,8},{10,11... | collective-permute-start | bytes 884744 | tf_op jit(solution)/shard_map/ppermute | solution.py:20
  32.5 4.1 %collective-permute-start.28 = (bf16[384,384]{1,0:T(8,128)(2,1)S(1)}, bf16[384,384]{1,0:T(8,128)(2,1)S(1)}, u32[]{:S(2)}, u32[]{:S(2)}) collective-permute-start(bf16[384,384]{1,0:T(8,128)(2,1)S(1)} %collective-permute-done.19.refs_1_), channel_id=1, source_target_pairs={{0,1},{1,0},{2,3},{3,2},{4,5},{5,4},{6,7},{7,6},{8,9},{9,8},{10,11... | collective-permute-start | bytes 884744 | tf_op jit(solution)/shard_map/ppermute | solution.py:20
  32.6 4.1 %collective-permute-start.26 = (bf16[384,384]{1,0:T(8,128)(2,1)S(1)}, bf16[384,384]{1,0:T(8,128)(2,1)S(1)}, u32[]{:S(2)}, u32[]{:S(2)}) collective-permute-start(bf16[384,384]{1,0:T(8,128)(2,1)S(1)} %collective-permute-done.18.refs_6_), channel_id=1, source_target_pairs={{0,1},{1,0},{2,3},{3,2},{4,5},{5,4},{6,7},{7,6},{8,9},{9,8},{10,11... | collective-permute-start | bytes 884744 | tf_op jit(solution)/shard_map/ppermute | solution.py:20
  36.0 1.6 %collective-permute-start.27 = (bf16[384,384]{1,0:T(8,128)(2,1)S(1)}, bf16[384,384]{1,0:T(8,128)(2,1)S(1)}, u32[]{:S(2)}, u32[]{:S(2)}) collective-permute-start(bf16[384,384]{1,0:T(8,128)(2,1)S(1)} %collective-permute-done.25.refs_7_), channel_id=1, source_target_pairs={{0,1},{1,0},{2,3},{3,2},{4,5},{5,4},{6,7},{7,6},{8,9},{9,8},{10,11... | collective-permute-start | bytes 884744 | tf_op jit(solution)/shard_map/ppermute | solution.py:20
  36.0 9.4 %collective-permute-start.24 = (bf16[384,384]{1,0:T(8,128)(2,1)S(1)}, bf16[384,384]{1,0:T(8,128)(2,1)S(1)}, u32[]{:S(2)}, u32[]{:S(2)}) collective-permute-start(bf16[384,384]{1,0:T(8,128)(2,1)S(1)} %collective-permute-done.18.refs_6_), channel_id=1, source_target_pairs={{0,2},{1,3},{2,0},{3,1},{4,6},{5,7},{6,4},{7,5},{8,10},{9,11},{10,... | collective-permute-start | bytes 884744 | tf_op jit(solution)/shard_map/ppermute | solution.py:20
  37.5 20.4 %copy-start.2 = (s32[1,1024]{1,0:T(1,128)S(1)}, s32[1,1024]{1,0:T(1,128)}, u32[]{:S(2)}) copy-start(s32[1,1024]{1,0:T(1,128)} %get-tuple-element.72.key_ref) | copy-start | bytes 12292
  37.6 21.0 %copy-start.4 = (bf16[1024,384]{1,0:T(8,128)(2,1)S(1)}, bf16[1024,384]{1,0:T(8,128)(2,1)}, u32[]{:S(2)}) copy-start(bf16[1024,384]{1,0:T(8,128)(2,1)} %rows_hbm_ref.1) | copy-start | bytes 2359300
  37.6 21.0 %copy-start.5 = (s32[1024]{0:T(1024)S(1)}, s32[1024]{0:T(1024)}, u32[]{:S(2)}) copy-start(s32[1024]{0:T(1024)} %param.6) | copy-start | bytes 12292
  37.6 21.0 %copy-start.6 = (s32[1024]{0:T(1024)S(1)}, s32[1024]{0:T(1024)}, u32[]{:S(2)}) copy-start(s32[1024]{0:T(1024)} %param.7) | copy-start | bytes 12292
  45.4 1.6 %collective-permute-start.32 = (bf16[384,384]{1,0:T(8,128)(2,1)S(1)}, bf16[384,384]{1,0:T(8,128)(2,1)S(1)}, u32[]{:S(2)}, u32[]{:S(2)}) collective-permute-start(bf16[384,384]{1,0:T(8,128)(2,1)S(1)} %collective-permute-done.24.refs_0_), channel_id=1, source_target_pairs={{0,1},{1,0},{2,3},{3,2},{4,5},{5,4},{6,7},{7,6},{8,9},{9,8},{10,11... | collective-permute-start | bytes 884744 | tf_op jit(solution)/shard_map/ppermute | solution.py:20
  49.2 4.7 %collective-permute-start.33 = (f32[1,384]{1,0:T(1,128)S(1)}, f32[1,384]{1,0:T(1,128)S(1)}, u32[]{:S(2)}, u32[]{:S(2)}) collective-permute-start(f32[1,384]{1,0:T(1,128)S(1)} %get-tuple-element.74), channel_id=1, source_target_pairs={{0,4},{1,5},{2,6},{3,7},{4,0},{5,1},{6,2},{7,3},{8,12},{9,13},{10,... | collective-permute-start | bytes 4616 | tf_op jit(solution)/shard_map/ppermute | solution.py:20
  51.4 4.5 %collective-permute-start.34 = (f32[1,384]{1,0:T(1,128)S(1)}, f32[1,384]{1,0:T(1,128)S(1)}, u32[]{:S(2)}, u32[]{:S(2)}) collective-permute-start(f32[1,384]{1,0:T(1,128)S(1)} %get-tuple-element.75), channel_id=1, source_target_pairs={{0,8},{1,9},{2,10},{3,11},{4,12},{5,13},{6,14},{7,15},{8,0},{9,1},... | collective-permute-start | bytes 4616 | tf_op jit(solution)/shard_map/ppermute | solution.py:20
  52.5 5.4 %collective-permute-start.35 = (f32[1,384]{1,0:T(1,128)S(1)}, f32[1,384]{1,0:T(1,128)S(1)}, u32[]{:S(2)}, u32[]{:S(2)}) collective-permute-start(f32[1,384]{1,0:T(1,128)S(1)} %get-tuple-element.76), channel_id=1, source_target_pairs={{0,12},{1,13},{2,14},{3,15},{4,8},{5,9},{6,10},{7,11},{8,4},{9,5},... | collective-permute-start | bytes 4616 | tf_op jit(solution)/shard_map/ppermute | solution.py:20
  58.7 0.6 %copy-start.7 = (f32[1024]{0:T(1024)}, f32[1024]{0:T(1024)S(1)}, u32[]{:S(2)}) copy-start(f32[1024]{0:T(1024)S(1)} %get-tuple-element.146) | copy-start | bytes 12292

commit v3 on v2

--- a/solution.py
+++ b/solution.py
@@ -11,6 +11,7 @@
 EXTRA = 16
 PAD_RANK = 65536.0
 LANES = 512
+WHOLE = 5 * 1024 * 1024
 VMEM_LIMIT = 48 * 1024 * 1024
 ROUTE_VMEM_LIMIT = 60 * 1024 * 1024
 
@@ -194,18 +195,20 @@
         best_ref[:, : start_ref.shape[1]] = start_ref[...]
 
     for lane_from, lane_to, column_from, column_to in jobs:
-
-        def one_tile(step, carry, column_from=column_from, column_to=column_to):
-            lanes = pl.ds(pl.multiple_of(step * LANES, LANES), LANES)
+        rows = sum(stop - start for _, start, stop in spans[column_from:column_to])
+        width = lane_to - lane_from if (lane_to - lane_from) * rows <= WHOLE else LANES
+
+        def one_tile(step, carry, width=width, lane_from=lane_from, column_from=column_from, column_to=column_to):
+            lanes = pl.ds(pl.multiple_of(lane_from + step * width, 128), width)
             query = query_ref[lanes, :]
             query_rank = query_rank_ref[:, lanes]
-            best = jnp.broadcast_to(best_ref[:, lanes], (8, LANES))
+            best = jnp.broadcast_to(best_ref[:, lanes], (8, width))
             for column_ref, start, stop in spans[column_from:column_to]:
                 best = fold(best, query, query_rank, column_ref, spread_ref[start:stop, :])
             best_ref[:, lanes] = jnp.max(best, axis=0, keepdims=True)
             return carry
 
-        lax.fori_loop(lane_from // LANES, lane_to // LANES, one_tile, 0)
+        lax.fori_loop(0, (lane_to - lane_from) // width, one_tile, 0)
     if split:
         for place, out_ref in enumerate(out_refs):
             out_ref[...] = best_ref[:, place * tile : place * tile + tile]
@@ -267,7 +270,7 @@
 
 def place_kernel(chunks, tile, key_ref, *refs):
     keys = key_ref[...]
-    out_ref = refs[chunks]
+    out_ref = refs[-1]
     gathered = jnp.zeros((16, keys.shape[1]), jnp.float32)
     line = lax.broadcasted_iota(jnp.int32, (16, tile), 0)
     for chunk in range(chunks):
@@ -279,19 +282,23 @@
         gathered += jnp.dot(
             parts.astype(jnp.bfloat16), one_hot(keys, chunk * tile, tile), preferred_element_type=jnp.float32
         )
-    out_ref[...] = jnp.sum(gathered, axis=0, keepdims=True)
-
-
-def place(chunks, tile, keys, values):
+    found = jnp.sum(gathered, axis=0, keepdims=True)
+    if len(refs) > chunks + 1:
+        over_ref, roomy_ref = refs[chunks : chunks + 2]
+        found = jnp.where(over_ref[:, :1] > 0, roomy_ref[...], found)
+    out_ref[...] = found
+
+
+def place(chunks, tile, keys, values, *instead):
     vmem = pl.BlockSpec(memory_space=pltpu.VMEM)
     return pl.pallas_call(
         functools.partial(place_kernel, chunks, tile),
         out_shape=jax.ShapeDtypeStruct(keys.shape, jnp.float32),
-        in_specs=[vmem] * (chunks + 1),
+        in_specs=[vmem] * (chunks + 1 + len(instead)),
         out_specs=vmem,
         compiler_params=pltpu.CompilerParams(vmem_limit_bytes=VMEM_LIMIT),
         name="place",
-    )(keys, *values)
+    )(keys, *values, *instead)
 
 
 def swap(block, mask):
@@ -302,9 +309,9 @@
     return lax.optimization_barrier((value, *others))[0]
 
 
-def give_back(chunks, tile, keys, best):
+def give_back(chunks, tile, keys, best, *instead):
     returned = [best[0]] + [from_partner(best[k], "owners", SHARDS * k) for k in range(1, chunks)]
-    return place(chunks, tile, keys, returned).reshape(keys.shape[1])
+    return place(chunks, tile, keys, returned, *instead).reshape(keys.shape[1])
 
 
 def roomy(chunks, tile, embeddings, buckets, ranks, home):
@@ -323,7 +330,6 @@
     sent, keys = route(((tile,),) * chunks, embeddings, buckets, ranks, home)
     lanes, wave = chunks * tile, chunks // 4
     first_lanes = 3 * wave * tile // LANES * LANES
-    half_lanes = 2 * wave * tile
 
     def hop(blocks, mask, *others):
         return [swap([after(piece, *others) for piece in block] if others else block, mask) for block in blocks]
@@ -340,14 +346,14 @@
     z2 = z_hop(2)
     z3 = z_hop(3)
     y0 = hop(z0, 2)
-    c0 = hop(z0, 1)
+    c0 = hop(z0, 1, z1[0][0])
     d0 = hop(y0, 1)
     y1 = hop(z1, 2)
     y2 = hop(z2, 2)
     seen = columns(z0, z1, z2, y0, c0, d0)
     k1, over, _ = compare(tile, seen, ((0, first_lanes, 0, len(seen)),), z0 + z1 + z2)
-    c1 = hop(z1, 1, k1)
-    c2 = hop(z2, 1, k1)
+    c1 = hop(z1, 1, z1[0][0])
+    c2 = hop(z2, 1, z2[0][0])
     d1 = hop(y1, 1, k1)
     z3 = [[after(piece, k1) for piece in block] for block in z3]
     y3 = hop(z3, 2)
@@ -358,9 +364,11 @@
     k2, over, held = compare(tile, every, jobs, z0 + z1 + z2 + z3, best=k1, over=over, keep=True)
     y3 = [[after(piece, k2) for piece in block] for block in y3]
     d3 = hop(y3, 1)
-    last = columns(y3, d3)
-    best, over, _ = compare(tile, last, ((0, lanes, 0, len(last)),), held=held, best=k2, over=over, split=True)
-    return give_back(chunks, tile, keys, best), over[0, 0] > 0
+    late = columns(y3)
+    k3, over, _ = compare(tile, late, ((0, lanes, 0, len(late)),), held=held, best=k2, over=over)
+    last = columns(d3)
+    best, over, _ = compare(tile, last, ((0, lanes, 0, len(last)),), held=held, best=k3, over=over, split=True)
+    return keys, best, over
 
 
 def body(embeddings, buckets, ranks):
@@ -369,16 +377,15 @@
     tile = -(-(3 * full // 4) // 128) * 128
     roomy_tile = -(-(full + EXTRA) // 128) * 128
     home = (lax.axis_index("owners") // SHARDS).astype(jnp.int32).reshape(1)
-    found, short = snug(chunks, tile, embeddings, buckets, ranks, home)
-    return lax.cond(
-        short,
+    operands = (embeddings, buckets, ranks, home)
+    keys, best, over = snug(chunks, tile, *operands)
+    other = lax.cond(
+        over[0, 0] > 0,
         functools.partial(roomy, chunks, roomy_tile),
-        lambda *_: found,
-        embeddings,
-        buckets,
-        ranks,
-        home,
+        lambda embeddings, *_: jnp.zeros((embeddings.shape[0],), jnp.float32),
+        *operands,
     )
+    return give_back(chunks, tile, keys, best, over, other.reshape(keys.shape))
 
 
 def solution(mesh):

time: 59.5 us -> 58 us (0.975)
  waiting for transfers between devices: 21.1 us -> 19.3 us
  starting transfers between devices: 18.2 us -> 19.7 us
    ppermute x18, waiting for transfers between devices: 21.1 us -> 19.3 us  [from_partner(): return lax.ppermute(value, axis, pairs)]
    ppermute x18, starting transfers between devices: 18.2 us -> 19.7 us  [from_partner(): return lax.ppermute(value, axis, pairs)]
    pallas_call x3 -> x4, Pallas kernels: 13.3 us -> 12.4 us  [compare(): pl.pallas_call(functools.partial(compare_kernel, plan), out_shape=outs, i...]
    pallas_call x1, Pallas kernels: 0.58 us -> 1.17 us  [place(): pl.pallas_call(functools.partial(place_kernel, chunks, tile), out_shape=j...]
    unnamed x12 -> x10, local copies, waits for them, and re-layouts: 1.56 us -> 0.99 us
  transfers between devices with their start and end apart: 18 -> 18, of which waited for: 8 -> 8; matrix products, arithmetic and copies ran while one was open for 0% -> 0% of each run, Pallas kernels for 19% -> 20%
where the time goes in v3:
time: 58 us; the launch traced here: 57.8 us
  starting transfers between devices  19.7 us (34%)
  waiting for transfers between devices  19.3 us (33%)
  Pallas kernels  17.7 us (31%)
  local copies, waits for them, and re-layouts  0.99 us (2%)
    ppermute x18, starting transfers between devices, from_partner(): return lax.ppermute(value, axis, pairs)  19.7 us
    ppermute x18, waiting for transfers between devices, from_partner(): return lax.ppermute(value, axis, pairs)  19.3 us
    pallas_call x4, Pallas kernels, compare(): pl.pallas_call(functools.partial(compare_kernel, plan), out_shape=outs, i...  12.4 us
    pallas_call x1, Pallas kernels, route(): pl.pallas_call(functools.partial(route_kernel, cuts), out_shape=shapes +...  4.16 us
    pallas_call x1, Pallas kernels, place(): pl.pallas_call(functools.partial(place_kernel, chunks, tile), out_shape=j...  1.17 us
  transfers between devices with their start and end apart: 18, of which 8 were waited for; matrix products, arithmetic and copies ran while one was open for 0% of the time, Pallas kernels for 20%

profile of v3, /device:TPU:0, one launch (start us, length us, event | category | flops | bytes accessed | tf_op | source)
XLA Modules:
  0.0 57.8 jit_solution(4824446822503412793)
XLA Ops:
  0.0 4.2 %route.3 = (bf16[384,384]{1,0:T(8,128)(2,1)}, bf16[384,384]{1,0:T(8,128)(2,1)}, bf16[384,384]{1,0:T(8,128)(2,1)}, bf16[384,384]{1,0:T(8,128)(2,1)}, s32[1,1024]{1,0:T(1,128)}) custom-call(s32[1]{0:T(128)} %bitcast.2.home_ref, bf16[1024,384]{1,0:T(8,128)(2,1)} %rows_hbm_ref.1, s32[1,1024]{1,0:T(1,128)} %bitcast.9, s32[1,1024]{1,0:T(1,128)} %bitcast.11), custom_call_target="tpu_custom_call" | custom-call | tf_op jit(solution)/shard_map/route/pallas_call | solution.py:123
  4.2 3.1 %collective-permute-start.19 = (bf16[384,384]{1,0:T(8,128)(2,1)}, bf16[384,384]{1,0:T(8,128)(2,1)S(1)}, u32[]{:S(2)}, u32[]{:S(2)}) collective-permute-start(bf16[384,384]{1,0:T(8,128)(2,1)} %get-tuple-element.60), channel_id=1, source_target_pairs={{0,4},{1,5},{2,6},{3,7},{4,0},{5,1},{6,2},{7,3},{8,12},{9,13},{10,... | collective-permute-start | bytes 884744 | tf_op jit(solution)/shard_map/ppermute | solution.py:21
  7.3 1.5 %collective-permute-start.21 = (bf16[384,384]{1,0:T(8,128)(2,1)}, bf16[384,384]{1,0:T(8,128)(2,1)S(1)}, u32[]{:S(2)}, u32[]{:S(2)}) collective-permute-start(bf16[384,384]{1,0:T(8,128)(2,1)} %get-tuple-element.62.refs_0_), channel_id=1, source_target_pairs={{0,2},{1,3},{2,0},{3,1},{4,6},{5,7},{6,4},{7,5},{8,10},{9,11},{10,... | collective-permute-start | bytes 884744 | tf_op jit(solution)/shard_map/ppermute | solution.py:21
  8.8 2.6 %collective-permute-start.20 = (bf16[384,384]{1,0:T(8,128)(2,1)}, bf16[384,384]{1,0:T(8,128)(2,1)S(1)}, u32[]{:S(2)}, u32[]{:S(2)}) collective-permute-start(bf16[384,384]{1,0:T(8,128)(2,1)} %get-tuple-element.61), channel_id=1, source_target_pairs={{0,8},{1,9},{2,10},{3,11},{4,12},{5,13},{6,14},{7,15},{8,0},{9,1},... | collective-permute-start | bytes 884744 | tf_op jit(solution)/shard_map/ppermute | solution.py:21
  11.4 8.1 %collective-permute-done.19.refs_1_ = bf16[384,384]{1,0:T(8,128)(2,1)S(1)} collective-permute-done((bf16[384,384]{1,0:T(8,128)(2,1)}, bf16[384,384]{1,0:T(8,128)(2,1)S(1)}, u32[]{:S(2)}, u32[]{:S(2)}) %collective-permute-start.19) | collective-permute-done | bytes 294944 | tf_op jit(solution)/shard_map/ppermute | solution.py:21
  19.4 0.5 collective-permute-start.23
  20.0 2.7 %collective-permute-start.30 = (bf16[384,384]{1,0:T(8,128)(2,1)S(1)}, bf16[384,384]{1,0:T(8,128)(2,1)S(1)}, u32[]{:S(2)}, u32[]{:S(2)}) collective-permute-start(bf16[384,384]{1,0:T(8,128)(2,1)S(1)} %collective-permute-done.19.refs_1_), channel_id=1, source_target_pairs={{0,2},{1,3},{2,0},{3,1},{4,6},{5,7},{6,4},{7,5},{8,10},{9,11},{10,... | collective-permute-start | bytes 884744 | tf_op jit(solution)/shard_map/ppermute | solution.py:21
  22.7 2.5 %collective-permute-start.18 = (bf16[384,384]{1,0:T(8,128)(2,1)}, bf16[384,384]{1,0:T(8,128)(2,1)S(1)}, u32[]{:S(2)}, u32[]{:S(2)}) collective-permute-start(bf16[384,384]{1,0:T(8,128)(2,1)} %get-tuple-element.58), channel_id=1, source_target_pairs={{0,12},{1,13},{2,14},{3,15},{4,8},{5,9},{6,10},{7,11},{8,4},{9,5},... | collective-permute-start | bytes 884744 | tf_op jit(solution)/shard_map/ppermute | solution.py:21
  25.1 0.0 collective-permute-done.20.refs_2_
  25.1 0.1 collective-permute-start.25
  25.2 0.5 collective-permute-start.29
  25.7 1.0 %copy-done = bf16[384,384]{1,0:T(8,128)(2,1)S(1)} copy-done((bf16[384,384]{1,0:T(8,128)(2,1)S(1)}, bf16[384,384]{1,0:T(8,128)(2,1)}, u32[]{:S(2)}) %copy-start) | copy-done | bytes 294936
  26.7 3.1 %compare.10 = (f32[1,1152]{1,0:T(1,128)S(1)}, s32[1,128]{1,0:T(1,128)S(1)}) custom-call(bf16[384,384]{1,0:T(8,128)(2,1)S(1)} %copy-done, bf16[384,384]{1,0:T(8,128)(2,1)S(1)} %collective-permute-done.19.refs_1_, bf16[384,384]{1,0:T(8,128)(2,1)S(1)} %collective-permute-done.20.refs_2_, bf16[384,384]{1,0:T(8,128)(2,1)S(1)} %collective-permute-done.21.refs_3_, ...), custom_call_target="tpu_custom_call" | custom-call | tf_op jit(solution)/shard_map/compare/pallas_call | solution.py:258
  29.8 0.7 %collective-permute-done.30.refs_12_ = bf16[384,384]{1,0:T(8,128)(2,1)S(1)} collective-permute-done((bf16[384,384]{1,0:T(8,128)(2,1)S(1)}, bf16[384,384]{1,0:T(8,128)(2,1)S(1)}, u32[]{:S(2)}, u32[]{:S(2)}) %collective-permute-start.30) | collective-permute-done | bytes 294944 | tf_op jit(solution)/shard_map/ppermute | solution.py:21
  30.5 2.9 %collective-permute-done.18.refs_6_ = bf16[384,384]{1,0:T(8,128)(2,1)S(1)} collective-permute-done((bf16[384,384]{1,0:T(8,128)(2,1)}, bf16[384,384]{1,0:T(8,128)(2,1)S(1)}, u32[]{:S(2)}, u32[]{:S(2)}) %collective-permute-start.18) | collective-permute-done | bytes 294944 | tf_op jit(solution)/shard_map/ppermute | solution.py:21
  33.4 2.7 %collective-permute-done.25.refs_7_ = bf16[384,384]{1,0:T(8,128)(2,1)S(1)} collective-permute-done((bf16[384,384]{1,0:T(8,128)(2,1)S(1)}, bf16[384,384]{1,0:T(8,128)(2,1)S(1)}, u32[]{:S(2)}, u32[]{:S(2)}) %collective-permute-start.25) | collective-permute-done | bytes 294944 | tf_op jit(solution)/shard_map/ppermute | solution.py:21
  36.2 1.7 %collective-permute-start.24 = (bf16[384,384]{1,0:T(8,128)(2,1)S(1)}, bf16[384,384]{1,0:T(8,128)(2,1)S(1)}, u32[]{:S(2)}, u32[]{:S(2)}) collective-permute-start(bf16[384,384]{1,0:T(8,128)(2,1)S(1)} %collective-permute-done.18.refs_6_), channel_id=1, source_target_pairs={{0,2},{1,3},{2,0},{3,1},{4,6},{5,7},{6,4},{7,5},{8,10},{9,11},{10,... | collective-permute-start | bytes 884744 | tf_op jit(solution)/shard_map/ppermute | solution.py:21
  37.9 7.3 %compare.11 = (f32[1,1536]{1,0:T(1,128)S(1)}, s32[1,128]{1,0:T(1,128)S(1)}, bf16[1536,384]{1,0:T(8,128)(2,1)S(1)}, f32[1,1536]{1,0:T(1,128)S(1)}) custom-call(bf16[384,384]{1,0:T(8,128)(2,1)S(1)} %copy-done, bf16[384,384]{1,0:T(8,128)(2,1)S(1)} %collective-permute-done.19.refs_1_, bf16[384,384]{1,0:T(8,128)(2,1)S(1)} %collective-permute-done.20.refs_2_, ...), custom_call_target="tpu_custom_call" | custom-call | tf_op jit(solution)/shard_map/compare/pallas_call | solution.py:258
  45.2 0.0 copy-start.4
  45.2 0.0 copy-start.5
  45.2 0.0 copy-start.6
  45.2 0.3 collective-permute-done.24.refs_0_
  45.6 1.1 %compare.12 = (f32[1,1536]{1,0:T(1,128)S(1)}, s32[1,128]{1,0:T(1,128)S(1)}) custom-call(bf16[384,384]{1,0:T(8,128)(2,1)S(1)} %collective-permute-done.24.refs_0_, bf16[1536,384]{1,0:T(8,128)(2,1)S(1)} %get-tuple-element.71.refs_1_, f32[1,1536]{1,0:T(1,128)S(1)} %get-tuple-element.72.refs_2_, f32[1,1536]{1,0:T(1,128)S(1)} %get-tuple-element.69.refs_3_, ...), custom_call_target="tpu_custom_call" | custom-call | tf_op jit(solution)/shard_map/compare/pallas_call | solution.py:258
  46.7 0.5 collective-permute-done.32.refs_0_
  47.2 0.9 %compare.13 = (f32[1,384]{1,0:T(1,128)S(1)}, f32[1,384]{1,0:T(1,128)S(1)}, f32[1,384]{1,0:T(1,128)S(1)}, f32[1,384]{1,0:T(1,128)S(1)}, s32[1,128]{1,0:T(1,128)S(1)}) custom-call(bf16[384,384]{1,0:T(8,128)(2,1)S(1)} %collective-permute-done.32.refs_0_, bf16[1536,384]{1,0:T(8,128)(2,1)S(1)} %get-tuple-element.71.refs_1_, ...), custom_call_target="tpu_custom_call" | custom-call | tf_op jit(solution)/shard_map/compare/pallas_call | solution.py:258
  48.1 0.0 copy-start.2
  48.2 1.6 %collective-permute-start.33 = (f32[1,384]{1,0:T(1,128)S(1)}, f32[1,384]{1,0:T(1,128)S(1)}, u32[]{:S(2)}, u32[]{:S(2)}) collective-permute-start(f32[1,384]{1,0:T(1,128)S(1)} %get-tuple-element.77), channel_id=1, source_target_pairs={{0,4},{1,5},{2,6},{3,7},{4,0},{5,1},{6,2},{7,3},{8,12},{9,13},{10,... | collective-permute-start | bytes 4616 | tf_op jit(solution)/shard_map/ppermute | solution.py:21
  49.8 1.5 %collective-permute-start.34 = (f32[1,384]{1,0:T(1,128)S(1)}, f32[1,384]{1,0:T(1,128)S(1)}, u32[]{:S(2)}, u32[]{:S(2)}) collective-permute-start(f32[1,384]{1,0:T(1,128)S(1)} %get-tuple-element.78), channel_id=1, source_target_pairs={{0,8},{1,9},{2,10},{3,11},{4,12},{5,13},{6,14},{7,15},{8,0},{9,1},... | collective-permute-start | bytes 4616 | tf_op jit(solution)/shard_map/ppermute | solution.py:21
  51.3 1.4 %collective-permute-start.35 = (f32[1,384]{1,0:T(1,128)S(1)}, f32[1,384]{1,0:T(1,128)S(1)}, u32[]{:S(2)}, u32[]{:S(2)}) collective-permute-start(f32[1,384]{1,0:T(1,128)S(1)} %get-tuple-element.79), channel_id=1, source_target_pairs={{0,12},{1,13},{2,14},{3,15},{4,8},{5,9},{6,10},{7,11},{8,4},{9,5},... | collective-permute-start | bytes 4616 | tf_op jit(solution)/shard_map/ppermute | solution.py:21
  52.6 1.7 %collective-permute-done.34.refs_2_ = f32[1,384]{1,0:T(1,128)S(1)} collective-permute-done((f32[1,384]{1,0:T(1,128)S(1)}, f32[1,384]{1,0:T(1,128)S(1)}, u32[]{:S(2)}, u32[]{:S(2)}) %collective-permute-start.34) | collective-permute-done | bytes 1568 | tf_op jit(solution)/shard_map/ppermute | solution.py:21
  54.3 2.4 %collective-permute-done.35.refs_3_ = f32[1,384]{1,0:T(1,128)S(1)} collective-permute-done((f32[1,384]{1,0:T(1,128)S(1)}, f32[1,384]{1,0:T(1,128)S(1)}, u32[]{:S(2)}, u32[]{:S(2)}) %collective-permute-start.35) | collective-permute-done | bytes 1568 | tf_op jit(solution)/shard_map/ppermute | solution.py:21
  56.7 1.2 %place.3 = f32[1,1024]{1,0:T(1,128)} custom-call(s32[1,1024]{1,0:T(1,128)S(1)} %copy-done.2, f32[1,384]{1,0:T(1,128)S(1)} %get-tuple-element.76.refs_0_, f32[1,384]{1,0:T(1,128)S(1)} %collective-permute-done.33.refs_1_, f32[1,384]{1,0:T(1,128)S(1)} %collective-permute-done.34.refs_2_, f32[1,384]{1,0:T(1,128)S(1)} %collective-permute-done.35.refs_3_, ...), custom_call_target="tpu_custom_call" | custom-call | tf_op jit(solution)/shard_map/place/pallas_call | solution.py:294
  (22 shorter events, 0.1 us)
Async XLA Ops:
  4.2 15.3 %collective-permute-start.19 = (bf16[384,384]{1,0:T(8,128)(2,1)}, bf16[384,384]{1,0:T(8,128)(2,1)S(1)}, u32[]{:S(2)}, u32[]{:S(2)}) collective-permute-start(bf16[384,384]{1,0:T(8,128)(2,1)} %get-tuple-element.60), channel_id=1, source_target_pairs={{0,4},{1,5},{2,6},{3,7},{4,0},{5,1},{6,2},{7,3},{8,12},{9,13},{10,... | collective-permute-start | bytes 884744 | tf_op jit(solution)/shard_map/ppermute | solution.py:21
  7.3 12.2 %collective-permute-start.21 = (bf16[384,384]{1,0:T(8,128)(2,1)}, bf16[384,384]{1,0:T(8,128)(2,1)S(1)}, u32[]{:S(2)}, u32[]{:S(2)}) collective-permute-start(bf16[384,384]{1,0:T(8,128)(2,1)} %get-tuple-element.62.refs_0_), channel_id=1, source_target_pairs={{0,2},{1,3},{2,0},{3,1},{4,6},{5,7},{6,4},{7,5},{8,10},{9,11},{10,... | collective-permute-start | bytes 884744 | tf_op jit(solution)/shard_map/ppermute | solution.py:21
  8.8 16.4 %collective-permute-start.20 = (bf16[384,384]{1,0:T(8,128)(2,1)}, bf16[384,384]{1,0:T(8,128)(2,1)S(1)}, u32[]{:S(2)}, u32[]{:S(2)}) collective-permute-start(bf16[384,384]{1,0:T(8,128)(2,1)} %get-tuple-element.61), channel_id=1, source_target_pairs={{0,8},{1,9},{2,10},{3,11},{4,12},{5,13},{6,14},{7,15},{8,0},{9,1},... | collective-permute-start | bytes 884744 | tf_op jit(solution)/shard_map/ppermute | solution.py:21
  19.4 5.8 %collective-permute-start.22 = (bf16[384,384]{1,0:T(8,128)(2,1)}, bf16[384,384]{1,0:T(8,128)(2,1)S(1)}, u32[]{:S(2)}, u32[]{:S(2)}) collective-permute-start(bf16[384,384]{1,0:T(8,128)(2,1)} %get-tuple-element.62.refs_0_), channel_id=1, source_target_pairs={{0,1},{1,0},{2,3},{3,2},{4,5},{5,4},{6,7},{7,6},{8,9},{9,8},{10,11... | collective-permute-start | bytes 884744 | tf_op jit(solution)/shard_map/ppermute | solution.py:21
  19.4 5.8 %collective-permute-start.23 = (bf16[384,384]{1,0:T(8,128)(2,1)S(1)}, bf16[384,384]{1,0:T(8,128)(2,1)S(1)}, u32[]{:S(2)}, u32[]{:S(2)}) collective-permute-start(bf16[384,384]{1,0:T(8,128)(2,1)S(1)} %collective-permute-done.21.refs_3_), channel_id=1, source_target_pairs={{0,1},{1,0},{2,3},{3,2},{4,5},{5,4},{6,7},{7,6},{8,9},{9,8},{10,11... | collective-permute-start | bytes 884744 | tf_op jit(solution)/shard_map/ppermute | solution.py:21
  20.0 10.5 %collective-permute-start.30 = (bf16[384,384]{1,0:T(8,128)(2,1)S(1)}, bf16[384,384]{1,0:T(8,128)(2,1)S(1)}, u32[]{:S(2)}, u32[]{:S(2)}) collective-permute-start(bf16[384,384]{1,0:T(8,128)(2,1)S(1)} %collective-permute-done.19.refs_1_), channel_id=1, source_target_pairs={{0,2},{1,3},{2,0},{3,1},{4,6},{5,7},{6,4},{7,5},{8,10},{9,11},{10,... | collective-permute-start | bytes 884744 | tf_op jit(solution)/shard_map/ppermute | solution.py:21
  22.7 10.8 %collective-permute-start.18 = (bf16[384,384]{1,0:T(8,128)(2,1)}, bf16[384,384]{1,0:T(8,128)(2,1)S(1)}, u32[]{:S(2)}, u32[]{:S(2)}) collective-permute-start(bf16[384,384]{1,0:T(8,128)(2,1)} %get-tuple-element.58), channel_id=1, source_target_pairs={{0,12},{1,13},{2,14},{3,15},{4,8},{5,9},{6,10},{7,11},{8,4},{9,5},... | collective-permute-start | bytes 884744 | tf_op jit(solution)/shard_map/ppermute | solution.py:21
  25.1 11.0 %collective-permute-start.25 = (bf16[384,384]{1,0:T(8,128)(2,1)S(1)}, bf16[384,384]{1,0:T(8,128)(2,1)S(1)}, u32[]{:S(2)}, u32[]{:S(2)}) collective-permute-start(bf16[384,384]{1,0:T(8,128)(2,1)S(1)} %collective-permute-done.20.refs_2_), channel_id=1, source_target_pairs={{0,2},{1,3},{2,0},{3,1},{4,6},{5,7},{6,4},{7,5},{8,10},{9,11},{10,... | collective-permute-start | bytes 884744 | tf_op jit(solution)/shard_map/ppermute | solution.py:21
  25.2 10.9 %collective-permute-start.28 = (bf16[384,384]{1,0:T(8,128)(2,1)S(1)}, bf16[384,384]{1,0:T(8,128)(2,1)S(1)}, u32[]{:S(2)}, u32[]{:S(2)}) collective-permute-start(bf16[384,384]{1,0:T(8,128)(2,1)S(1)} %collective-permute-done.19.refs_1_), channel_id=1, source_target_pairs={{0,1},{1,0},{2,3},{3,2},{4,5},{5,4},{6,7},{7,6},{8,9},{9,8},{10,11... | collective-permute-start | bytes 884744 | tf_op jit(solution)/shard_map/ppermute | solution.py:21
  25.2 12.7 %collective-permute-start.29 = (bf16[384,384]{1,0:T(8,128)(2,1)S(1)}, bf16[384,384]{1,0:T(8,128)(2,1)S(1)}, u32[]{:S(2)}, u32[]{:S(2)}) collective-permute-start(bf16[384,384]{1,0:T(8,128)(2,1)S(1)} %collective-permute-done.20.refs_2_), channel_id=1, source_target_pairs={{0,1},{1,0},{2,3},{3,2},{4,5},{5,4},{6,7},{7,6},{8,9},{9,8},{10,11... | collective-permute-start | bytes 884744 | tf_op jit(solution)/shard_map/ppermute | solution.py:21
  25.7 1.0 %copy-start = (bf16[384,384]{1,0:T(8,128)(2,1)S(1)}, bf16[384,384]{1,0:T(8,128)(2,1)}, u32[]{:S(2)}) copy-start(bf16[384,384]{1,0:T(8,128)(2,1)} %get-tuple-element.62.refs_0_) | copy-start | bytes 884740
  30.5 7.4 %collective-permute-start.31 = (bf16[384,384]{1,0:T(8,128)(2,1)S(1)}, bf16[384,384]{1,0:T(8,128)(2,1)S(1)}, u32[]{:S(2)}, u32[]{:S(2)}) collective-permute-start(bf16[384,384]{1,0:T(8,128)(2,1)S(1)} %collective-permute-done.30.refs_12_), channel_id=1, source_target_pairs={{0,1},{1,0},{2,3},{3,2},{4,5},{5,4},{6,7},{7,6},{8,9},{9,8},{10,11... | collective-permute-start | bytes 884744 | tf_op jit(solution)/shard_map/ppermute | solution.py:21
  33.4 4.5 %collective-permute-start.26 = (bf16[384,384]{1,0:T(8,128)(2,1)S(1)}, bf16[384,384]{1,0:T(8,128)(2,1)S(1)}, u32[]{:S(2)}, u32[]{:S(2)}) collective-permute-start(bf16[384,384]{1,0:T(8,128)(2,1)S(1)} %collective-permute-done.18.refs_6_), channel_id=1, source_target_pairs={{0,1},{1,0},{2,3},{3,2},{4,5},{5,4},{6,7},{7,6},{8,9},{9,8},{10,11... | collective-permute-start | bytes 884744 | tf_op jit(solution)/shard_map/ppermute | solution.py:21
  36.2 1.8 %collective-permute-start.27 = (bf16[384,384]{1,0:T(8,128)(2,1)S(1)}, bf16[384,384]{1,0:T(8,128)(2,1)S(1)}, u32[]{:S(2)}, u32[]{:S(2)}) collective-permute-start(bf16[384,384]{1,0:T(8,128)(2,1)S(1)} %collective-permute-done.25.refs_7_), channel_id=1, source_target_pairs={{0,1},{1,0},{2,3},{3,2},{4,5},{5,4},{6,7},{7,6},{8,9},{9,8},{10,11... | collective-permute-start | bytes 884744 | tf_op jit(solution)/shard_map/ppermute | solution.py:21
  36.2 9.4 %collective-permute-start.24 = (bf16[384,384]{1,0:T(8,128)(2,1)S(1)}, bf16[384,384]{1,0:T(8,128)(2,1)S(1)}, u32[]{:S(2)}, u32[]{:S(2)}) collective-permute-start(bf16[384,384]{1,0:T(8,128)(2,1)S(1)} %collective-permute-done.18.refs_6_), channel_id=1, source_target_pairs={{0,2},{1,3},{2,0},{3,1},{4,6},{5,7},{6,4},{7,5},{8,10},{9,11},{10,... | collective-permute-start | bytes 884744 | tf_op jit(solution)/shard_map/ppermute | solution.py:21
  45.2 2.9 %copy-start.4 = (bf16[1024,384]{1,0:T(8,128)(2,1)S(1)}, bf16[1024,384]{1,0:T(8,128)(2,1)}, u32[]{:S(2)}) copy-start(bf16[1024,384]{1,0:T(8,128)(2,1)} %rows_hbm_ref.1) | copy-start | bytes 2359300
  45.2 2.9 %copy-start.5 = (s32[1024]{0:T(1024)S(1)}, s32[1024]{0:T(1024)}, u32[]{:S(2)}) copy-start(s32[1024]{0:T(1024)} %param.6) | copy-start | bytes 12292
  45.2 2.9 %copy-start.6 = (s32[1024]{0:T(1024)S(1)}, s32[1024]{0:T(1024)}, u32[]{:S(2)}) copy-start(s32[1024]{0:T(1024)} %param.7) | copy-start | bytes 12292
  45.6 1.6 %collective-permute-start.32 = (bf16[384,384]{1,0:T(8,128)(2,1)S(1)}, bf16[384,384]{1,0:T(8,128)(2,1)S(1)}, u32[]{:S(2)}, u32[]{:S(2)}) collective-permute-start(bf16[384,384]{1,0:T(8,128)(2,1)S(1)} %collective-permute-done.24.refs_0_), channel_id=1, source_target_pairs={{0,1},{1,0},{2,3},{3,2},{4,5},{5,4},{6,7},{7,6},{8,9},{9,8},{10,11... | collective-permute-start | bytes 884744 | tf_op jit(solution)/shard_map/ppermute | solution.py:21
  48.1 8.5 %copy-start.2 = (s32[1,1024]{1,0:T(1,128)S(1)}, s32[1,1024]{1,0:T(1,128)}, u32[]{:S(2)}) copy-start(s32[1,1024]{1,0:T(1,128)} %get-tuple-element.57.key_ref) | copy-start | bytes 12292
  48.2 4.5 %collective-permute-start.33 = (f32[1,384]{1,0:T(1,128)S(1)}, f32[1,384]{1,0:T(1,128)S(1)}, u32[]{:S(2)}, u32[]{:S(2)}) collective-permute-start(f32[1,384]{1,0:T(1,128)S(1)} %get-tuple-element.77), channel_id=1, source_target_pairs={{0,4},{1,5},{2,6},{3,7},{4,0},{5,1},{6,2},{7,3},{8,12},{9,13},{10,... | collective-permute-start | bytes 4616 | tf_op jit(solution)/shard_map/ppermute | solution.py:21
  49.8 4.5 %collective-permute-start.34 = (f32[1,384]{1,0:T(1,128)S(1)}, f32[1,384]{1,0:T(1,128)S(1)}, u32[]{:S(2)}, u32[]{:S(2)}) collective-permute-start(f32[1,384]{1,0:T(1,128)S(1)} %get-tuple-element.78), channel_id=1, source_target_pairs={{0,8},{1,9},{2,10},{3,11},{4,12},{5,13},{6,14},{7,15},{8,0},{9,1},... | collective-permute-start | bytes 4616 | tf_op jit(solution)/shard_map/ppermute | solution.py:21
  51.3 5.4 %collective-permute-start.35 = (f32[1,384]{1,0:T(1,128)S(1)}, f32[1,384]{1,0:T(1,128)S(1)}, u32[]{:S(2)}, u32[]{:S(2)}) collective-permute-start(f32[1,384]{1,0:T(1,128)S(1)} %get-tuple-element.79), channel_id=1, source_target_pairs={{0,12},{1,13},{2,14},{3,15},{4,8},{5,9},{6,10},{7,11},{8,4},{9,5},... | collective-permute-start | bytes 4616 | tf_op jit(solution)/shard_map/ppermute | solution.py:21

commit v4 on v3

--- a/solution.py
+++ b/solution.py
@@ -274,7 +274,7 @@
     gathered = jnp.zeros((16, keys.shape[1]), jnp.float32)
     line = lax.broadcasted_iota(jnp.int32, (16, tile), 0)
     for chunk in range(chunks):
-        value = refs[chunk][...]
+        value = refs[chunks - 1 - chunk][...]
         first = value.astype(jnp.bfloat16).astype(jnp.float32)
         second = (value - first).astype(jnp.bfloat16).astype(jnp.float32)
         third = value - first - second
@@ -298,7 +298,7 @@
         out_specs=vmem,
         compiler_params=pltpu.CompilerParams(vmem_limit_bytes=VMEM_LIMIT),
         name="place",
-    )(keys, *values, *instead)
+    )(keys, *reversed(values), *instead)
 
 
 def swap(block, mask):

time: 58 us -> 56.6 us (0.976)
  waiting for transfers between devices: 19.3 us -> 17.8 us
    ppermute x18, waiting for transfers between devices: 19.3 us -> 17.8 us  [from_partner(): return lax.ppermute(value, axis, pairs)]
where the time goes in v4:
time: 56.6 us; the launch traced here: 56.4 us
  starting transfers between devices  19.7 us (35%)
  waiting for transfers between devices  17.8 us (31%)
  Pallas kernels  17.7 us (31%)
  local copies, waits for them, and re-layouts  0.99 us (2%)
    ppermute x18, starting transfers between devices, from_partner(): return lax.ppermute(value, axis, pairs)  19.7 us
    ppermute x18, waiting for transfers between devices, from_partner(): return lax.ppermute(value, axis, pairs)  17.8 us
    pallas_call x4, Pallas kernels, compare(): pl.pallas_call(functools.partial(compare_kernel, plan), out_shape=outs, i...  12.4 us
    pallas_call x1, Pallas kernels, route(): pl.pallas_call(functools.partial(route_kernel, cuts), out_shape=shapes +...  4.16 us
    pallas_call x1, Pallas kernels, place(): pl.pallas_call(functools.partial(place_kernel, chunks, tile), out_shape=j...  1.18 us
  transfers between devices with their start and end apart: 18, of which 8 were waited for; matrix products, arithmetic and copies ran while one was open for 0% of the time, Pallas kernels for 20%

profile of v4, /device:TPU:0, one launch (start us, length us, event | category | flops | bytes accessed | tf_op | source)
XLA Modules:
  0.0 56.4 jit_solution(8848406570130097388)
XLA Ops:
  0.0 4.2 %route.3 = (bf16[384,384]{1,0:T(8,128)(2,1)}, bf16[384,384]{1,0:T(8,128)(2,1)}, bf16[384,384]{1,0:T(8,128)(2,1)}, bf16[384,384]{1,0:T(8,128)(2,1)}, s32[1,1024]{1,0:T(1,128)}) custom-call(s32[1]{0:T(128)} %bitcast.2.home_ref, bf16[1024,384]{1,0:T(8,128)(2,1)} %rows_hbm_ref.1, s32[1,1024]{1,0:T(1,128)} %bitcast.9, s32[1,1024]{1,0:T(1,128)} %bitcast.11), custom_call_target="tpu_custom_call" | custom-call | tf_op jit(solution)/shard_map/route/pallas_call | solution.py:123
  4.2 3.1 %collective-permute-start.19 = (bf16[384,384]{1,0:T(8,128)(2,1)}, bf16[384,384]{1,0:T(8,128)(2,1)S(1)}, u32[]{:S(2)}, u32[]{:S(2)}) collective-permute-start(bf16[384,384]{1,0:T(8,128)(2,1)} %get-tuple-element.60), channel_id=1, source_target_pairs={{0,4},{1,5},{2,6},{3,7},{4,0},{5,1},{6,2},{7,3},{8,12},{9,13},{10,... | collective-permute-start | bytes 884744 | tf_op jit(solution)/shard_map/ppermute | solution.py:21
  7.3 1.5 %collective-permute-start.21 = (bf16[384,384]{1,0:T(8,128)(2,1)}, bf16[384,384]{1,0:T(8,128)(2,1)S(1)}, u32[]{:S(2)}, u32[]{:S(2)}) collective-permute-start(bf16[384,384]{1,0:T(8,128)(2,1)} %get-tuple-element.62.refs_0_), channel_id=1, source_target_pairs={{0,2},{1,3},{2,0},{3,1},{4,6},{5,7},{6,4},{7,5},{8,10},{9,11},{10,... | collective-permute-start | bytes 884744 | tf_op jit(solution)/shard_map/ppermute | solution.py:21
  8.8 2.6 %collective-permute-start.20 = (bf16[384,384]{1,0:T(8,128)(2,1)}, bf16[384,384]{1,0:T(8,128)(2,1)S(1)}, u32[]{:S(2)}, u32[]{:S(2)}) collective-permute-start(bf16[384,384]{1,0:T(8,128)(2,1)} %get-tuple-element.61), channel_id=1, source_target_pairs={{0,8},{1,9},{2,10},{3,11},{4,12},{5,13},{6,14},{7,15},{8,0},{9,1},... | collective-permute-start | bytes 884744 | tf_op jit(solution)/shard_map/ppermute | solution.py:21
  11.4 8.1 %collective-permute-done.19.refs_1_ = bf16[384,384]{1,0:T(8,128)(2,1)S(1)} collective-permute-done((bf16[384,384]{1,0:T(8,128)(2,1)}, bf16[384,384]{1,0:T(8,128)(2,1)S(1)}, u32[]{:S(2)}, u32[]{:S(2)}) %collective-permute-start.19) | collective-permute-done | bytes 294944 | tf_op jit(solution)/shard_map/ppermute | solution.py:21
  19.4 0.0 collective-permute-start.22
  19.4 0.5 collective-permute-start.23
  20.0 2.7 %collective-permute-start.30 = (bf16[384,384]{1,0:T(8,128)(2,1)S(1)}, bf16[384,384]{1,0:T(8,128)(2,1)S(1)}, u32[]{:S(2)}, u32[]{:S(2)}) collective-permute-start(bf16[384,384]{1,0:T(8,128)(2,1)S(1)} %collective-permute-done.19.refs_1_), channel_id=1, source_target_pairs={{0,2},{1,3},{2,0},{3,1},{4,6},{5,7},{6,4},{7,5},{8,10},{9,11},{10,... | collective-permute-start | bytes 884744 | tf_op jit(solution)/shard_map/ppermute | solution.py:21
  22.7 2.5 %collective-permute-start.18 = (bf16[384,384]{1,0:T(8,128)(2,1)}, bf16[384,384]{1,0:T(8,128)(2,1)S(1)}, u32[]{:S(2)}, u32[]{:S(2)}) collective-permute-start(bf16[384,384]{1,0:T(8,128)(2,1)} %get-tuple-element.58), channel_id=1, source_target_pairs={{0,12},{1,13},{2,14},{3,15},{4,8},{5,9},{6,10},{7,11},{8,4},{9,5},... | collective-permute-start | bytes 884744 | tf_op jit(solution)/shard_map/ppermute | solution.py:21
  25.1 0.1 collective-permute-start.25
  25.2 0.5 collective-permute-start.29
  25.7 1.0 %copy-done = bf16[384,384]{1,0:T(8,128)(2,1)S(1)} copy-done((bf16[384,384]{1,0:T(8,128)(2,1)S(1)}, bf16[384,384]{1,0:T(8,128)(2,1)}, u32[]{:S(2)}) %copy-start) | copy-done | bytes 294936
  26.7 3.1 %compare.10 = (f32[1,1152]{1,0:T(1,128)S(1)}, s32[1,128]{1,0:T(1,128)S(1)}) custom-call(bf16[384,384]{1,0:T(8,128)(2,1)S(1)} %copy-done, bf16[384,384]{1,0:T(8,128)(2,1)S(1)} %collective-permute-done.19.refs_1_, bf16[384,384]{1,0:T(8,128)(2,1)S(1)} %collective-permute-done.20.refs_2_, bf16[384,384]{1,0:T(8,128)(2,1)S(1)} %collective-permute-done.21.refs_3_, ...), custom_call_target="tpu_custom_call" | custom-call | tf_op jit(solution)/shard_map/compare/pallas_call | solution.py:258
  29.8 0.7 %collective-permute-done.30.refs_12_ = bf16[384,384]{1,0:T(8,128)(2,1)S(1)} collective-permute-done((bf16[384,384]{1,0:T(8,128)(2,1)S(1)}, bf16[384,384]{1,0:T(8,128)(2,1)S(1)}, u32[]{:S(2)}, u32[]{:S(2)}) %collective-permute-start.30) | collective-permute-done | bytes 294944 | tf_op jit(solution)/shard_map/ppermute | solution.py:21
  30.5 2.9 %collective-permute-done.18.refs_6_ = bf16[384,384]{1,0:T(8,128)(2,1)S(1)} collective-permute-done((bf16[384,384]{1,0:T(8,128)(2,1)}, bf16[384,384]{1,0:T(8,128)(2,1)S(1)}, u32[]{:S(2)}, u32[]{:S(2)}) %collective-permute-start.18) | collective-permute-done | bytes 294944 | tf_op jit(solution)/shard_map/ppermute | solution.py:21
  33.4 2.7 %collective-permute-done.25.refs_7_ = bf16[384,384]{1,0:T(8,128)(2,1)S(1)} collective-permute-done((bf16[384,384]{1,0:T(8,128)(2,1)S(1)}, bf16[384,384]{1,0:T(8,128)(2,1)S(1)}, u32[]{:S(2)}, u32[]{:S(2)}) %collective-permute-start.25) | collective-permute-done | bytes 294944 | tf_op jit(solution)/shard_map/ppermute | solution.py:21
  36.2 1.7 %collective-permute-start.24 = (bf16[384,384]{1,0:T(8,128)(2,1)S(1)}, bf16[384,384]{1,0:T(8,128)(2,1)S(1)}, u32[]{:S(2)}, u32[]{:S(2)}) collective-permute-start(bf16[384,384]{1,0:T(8,128)(2,1)S(1)} %collective-permute-done.18.refs_6_), channel_id=1, source_target_pairs={{0,2},{1,3},{2,0},{3,1},{4,6},{5,7},{6,4},{7,5},{8,10},{9,11},{10,... | collective-permute-start | bytes 884744 | tf_op jit(solution)/shard_map/ppermute | solution.py:21
  37.9 7.3 %compare.11 = (f32[1,1536]{1,0:T(1,128)S(1)}, s32[1,128]{1,0:T(1,128)S(1)}, bf16[1536,384]{1,0:T(8,128)(2,1)S(1)}, f32[1,1536]{1,0:T(1,128)S(1)}) custom-call(bf16[384,384]{1,0:T(8,128)(2,1)S(1)} %copy-done, bf16[384,384]{1,0:T(8,128)(2,1)S(1)} %collective-permute-done.19.refs_1_, bf16[384,384]{1,0:T(8,128)(2,1)S(1)} %collective-permute-done.20.refs_2_, ...), custom_call_target="tpu_custom_call" | custom-call | tf_op jit(solution)/shard_map/compare/pallas_call | solution.py:258
  45.2 0.0 copy-start.4
  45.2 0.0 copy-start.5
  45.2 0.0 copy-start.6
  45.2 0.3 collective-permute-done.24.refs_0_
  45.6 1.1 %compare.12 = (f32[1,1536]{1,0:T(1,128)S(1)}, s32[1,128]{1,0:T(1,128)S(1)}) custom-call(bf16[384,384]{1,0:T(8,128)(2,1)S(1)} %collective-permute-done.24.refs_0_, bf16[1536,384]{1,0:T(8,128)(2,1)S(1)} %get-tuple-element.71.refs_1_, f32[1,1536]{1,0:T(1,128)S(1)} %get-tuple-element.72.refs_2_, f32[1,1536]{1,0:T(1,128)S(1)} %get-tuple-element.69.refs_3_, ...), custom_call_target="tpu_custom_call" | custom-call | tf_op jit(solution)/shard_map/compare/pallas_call | solution.py:258
  46.7 0.5 collective-permute-done.32.refs_0_
  47.2 0.9 %compare.13 = (f32[1,384]{1,0:T(1,128)S(1)}, f32[1,384]{1,0:T(1,128)S(1)}, f32[1,384]{1,0:T(1,128)S(1)}, f32[1,384]{1,0:T(1,128)S(1)}, s32[1,128]{1,0:T(1,128)S(1)}) custom-call(bf16[384,384]{1,0:T(8,128)(2,1)S(1)} %collective-permute-done.32.refs_0_, bf16[1536,384]{1,0:T(8,128)(2,1)S(1)} %get-tuple-element.71.refs_1_, ...), custom_call_target="tpu_custom_call" | custom-call | tf_op jit(solution)/shard_map/compare/pallas_call | solution.py:258
  48.1 0.0 copy-start.2
  48.2 2.5 %collective-permute-start.33 = (f32[1,384]{1,0:T(1,128)S(1)}, f32[1,384]{1,0:T(1,128)S(1)}, u32[]{:S(2)}, u32[]{:S(2)}) collective-permute-start(f32[1,384]{1,0:T(1,128)S(1)} %get-tuple-element.76), channel_id=1, source_target_pairs={{0,12},{1,13},{2,14},{3,15},{4,8},{5,9},{6,10},{7,11},{8,4},{9,5},... | collective-permute-start | bytes 4616 | tf_op jit(solution)/shard_map/ppermute | solution.py:21
  50.7 0.6 %collective-permute-start.34 = (f32[1,384]{1,0:T(1,128)S(1)}, f32[1,384]{1,0:T(1,128)S(1)}, u32[]{:S(2)}, u32[]{:S(2)}) collective-permute-start(f32[1,384]{1,0:T(1,128)S(1)} %get-tuple-element.77), channel_id=1, source_target_pairs={{0,8},{1,9},{2,10},{3,11},{4,12},{5,13},{6,14},{7,15},{8,0},{9,1},... | collective-permute-start | bytes 4616 | tf_op jit(solution)/shard_map/ppermute | solution.py:21
  51.3 1.3 %collective-permute-start.35 = (f32[1,384]{1,0:T(1,128)S(1)}, f32[1,384]{1,0:T(1,128)S(1)}, u32[]{:S(2)}, u32[]{:S(2)}) collective-permute-start(f32[1,384]{1,0:T(1,128)S(1)} %get-tuple-element.78), channel_id=1, source_target_pairs={{0,4},{1,5},{2,6},{3,7},{4,0},{5,1},{6,2},{7,3},{8,12},{9,13},{10,... | collective-permute-start | bytes 4616 | tf_op jit(solution)/shard_map/ppermute | solution.py:21
  52.6 1.0 %collective-permute-done.33.refs_0_ = f32[1,384]{1,0:T(1,128)S(1)} collective-permute-done((f32[1,384]{1,0:T(1,128)S(1)}, f32[1,384]{1,0:T(1,128)S(1)}, u32[]{:S(2)}, u32[]{:S(2)}) %collective-permute-start.33) | collective-permute-done | bytes 1568 | tf_op jit(solution)/shard_map/ppermute | solution.py:21
  53.6 1.6 %collective-permute-done.34.refs_1_ = f32[1,384]{1,0:T(1,128)S(1)} collective-permute-done((f32[1,384]{1,0:T(1,128)S(1)}, f32[1,384]{1,0:T(1,128)S(1)}, u32[]{:S(2)}, u32[]{:S(2)}) %collective-permute-start.34) | collective-permute-done | bytes 1568 | tf_op jit(solution)/shard_map/ppermute | solution.py:21
  55.2 1.2 %place.3 = f32[1,1024]{1,0:T(1,128)} custom-call(s32[1,1024]{1,0:T(1,128)S(1)} %copy-done.2, f32[1,384]{1,0:T(1,128)S(1)} %collective-permute-done.33.refs_0_, f32[1,384]{1,0:T(1,128)S(1)} %collective-permute-done.34.refs_1_, f32[1,384]{1,0:T(1,128)S(1)} %collective-permute-done.35.refs_2_, f32[1,384]{1,0:T(1,128)S(1)} %get-tuple-element.79.refs_3_, ...), custom_call_target="tpu_custom_call" | custom-call | tf_op jit(solution)/shard_map/place/pallas_call | solution.py:294
  (22 shorter events, 0.1 us)
Async XLA Ops:
  4.2 15.3 %collective-permute-start.19 = (bf16[384,384]{1,0:T(8,128)(2,1)}, bf16[384,384]{1,0:T(8,128)(2,1)S(1)}, u32[]{:S(2)}, u32[]{:S(2)}) collective-permute-start(bf16[384,384]{1,0:T(8,128)(2,1)} %get-tuple-element.60), channel_id=1, source_target_pairs={{0,4},{1,5},{2,6},{3,7},{4,0},{5,1},{6,2},{7,3},{8,12},{9,13},{10,... | collective-permute-start | bytes 884744 | tf_op jit(solution)/shard_map/ppermute | solution.py:21
  7.3 12.2 %collective-permute-start.21 = (bf16[384,384]{1,0:T(8,128)(2,1)}, bf16[384,384]{1,0:T(8,128)(2,1)S(1)}, u32[]{:S(2)}, u32[]{:S(2)}) collective-permute-start(bf16[384,384]{1,0:T(8,128)(2,1)} %get-tuple-element.62.refs_0_), channel_id=1, source_target_pairs={{0,2},{1,3},{2,0},{3,1},{4,6},{5,7},{6,4},{7,5},{8,10},{9,11},{10,... | collective-permute-start | bytes 884744 | tf_op jit(solution)/shard_map/ppermute | solution.py:21
  8.8 16.4 %collective-permute-start.20 = (bf16[384,384]{1,0:T(8,128)(2,1)}, bf16[384,384]{1,0:T(8,128)(2,1)S(1)}, u32[]{:S(2)}, u32[]{:S(2)}) collective-permute-start(bf16[384,384]{1,0:T(8,128)(2,1)} %get-tuple-element.61), channel_id=1, source_target_pairs={{0,8},{1,9},{2,10},{3,11},{4,12},{5,13},{6,14},{7,15},{8,0},{9,1},... | collective-permute-start | bytes 884744 | tf_op jit(solution)/shard_map/ppermute | solution.py:21
  19.4 5.8 %collective-permute-start.22 = (bf16[384,384]{1,0:T(8,128)(2,1)}, bf16[384,384]{1,0:T(8,128)(2,1)S(1)}, u32[]{:S(2)}, u32[]{:S(2)}) collective-permute-start(bf16[384,384]{1,0:T(8,128)(2,1)} %get-tuple-element.62.refs_0_), channel_id=1, source_target_pairs={{0,1},{1,0},{2,3},{3,2},{4,5},{5,4},{6,7},{7,6},{8,9},{9,8},{10,11... | collective-permute-start | bytes 884744 | tf_op jit(solution)/shard_map/ppermute | solution.py:21
  19.4 5.8 %collective-permute-start.23 = (bf16[384,384]{1,0:T(8,128)(2,1)S(1)}, bf16[384,384]{1,0:T(8,128)(2,1)S(1)}, u32[]{:S(2)}, u32[]{:S(2)}) collective-permute-start(bf16[384,384]{1,0:T(8,128)(2,1)S(1)} %collective-permute-done.21.refs_3_), channel_id=1, source_target_pairs={{0,1},{1,0},{2,3},{3,2},{4,5},{5,4},{6,7},{7,6},{8,9},{9,8},{10,11... | collective-permute-start | bytes 884744 | tf_op jit(solution)/shard_map/ppermute | solution.py:21
  20.0 10.5 %collective-permute-start.30 = (bf16[384,384]{1,0:T(8,128)(2,1)S(1)}, bf16[384,384]{1,0:T(8,128)(2,1)S(1)}, u32[]{:S(2)}, u32[]{:S(2)}) collective-permute-start(bf16[384,384]{1,0:T(8,128)(2,1)S(1)} %collective-permute-done.19.refs_1_), channel_id=1, source_target_pairs={{0,2},{1,3},{2,0},{3,1},{4,6},{5,7},{6,4},{7,5},{8,10},{9,11},{10,... | collective-permute-start | bytes 884744 | tf_op jit(solution)/shard_map/ppermute | solution.py:21
  22.7 10.8 %collective-permute-start.18 = (bf16[384,384]{1,0:T(8,128)(2,1)}, bf16[384,384]{1,0:T(8,128)(2,1)S(1)}, u32[]{:S(2)}, u32[]{:S(2)}) collective-permute-start(bf16[384,384]{1,0:T(8,128)(2,1)} %get-tuple-element.58), channel_id=1, source_target_pairs={{0,12},{1,13},{2,14},{3,15},{4,8},{5,9},{6,10},{7,11},{8,4},{9,5},... | collective-permute-start | bytes 884744 | tf_op jit(solution)/shard_map/ppermute | solution.py:21
  25.1 11.0 %collective-permute-start.25 = (bf16[384,384]{1,0:T(8,128)(2,1)S(1)}, bf16[384,384]{1,0:T(8,128)(2,1)S(1)}, u32[]{:S(2)}, u32[]{:S(2)}) collective-permute-start(bf16[384,384]{1,0:T(8,128)(2,1)S(1)} %collective-permute-done.20.refs_2_), channel_id=1, source_target_pairs={{0,2},{1,3},{2,0},{3,1},{4,6},{5,7},{6,4},{7,5},{8,10},{9,11},{10,... | collective-permute-start | bytes 884744 | tf_op jit(solution)/shard_map/ppermute | solution.py:21
  25.2 10.9 %collective-permute-start.28 = (bf16[384,384]{1,0:T(8,128)(2,1)S(1)}, bf16[384,384]{1,0:T(8,128)(2,1)S(1)}, u32[]{:S(2)}, u32[]{:S(2)}) collective-permute-start(bf16[384,384]{1,0:T(8,128)(2,1)S(1)} %collective-permute-done.19.refs_1_), channel_id=1, source_target_pairs={{0,1},{1,0},{2,3},{3,2},{4,5},{5,4},{6,7},{7,6},{8,9},{9,8},{10,11... | collective-permute-start | bytes 884744 | tf_op jit(solution)/shard_map/ppermute | solution.py:21
  25.2 12.7 %collective-permute-start.29 = (bf16[384,384]{1,0:T(8,128)(2,1)S(1)}, bf16[384,384]{1,0:T(8,128)(2,1)S(1)}, u32[]{:S(2)}, u32[]{:S(2)}) collective-permute-start(bf16[384,384]{1,0:T(8,128)(2,1)S(1)} %collective-permute-done.20.refs_2_), channel_id=1, source_target_pairs={{0,1},{1,0},{2,3},{3,2},{4,5},{5,4},{6,7},{7,6},{8,9},{9,8},{10,11... | collective-permute-start | bytes 884744 | tf_op jit(solution)/shard_map/ppermute | solution.py:21
  25.7 1.0 %copy-start = (bf16[384,384]{1,0:T(8,128)(2,1)S(1)}, bf16[384,384]{1,0:T(8,128)(2,1)}, u32[]{:S(2)}) copy-start(bf16[384,384]{1,0:T(8,128)(2,1)} %get-tuple-element.62.refs_0_) | copy-start | bytes 884740
  30.5 7.4 %collective-permute-start.31 = (bf16[384,384]{1,0:T(8,128)(2,1)S(1)}, bf16[384,384]{1,0:T(8,128)(2,1)S(1)}, u32[]{:S(2)}, u32[]{:S(2)}) collective-permute-start(bf16[384,384]{1,0:T(8,128)(2,1)S(1)} %collective-permute-done.30.refs_12_), channel_id=1, source_target_pairs={{0,1},{1,0},{2,3},{3,2},{4,5},{5,4},{6,7},{7,6},{8,9},{9,8},{10,11... | collective-permute-start | bytes 884744 | tf_op jit(solution)/shard_map/ppermute | solution.py:21
  33.4 4.5 %collective-permute-start.26 = (bf16[384,384]{1,0:T(8,128)(2,1)S(1)}, bf16[384,384]{1,0:T(8,128)(2,1)S(1)}, u32[]{:S(2)}, u32[]{:S(2)}) collective-permute-start(bf16[384,384]{1,0:T(8,128)(2,1)S(1)} %collective-permute-done.18.refs_6_), channel_id=1, source_target_pairs={{0,1},{1,0},{2,3},{3,2},{4,5},{5,4},{6,7},{7,6},{8,9},{9,8},{10,11... | collective-permute-start | bytes 884744 | tf_op jit(solution)/shard_map/ppermute | solution.py:21
  36.2 1.8 %collective-permute-start.27 = (bf16[384,384]{1,0:T(8,128)(2,1)S(1)}, bf16[384,384]{1,0:T(8,128)(2,1)S(1)}, u32[]{:S(2)}, u32[]{:S(2)}) collective-permute-start(bf16[384,384]{1,0:T(8,128)(2,1)S(1)} %collective-permute-done.25.refs_7_), channel_id=1, source_target_pairs={{0,1},{1,0},{2,3},{3,2},{4,5},{5,4},{6,7},{7,6},{8,9},{9,8},{10,11... | collective-permute-start | bytes 884744 | tf_op jit(solution)/shard_map/ppermute | solution.py:21
  36.2 9.4 %collective-permute-start.24 = (bf16[384,384]{1,0:T(8,128)(2,1)S(1)}, bf16[384,384]{1,0:T(8,128)(2,1)S(1)}, u32[]{:S(2)}, u32[]{:S(2)}) collective-permute-start(bf16[384,384]{1,0:T(8,128)(2,1)S(1)} %collective-permute-done.18.refs_6_), channel_id=1, source_target_pairs={{0,2},{1,3},{2,0},{3,1},{4,6},{5,7},{6,4},{7,5},{8,10},{9,11},{10,... | collective-permute-start | bytes 884744 | tf_op jit(solution)/shard_map/ppermute | solution.py:21
  45.2 2.9 %copy-start.4 = (bf16[1024,384]{1,0:T(8,128)(2,1)S(1)}, bf16[1024,384]{1,0:T(8,128)(2,1)}, u32[]{:S(2)}) copy-start(bf16[1024,384]{1,0:T(8,128)(2,1)} %rows_hbm_ref.1) | copy-start | bytes 2359300
  45.2 2.9 %copy-start.5 = (s32[1024]{0:T(1024)S(1)}, s32[1024]{0:T(1024)}, u32[]{:S(2)}) copy-start(s32[1024]{0:T(1024)} %param.6) | copy-start | bytes 12292
  45.2 2.9 %copy-start.6 = (s32[1024]{0:T(1024)S(1)}, s32[1024]{0:T(1024)}, u32[]{:S(2)}) copy-start(s32[1024]{0:T(1024)} %param.7) | copy-start | bytes 12292
  45.6 1.6 %collective-permute-start.32 = (bf16[384,384]{1,0:T(8,128)(2,1)S(1)}, bf16[384,384]{1,0:T(8,128)(2,1)S(1)}, u32[]{:S(2)}, u32[]{:S(2)}) collective-permute-start(bf16[384,384]{1,0:T(8,128)(2,1)S(1)} %collective-permute-done.24.refs_0_), channel_id=1, source_target_pairs={{0,1},{1,0},{2,3},{3,2},{4,5},{5,4},{6,7},{7,6},{8,9},{9,8},{10,11... | collective-permute-start | bytes 884744 | tf_op jit(solution)/shard_map/ppermute | solution.py:21
  48.1 7.1 %copy-start.2 = (s32[1,1024]{1,0:T(1,128)S(1)}, s32[1,1024]{1,0:T(1,128)}, u32[]{:S(2)}) copy-start(s32[1,1024]{1,0:T(1,128)} %get-tuple-element.57.key_ref) | copy-start | bytes 12292
  48.2 5.4 %collective-permute-start.33 = (f32[1,384]{1,0:T(1,128)S(1)}, f32[1,384]{1,0:T(1,128)S(1)}, u32[]{:S(2)}, u32[]{:S(2)}) collective-permute-start(f32[1,384]{1,0:T(1,128)S(1)} %get-tuple-element.76), channel_id=1, source_target_pairs={{0,12},{1,13},{2,14},{3,15},{4,8},{5,9},{6,10},{7,11},{8,4},{9,5},... | collective-permute-start | bytes 4616 | tf_op jit(solution)/shard_map/ppermute | solution.py:21
  50.7 4.5 %collective-permute-start.34 = (f32[1,384]{1,0:T(1,128)S(1)}, f32[1,384]{1,0:T(1,128)S(1)}, u32[]{:S(2)}, u32[]{:S(2)}) collective-permute-start(f32[1,384]{1,0:T(1,128)S(1)} %get-tuple-element.77), channel_id=1, source_target_pairs={{0,8},{1,9},{2,10},{3,11},{4,12},{5,13},{6,14},{7,15},{8,0},{9,1},... | collective-permute-start | bytes 4616 | tf_op jit(solution)/shard_map/ppermute | solution.py:21
  51.3 3.9 %collective-permute-start.35 = (f32[1,384]{1,0:T(1,128)S(1)}, f32[1,384]{1,0:T(1,128)S(1)}, u32[]{:S(2)}, u32[]{:S(2)}) collective-permute-start(f32[1,384]{1,0:T(1,128)S(1)} %get-tuple-element.78), channel_id=1, source_target_pairs={{0,4},{1,5},{2,6},{3,7},{4,0},{5,1},{6,2},{7,3},{8,12},{9,13},{10,... | collective-permute-start | bytes 4616 | tf_op jit(solution)/shard_map/ppermute | solution.py:21

commit v5 on v4

--- a/solution.py
+++ b/solution.py
@@ -13,7 +13,7 @@
 LANES = 512
 WHOLE = 5 * 1024 * 1024
 VMEM_LIMIT = 48 * 1024 * 1024
-ROUTE_VMEM_LIMIT = 60 * 1024 * 1024
+ROUTE_VMEM_LIMIT = 48 * 1024 * 1024
 
 
 def from_partner(value, axis, mask):

time: 56.6 us -> 55.4 us (0.979)
  Pallas kernels: 17.7 us -> 16.7 us
  local copies, waits for them, and re-layouts: 0.99 us -> 0.02 us
  waiting for transfers between devices: 17.8 us -> 18.6 us
    unnamed x10 -> x6, local copies, waits for them, and re-layouts: 0.99 us -> 0.02 us
    pallas_call x1, Pallas kernels: 4.16 us -> 3.22 us  [route(): pl.pallas_call(functools.partial(route_kernel, cuts), out_shape=shapes +...]
    ppermute x18, waiting for transfers between devices: 17.8 us -> 18.6 us  [from_partner(): return lax.ppermute(value, axis, pairs)]
  transfers between devices with their start and end apart: 18 -> 18, of which waited for: 8 -> 8; matrix products, arithmetic and copies ran while one was open for 0% -> 0% of each run, Pallas kernels for 20% -> 21%
where the time goes in v5:
time: 55.4 us; the launch traced here: 55.2 us
  starting transfers between devices  19.7 us (36%)
  waiting for transfers between devices  18.6 us (34%)
  Pallas kernels  16.7 us (30%)
    ppermute x18, starting transfers between devices, from_partner(): return lax.ppermute(value, axis, pairs)  19.7 us
    ppermute x18, waiting for transfers between devices, from_partner(): return lax.ppermute(value, axis, pairs)  18.6 us
    pallas_call x4, Pallas kernels, compare(): pl.pallas_call(functools.partial(compare_kernel, plan), out_shape=outs, i...  12.4 us
    pallas_call x1, Pallas kernels, route(): pl.pallas_call(functools.partial(route_kernel, cuts), out_shape=shapes +...  3.22 us
    pallas_call x1, Pallas kernels, place(): pl.pallas_call(functools.partial(place_kernel, chunks, tile), out_shape=j...  1.18 us
  transfers between devices with their start and end apart: 18, of which 8 were waited for; matrix products, arithmetic and copies ran while one was open for 0% of the time, Pallas kernels for 21%

profile of v5, /device:TPU:0, one launch (start us, length us, event | category | flops | bytes accessed | tf_op | source)
XLA Modules:
  0.0 55.2 jit_solution(1207030810070732303)
XLA Ops:
  0.0 3.2 %route.3 = (bf16[384,384]{1,0:T(8,128)(2,1)S(1)}, bf16[384,384]{1,0:T(8,128)(2,1)S(1)}, bf16[384,384]{1,0:T(8,128)(2,1)S(1)}, bf16[384,384]{1,0:T(8,128)(2,1)S(1)}, s32[1,1024]{1,0:T(1,128)S(1)}) custom-call(s32[1]{0:T(128)} %bitcast.2.home_ref, bf16[1024,384]{1,0:T(8,128)(2,1)} %rows_hbm_ref.1, s32[1,1024]{1,0:T(1,128)} %bitcast.9, s32[1,1024]{1,0:T(1,128)} %bitcast.11), custom_call_target="tpu_custom_call" | custom-call | tf_op jit(solution)/shard_map/route/pallas_call | solution.py:123
  3.2 3.1 %collective-permute-start.19 = (bf16[384,384]{1,0:T(8,128)(2,1)S(1)}, bf16[384,384]{1,0:T(8,128)(2,1)S(1)}, u32[]{:S(2)}, u32[]{:S(2)}) collective-permute-start(bf16[384,384]{1,0:T(8,128)(2,1)S(1)} %get-tuple-element.60), channel_id=1, source_target_pairs={{0,4},{1,5},{2,6},{3,7},{4,0},{5,1},{6,2},{7,3},{8,12},{9,13},{10,... | collective-permute-start | bytes 884744 | tf_op jit(solution)/shard_map/ppermute | solution.py:21
  6.3 1.5 %collective-permute-start.21 = (bf16[384,384]{1,0:T(8,128)(2,1)S(1)}, bf16[384,384]{1,0:T(8,128)(2,1)S(1)}, u32[]{:S(2)}, u32[]{:S(2)}) collective-permute-start(bf16[384,384]{1,0:T(8,128)(2,1)S(1)} %get-tuple-element.62.refs_0_), channel_id=1, source_target_pairs={{0,2},{1,3},{2,0},{3,1},{4,6},{5,7},{6,4},{7,5},{8,10},{9,11},{10,... | collective-permute-start | bytes 884744 | tf_op jit(solution)/shard_map/ppermute | solution.py:21
  7.8 2.6 %collective-permute-start.20 = (bf16[384,384]{1,0:T(8,128)(2,1)S(1)}, bf16[384,384]{1,0:T(8,128)(2,1)S(1)}, u32[]{:S(2)}, u32[]{:S(2)}) collective-permute-start(bf16[384,384]{1,0:T(8,128)(2,1)S(1)} %get-tuple-element.61), channel_id=1, source_target_pairs={{0,8},{1,9},{2,10},{3,11},{4,12},{5,13},{6,14},{7,15},{8,0},{9,1},... | collective-permute-start | bytes 884744 | tf_op jit(solution)/shard_map/ppermute | solution.py:21
  10.4 7.9 %collective-permute-done.19.refs_1_ = bf16[384,384]{1,0:T(8,128)(2,1)S(1)} collective-permute-done((bf16[384,384]{1,0:T(8,128)(2,1)S(1)}, bf16[384,384]{1,0:T(8,128)(2,1)S(1)}, u32[]{:S(2)}, u32[]{:S(2)}) %collective-permute-start.19) | collective-permute-done | bytes 294944 | tf_op jit(solution)/shard_map/ppermute | solution.py:21
  18.3 0.0 collective-permute-start.22
  18.3 0.0 collective-permute-done.21.refs_3_
  18.3 0.5 collective-permute-start.23
  18.8 2.7 %collective-permute-start.30 = (bf16[384,384]{1,0:T(8,128)(2,1)S(1)}, bf16[384,384]{1,0:T(8,128)(2,1)S(1)}, u32[]{:S(2)}, u32[]{:S(2)}) collective-permute-start(bf16[384,384]{1,0:T(8,128)(2,1)S(1)} %collective-permute-done.19.refs_1_), channel_id=1, source_target_pairs={{0,2},{1,3},{2,0},{3,1},{4,6},{5,7},{6,4},{7,5},{8,10},{9,11},{10,... | collective-permute-start | bytes 884744 | tf_op jit(solution)/shard_map/ppermute | solution.py:21
  21.5 2.5 %collective-permute-start.18 = (bf16[384,384]{1,0:T(8,128)(2,1)S(1)}, bf16[384,384]{1,0:T(8,128)(2,1)S(1)}, u32[]{:S(2)}, u32[]{:S(2)}) collective-permute-start(bf16[384,384]{1,0:T(8,128)(2,1)S(1)} %get-tuple-element.58), channel_id=1, source_target_pairs={{0,12},{1,13},{2,14},{3,15},{4,8},{5,9},{6,10},{7,11},{8,4},{9,5},... | collective-permute-start | bytes 884744 | tf_op jit(solution)/shard_map/ppermute | solution.py:21
  24.0 0.1 collective-permute-start.25
  24.1 0.0 collective-permute-done.22.refs_4_
  24.1 0.5 collective-permute-start.29
  24.6 3.1 %compare.10 = (f32[1,1152]{1,0:T(1,128)S(1)}, s32[1,128]{1,0:T(1,128)S(1)}) custom-call(bf16[384,384]{1,0:T(8,128)(2,1)S(1)} %get-tuple-element.62.refs_0_, bf16[384,384]{1,0:T(8,128)(2,1)S(1)} %collective-permute-done.19.refs_1_, bf16[384,384]{1,0:T(8,128)(2,1)S(1)} %collective-permute-done.20.refs_2_, ...), custom_call_target="tpu_custom_call" | custom-call | tf_op jit(solution)/shard_map/compare/pallas_call | solution.py:258
  27.7 1.6 %collective-permute-done.30.refs_12_ = bf16[384,384]{1,0:T(8,128)(2,1)S(1)} collective-permute-done((bf16[384,384]{1,0:T(8,128)(2,1)S(1)}, bf16[384,384]{1,0:T(8,128)(2,1)S(1)}, u32[]{:S(2)}, u32[]{:S(2)}) %collective-permute-start.30) | collective-permute-done | bytes 294944 | tf_op jit(solution)/shard_map/ppermute | solution.py:21
  29.3 2.7 %collective-permute-done.18.refs_6_ = bf16[384,384]{1,0:T(8,128)(2,1)S(1)} collective-permute-done((bf16[384,384]{1,0:T(8,128)(2,1)S(1)}, bf16[384,384]{1,0:T(8,128)(2,1)S(1)}, u32[]{:S(2)}, u32[]{:S(2)}) %collective-permute-start.18) | collective-permute-done | bytes 294944 | tf_op jit(solution)/shard_map/ppermute | solution.py:21
  32.0 2.9 %collective-permute-done.25.refs_7_ = bf16[384,384]{1,0:T(8,128)(2,1)S(1)} collective-permute-done((bf16[384,384]{1,0:T(8,128)(2,1)S(1)}, bf16[384,384]{1,0:T(8,128)(2,1)S(1)}, u32[]{:S(2)}, u32[]{:S(2)}) %collective-permute-start.25) | collective-permute-done | bytes 294944 | tf_op jit(solution)/shard_map/ppermute | solution.py:21
  35.0 1.7 %collective-permute-start.24 = (bf16[384,384]{1,0:T(8,128)(2,1)S(1)}, bf16[384,384]{1,0:T(8,128)(2,1)S(1)}, u32[]{:S(2)}, u32[]{:S(2)}) collective-permute-start(bf16[384,384]{1,0:T(8,128)(2,1)S(1)} %collective-permute-done.18.refs_6_), channel_id=1, source_target_pairs={{0,2},{1,3},{2,0},{3,1},{4,6},{5,7},{6,4},{7,5},{8,10},{9,11},{10,... | collective-permute-start | bytes 884744 | tf_op jit(solution)/shard_map/ppermute | solution.py:21
  36.8 7.3 %compare.11 = (f32[1,1536]{1,0:T(1,128)S(1)}, s32[1,128]{1,0:T(1,128)S(1)}, bf16[1536,384]{1,0:T(8,128)(2,1)S(1)}, f32[1,1536]{1,0:T(1,128)S(1)}) custom-call(bf16[384,384]{1,0:T(8,128)(2,1)S(1)} %get-tuple-element.62.refs_0_, bf16[384,384]{1,0:T(8,128)(2,1)S(1)} %collective-permute-done.19.refs_1_, bf16[384,384]{1,0:T(8,128)(2,1)S(1)} %collective-permute-done.20.refs_2_, ...), custom_call_target="tpu_custom_call" | custom-call | tf_op jit(solution)/shard_map/compare/pallas_call | solution.py:258
  44.1 0.0 copy-start
  44.1 0.0 copy-start.1
  44.1 0.0 copy-start.2
  44.1 0.3 collective-permute-done.24.refs_0_
  44.4 1.1 %compare.12 = (f32[1,1536]{1,0:T(1,128)S(1)}, s32[1,128]{1,0:T(1,128)S(1)}) custom-call(bf16[384,384]{1,0:T(8,128)(2,1)S(1)} %collective-permute-done.24.refs_0_, bf16[1536,384]{1,0:T(8,128)(2,1)S(1)} %get-tuple-element.71.refs_1_, f32[1,1536]{1,0:T(1,128)S(1)} %get-tuple-element.72.refs_2_, f32[1,1536]{1,0:T(1,128)S(1)} %get-tuple-element.69.refs_3_, ...), custom_call_target="tpu_custom_call" | custom-call | tf_op jit(solution)/shard_map/compare/pallas_call | solution.py:258
  45.5 0.5 collective-permute-done.32.refs_0_
  46.0 0.9 %compare.13 = (f32[1,384]{1,0:T(1,128)S(1)}, f32[1,384]{1,0:T(1,128)S(1)}, f32[1,384]{1,0:T(1,128)S(1)}, f32[1,384]{1,0:T(1,128)S(1)}, s32[1,128]{1,0:T(1,128)S(1)}) custom-call(bf16[384,384]{1,0:T(8,128)(2,1)S(1)} %collective-permute-done.32.refs_0_, bf16[1536,384]{1,0:T(8,128)(2,1)S(1)} %get-tuple-element.71.refs_1_, ...), custom_call_target="tpu_custom_call" | custom-call | tf_op jit(solution)/shard_map/compare/pallas_call | solution.py:258
  47.0 2.5 %collective-permute-start.33 = (f32[1,384]{1,0:T(1,128)S(1)}, f32[1,384]{1,0:T(1,128)S(1)}, u32[]{:S(2)}, u32[]{:S(2)}) collective-permute-start(f32[1,384]{1,0:T(1,128)S(1)} %get-tuple-element.76), channel_id=1, source_target_pairs={{0,12},{1,13},{2,14},{3,15},{4,8},{5,9},{6,10},{7,11},{8,4},{9,5},... | collective-permute-start | bytes 4616 | tf_op jit(solution)/shard_map/ppermute | solution.py:21
  49.6 0.6 %collective-permute-start.34 = (f32[1,384]{1,0:T(1,128)S(1)}, f32[1,384]{1,0:T(1,128)S(1)}, u32[]{:S(2)}, u32[]{:S(2)}) collective-permute-start(f32[1,384]{1,0:T(1,128)S(1)} %get-tuple-element.77), channel_id=1, source_target_pairs={{0,8},{1,9},{2,10},{3,11},{4,12},{5,13},{6,14},{7,15},{8,0},{9,1},... | collective-permute-start | bytes 4616 | tf_op jit(solution)/shard_map/ppermute | solution.py:21
  50.1 1.4 %collective-permute-start.35 = (f32[1,384]{1,0:T(1,128)S(1)}, f32[1,384]{1,0:T(1,128)S(1)}, u32[]{:S(2)}, u32[]{:S(2)}) collective-permute-start(f32[1,384]{1,0:T(1,128)S(1)} %get-tuple-element.78), channel_id=1, source_target_pairs={{0,4},{1,5},{2,6},{3,7},{4,0},{5,1},{6,2},{7,3},{8,12},{9,13},{10,... | collective-permute-start | bytes 4616 | tf_op jit(solution)/shard_map/ppermute | solution.py:21
  51.5 1.0 %collective-permute-done.33.refs_0_ = f32[1,384]{1,0:T(1,128)S(1)} collective-permute-done((f32[1,384]{1,0:T(1,128)S(1)}, f32[1,384]{1,0:T(1,128)S(1)}, u32[]{:S(2)}, u32[]{:S(2)}) %collective-permute-start.33) | collective-permute-done | bytes 1568 | tf_op jit(solution)/shard_map/ppermute | solution.py:21
  52.5 1.6 %collective-permute-done.34.refs_1_ = f32[1,384]{1,0:T(1,128)S(1)} collective-permute-done((f32[1,384]{1,0:T(1,128)S(1)}, f32[1,384]{1,0:T(1,128)S(1)}, u32[]{:S(2)}, u32[]{:S(2)}) %collective-permute-start.34) | collective-permute-done | bytes 1568 | tf_op jit(solution)/shard_map/ppermute | solution.py:21
  54.0 1.2 %place.3 = f32[1,1024]{1,0:T(1,128)} custom-call(s32[1,1024]{1,0:T(1,128)S(1)} %get-tuple-element.57.key_ref, f32[1,384]{1,0:T(1,128)S(1)} %collective-permute-done.33.refs_0_, f32[1,384]{1,0:T(1,128)S(1)} %collective-permute-done.34.refs_1_, f32[1,384]{1,0:T(1,128)S(1)} %collective-permute-done.35.refs_2_, f32[1,384]{1,0:T(1,128)S(1)} %get-tuple-element.79.refs_3_, ...), custom_call_target="tpu_custom_call" | custom-call | tf_op jit(solution)/shard_map/place/pallas_call | solution.py:294
  (18 shorter events, 0.1 us)
Async XLA Ops:
  3.2 15.1 %collective-permute-start.19 = (bf16[384,384]{1,0:T(8,128)(2,1)S(1)}, bf16[384,384]{1,0:T(8,128)(2,1)S(1)}, u32[]{:S(2)}, u32[]{:S(2)}) collective-permute-start(bf16[384,384]{1,0:T(8,128)(2,1)S(1)} %get-tuple-element.60), channel_id=1, source_target_pairs={{0,4},{1,5},{2,6},{3,7},{4,0},{5,1},{6,2},{7,3},{8,12},{9,13},{10,... | collective-permute-start | bytes 884744 | tf_op jit(solution)/shard_map/ppermute | solution.py:21
  6.3 12.0 %collective-permute-start.21 = (bf16[384,384]{1,0:T(8,128)(2,1)S(1)}, bf16[384,384]{1,0:T(8,128)(2,1)S(1)}, u32[]{:S(2)}, u32[]{:S(2)}) collective-permute-start(bf16[384,384]{1,0:T(8,128)(2,1)S(1)} %get-tuple-element.62.refs_0_), channel_id=1, source_target_pairs={{0,2},{1,3},{2,0},{3,1},{4,6},{5,7},{6,4},{7,5},{8,10},{9,11},{10,... | collective-permute-start | bytes 884744 | tf_op jit(solution)/shard_map/ppermute | solution.py:21
  7.8 16.1 %collective-permute-start.20 = (bf16[384,384]{1,0:T(8,128)(2,1)S(1)}, bf16[384,384]{1,0:T(8,128)(2,1)S(1)}, u32[]{:S(2)}, u32[]{:S(2)}) collective-permute-start(bf16[384,384]{1,0:T(8,128)(2,1)S(1)} %get-tuple-element.61), channel_id=1, source_target_pairs={{0,8},{1,9},{2,10},{3,11},{4,12},{5,13},{6,14},{7,15},{8,0},{9,1},... | collective-permute-start | bytes 884744 | tf_op jit(solution)/shard_map/ppermute | solution.py:21
  18.3 5.8 %collective-permute-start.22 = (bf16[384,384]{1,0:T(8,128)(2,1)S(1)}, bf16[384,384]{1,0:T(8,128)(2,1)S(1)}, u32[]{:S(2)}, u32[]{:S(2)}) collective-permute-start(bf16[384,384]{1,0:T(8,128)(2,1)S(1)} %get-tuple-element.62.refs_0_), channel_id=1, source_target_pairs={{0,1},{1,0},{2,3},{3,2},{4,5},{5,4},{6,7},{7,6},{8,9},{9,8},{10,11... | collective-permute-start | bytes 884744 | tf_op jit(solution)/shard_map/ppermute | solution.py:21
  18.3 5.8 %collective-permute-start.23 = (bf16[384,384]{1,0:T(8,128)(2,1)S(1)}, bf16[384,384]{1,0:T(8,128)(2,1)S(1)}, u32[]{:S(2)}, u32[]{:S(2)}) collective-permute-start(bf16[384,384]{1,0:T(8,128)(2,1)S(1)} %collective-permute-done.21.refs_3_), channel_id=1, source_target_pairs={{0,1},{1,0},{2,3},{3,2},{4,5},{5,4},{6,7},{7,6},{8,9},{9,8},{10,11... | collective-permute-start | bytes 884744 | tf_op jit(solution)/shard_map/ppermute | solution.py:21
  18.8 10.5 %collective-permute-start.30 = (bf16[384,384]{1,0:T(8,128)(2,1)S(1)}, bf16[384,384]{1,0:T(8,128)(2,1)S(1)}, u32[]{:S(2)}, u32[]{:S(2)}) collective-permute-start(bf16[384,384]{1,0:T(8,128)(2,1)S(1)} %collective-permute-done.19.refs_1_), channel_id=1, source_target_pairs={{0,2},{1,3},{2,0},{3,1},{4,6},{5,7},{6,4},{7,5},{8,10},{9,11},{10,... | collective-permute-start | bytes 884744 | tf_op jit(solution)/shard_map/ppermute | solution.py:21
  21.5 10.5 %collective-permute-start.18 = (bf16[384,384]{1,0:T(8,128)(2,1)S(1)}, bf16[384,384]{1,0:T(8,128)(2,1)S(1)}, u32[]{:S(2)}, u32[]{:S(2)}) collective-permute-start(bf16[384,384]{1,0:T(8,128)(2,1)S(1)} %get-tuple-element.58), channel_id=1, source_target_pairs={{0,12},{1,13},{2,14},{3,15},{4,8},{5,9},{6,10},{7,11},{8,4},{9,5},... | collective-permute-start | bytes 884744 | tf_op jit(solution)/shard_map/ppermute | solution.py:21
  24.0 11.0 %collective-permute-start.25 = (bf16[384,384]{1,0:T(8,128)(2,1)S(1)}, bf16[384,384]{1,0:T(8,128)(2,1)S(1)}, u32[]{:S(2)}, u32[]{:S(2)}) collective-permute-start(bf16[384,384]{1,0:T(8,128)(2,1)S(1)} %collective-permute-done.20.refs_2_), channel_id=1, source_target_pairs={{0,2},{1,3},{2,0},{3,1},{4,6},{5,7},{6,4},{7,5},{8,10},{9,11},{10,... | collective-permute-start | bytes 884744 | tf_op jit(solution)/shard_map/ppermute | solution.py:21
  24.1 10.9 %collective-permute-start.28 = (bf16[384,384]{1,0:T(8,128)(2,1)S(1)}, bf16[384,384]{1,0:T(8,128)(2,1)S(1)}, u32[]{:S(2)}, u32[]{:S(2)}) collective-permute-start(bf16[384,384]{1,0:T(8,128)(2,1)S(1)} %collective-permute-done.19.refs_1_), channel_id=1, source_target_pairs={{0,1},{1,0},{2,3},{3,2},{4,5},{5,4},{6,7},{7,6},{8,9},{9,8},{10,11... | collective-permute-start | bytes 884744 | tf_op jit(solution)/shard_map/ppermute | solution.py:21
  24.1 12.7 %collective-permute-start.29 = (bf16[384,384]{1,0:T(8,128)(2,1)S(1)}, bf16[384,384]{1,0:T(8,128)(2,1)S(1)}, u32[]{:S(2)}, u32[]{:S(2)}) collective-permute-start(bf16[384,384]{1,0:T(8,128)(2,1)S(1)} %collective-permute-done.20.refs_2_), channel_id=1, source_target_pairs={{0,1},{1,0},{2,3},{3,2},{4,5},{5,4},{6,7},{7,6},{8,9},{9,8},{10,11... | collective-permute-start | bytes 884744 | tf_op jit(solution)/shard_map/ppermute | solution.py:21
  29.3 7.4 %collective-permute-start.31 = (bf16[384,384]{1,0:T(8,128)(2,1)S(1)}, bf16[384,384]{1,0:T(8,128)(2,1)S(1)}, u32[]{:S(2)}, u32[]{:S(2)}) collective-permute-start(bf16[384,384]{1,0:T(8,128)(2,1)S(1)} %collective-permute-done.30.refs_12_), channel_id=1, source_target_pairs={{0,1},{1,0},{2,3},{3,2},{4,5},{5,4},{6,7},{7,6},{8,9},{9,8},{10,11... | collective-permute-start | bytes 884744 | tf_op jit(solution)/shard_map/ppermute | solution.py:21
  32.0 4.7 %collective-permute-start.26 = (bf16[384,384]{1,0:T(8,128)(2,1)S(1)}, bf16[384,384]{1,0:T(8,128)(2,1)S(1)}, u32[]{:S(2)}, u32[]{:S(2)}) collective-permute-start(bf16[384,384]{1,0:T(8,128)(2,1)S(1)} %collective-permute-done.18.refs_6_), channel_id=1, source_target_pairs={{0,1},{1,0},{2,3},{3,2},{4,5},{5,4},{6,7},{7,6},{8,9},{9,8},{10,11... | collective-permute-start | bytes 884744 | tf_op jit(solution)/shard_map/ppermute | solution.py:21
  35.0 1.8 %collective-permute-start.27 = (bf16[384,384]{1,0:T(8,128)(2,1)S(1)}, bf16[384,384]{1,0:T(8,128)(2,1)S(1)}, u32[]{:S(2)}, u32[]{:S(2)}) collective-permute-start(bf16[384,384]{1,0:T(8,128)(2,1)S(1)} %collective-permute-done.25.refs_7_), channel_id=1, source_target_pairs={{0,1},{1,0},{2,3},{3,2},{4,5},{5,4},{6,7},{7,6},{8,9},{9,8},{10,11... | collective-permute-start | bytes 884744 | tf_op jit(solution)/shard_map/ppermute | solution.py:21
  35.0 9.4 %collective-permute-start.24 = (bf16[384,384]{1,0:T(8,128)(2,1)S(1)}, bf16[384,384]{1,0:T(8,128)(2,1)S(1)}, u32[]{:S(2)}, u32[]{:S(2)}) collective-permute-start(bf16[384,384]{1,0:T(8,128)(2,1)S(1)} %collective-permute-done.18.refs_6_), channel_id=1, source_target_pairs={{0,2},{1,3},{2,0},{3,1},{4,6},{5,7},{6,4},{7,5},{8,10},{9,11},{10,... | collective-permute-start | bytes 884744 | tf_op jit(solution)/shard_map/ppermute | solution.py:21
  44.1 2.9 %copy-start = (bf16[1024,384]{1,0:T(8,128)(2,1)S(1)}, bf16[1024,384]{1,0:T(8,128)(2,1)}, u32[]{:S(2)}) copy-start(bf16[1024,384]{1,0:T(8,128)(2,1)} %rows_hbm_ref.1) | copy-start | bytes 2359300
  44.1 2.9 %copy-start.1 = (s32[1024]{0:T(1024)S(1)}, s32[1024]{0:T(1024)}, u32[]{:S(2)}) copy-start(s32[1024]{0:T(1024)} %param.6) | copy-start | bytes 12292
  44.1 2.9 %copy-start.2 = (s32[1024]{0:T(1024)S(1)}, s32[1024]{0:T(1024)}, u32[]{:S(2)}) copy-start(s32[1024]{0:T(1024)} %param.7) | copy-start | bytes 12292
  44.4 1.6 %collective-permute-start.32 = (bf16[384,384]{1,0:T(8,128)(2,1)S(1)}, bf16[384,384]{1,0:T(8,128)(2,1)S(1)}, u32[]{:S(2)}, u32[]{:S(2)}) collective-permute-start(bf16[384,384]{1,0:T(8,128)(2,1)S(1)} %collective-permute-done.24.refs_0_), channel_id=1, source_target_pairs={{0,1},{1,0},{2,3},{3,2},{4,5},{5,4},{6,7},{7,6},{8,9},{9,8},{10,11... | collective-permute-start | bytes 884744 | tf_op jit(solution)/shard_map/ppermute | solution.py:21
  47.0 5.4 %collective-permute-start.33 = (f32[1,384]{1,0:T(1,128)S(1)}, f32[1,384]{1,0:T(1,128)S(1)}, u32[]{:S(2)}, u32[]{:S(2)}) collective-permute-start(f32[1,384]{1,0:T(1,128)S(1)} %get-tuple-element.76), channel_id=1, source_target_pairs={{0,12},{1,13},{2,14},{3,15},{4,8},{5,9},{6,10},{7,11},{8,4},{9,5},... | collective-permute-start | bytes 4616 | tf_op jit(solution)/shard_map/ppermute | solution.py:21
  49.6 4.5 %collective-permute-start.34 = (f32[1,384]{1,0:T(1,128)S(1)}, f32[1,384]{1,0:T(1,128)S(1)}, u32[]{:S(2)}, u32[]{:S(2)}) collective-permute-start(f32[1,384]{1,0:T(1,128)S(1)} %get-tuple-element.77), channel_id=1, source_target_pairs={{0,8},{1,9},{2,10},{3,11},{4,12},{5,13},{6,14},{7,15},{8,0},{9,1},... | collective-permute-start | bytes 4616 | tf_op jit(solution)/shard_map/ppermute | solution.py:21
  50.1 3.9 %collective-permute-start.35 = (f32[1,384]{1,0:T(1,128)S(1)}, f32[1,384]{1,0:T(1,128)S(1)}, u32[]{:S(2)}, u32[]{:S(2)}) collective-permute-start(f32[1,384]{1,0:T(1,128)S(1)} %get-tuple-element.78), channel_id=1, source_target_pairs={{0,4},{1,5},{2,6},{3,7},{4,0},{5,1},{6,2},{7,3},{8,12},{9,13},{10,... | collective-permute-start | bytes 4616 | tf_op jit(solution)/shard_map/ppermute | solution.py:21
